TPU v7x, 32 devices: a whole 2x2x4 slice. The times are simulated.
32 devices in a mesh: group: 4 (over y, x), tile: 8 (over z, core).
Axes of the slice: x: 2, y: 2, z: 4, core: 2. Of those that a mesh axis runs over, the one named last changes fastest.
Arguments:
- points: float32 [7, 35, 16384], P(None, None, ('group', 'tile')), parts along dimension 2
- point_counts: int32 [16384], P(('group', 'tile')), parts along dimension 0, may hold values from 1 to 35, as said below
- voxel_cells: int32 [16384], P(('group', 'tile')), parts along dimension 0, may hold values from 0 to 131071, as said below
- anchor_labels: int32 [2, 1024, 128], P(None, ('group', 'tile')), parts along dimension 1, may hold values from -1 to 1, as said below
- box_targets: float32 [14, 1024, 128], P(None, ('group', 'tile')), parts along dimension 1, may hold values from -4 to 4
- weights: float32 [3297280], P(('group', 'tile')), parts along dimension 0
- adam_m: float32 [3297280], P(('group', 'tile')), parts along dimension 0
- adam_v: float32 [3297280], P(('group', 'tile')), parts along dimension 0, as said below
- outer_momentum: float32 [3297280], P(('group', 'tile')), parts along dimension 0, may hold values from -0.12 to 0.12
Outputs:
- adam_m_new: float32 [3297280], P(('group', 'tile')), parts along dimension 0
- adam_v_new: float32 [3297280], P(('group', 'tile')), parts along dimension 0
- outer_momentum_new: float32 [3297280], P(('group', 'tile')), parts along dimension 0
- weights_new: float32 [3297280], P(('group', 'tile')), parts along dimension 0
- loss_sum: float32 [4], P('group'), parts along dimension 0
- positives: float32 [4], P('group'), parts along dimension 0
There are 4 independent parts, one for each index of `group`. A program takes and returns all parts, laid end to end along the dimension named above; each array names one. Nothing has to cross between parts.
Inputs may be any that keep to these rules, and one draw needn't show every extreme that they name: `point_counts`: some voxel holds 35 points in every draw. `voxel_cells`: the 512 slots of a device, devices in order, hold voxels in the rows of that device's block of 32 map rows; no two voxels share a cell; a cell number is (row * 128 + column) * 4 + height layer. `anchor_labels`: 1 marks positive anchors, 0 negative ones, -1 anchors left out of the loss. `adam_v`: every entry is positive.
All inputs are finite; a program needn't handle non-finite values.
Results may differ from a plain program's by a relative error of at most 0.0003.
The roundings to bfloat16 on the way count: a program that leaves them out, or rounds other values in their place, can miss the bound.
Values may be sent and summed in bfloat16 or wider, within the bound.
A program may use at most 192 MiB of HBM per device.

v0:
```python
import math

import jax
import jax.numpy as jnp
from jax import lax
from jax.sharding import PartitionSpec as P

C1 = 32
C2 = 128
CM = 64
CR1 = 128
CR2 = 128
CR3 = 256
ANCH = 2
ZD = 4
H_SCENE = 200
STEP = 10
DO = 2


PRECISE = lax.Precision.HIGHEST
FOCAL_ALPHA = 0.25
HUBER_BETA = 1.0 / 9.0
NORM_EPSILON = 1e-05
INNER_RATE = 0.05
FIRST_DECAY = 0.9
SECOND_DECAY = 0.999
ADAM_EPSILON = 1e-08
WEIGHT_DECAY = 0.01
OUTER_RATE = 0.7
OUTER_MOMENT = 0.9
LAYER_NAMES = ("mid", "one", "two", "three")


def with_halo(cells, sides, width):
    for axis, dim in sides:
        count = lax.axis_size(axis)
        ends = count - 1
        head = lax.slice_in_dim(cells, 0, width, axis=dim)
        tail = lax.slice_in_dim(cells, cells.shape[dim] - width, cells.shape[dim], axis=dim)
        cells = jnp.concatenate(
            [
                lax.ppermute(tail, axis, [(i, (i + 1) % count) for i in range(ends)]),
                cells,
                lax.ppermute(head, axis, [((i + 1) % count, i) for i in range(ends)]),
            ],
            axis=dim,
        )
    return cells


def shapes():
    return [
        ("w_vfe", (7, C1)),
        ("gamma", (C1,)),
        ("beta", (C1,)),
        ("w_fc", (2 * C1, C2)),
        ("b_fc", (C2,)),
        ("w_mid", (3, 3, 3, C2, CM)),
        ("b_mid", (CM,)),
        ("w_one", (3, 3, DO * CM, CR1)),
        ("b_one", (CR1,)),
        ("w_two", (3, 3, CR1, CR2)),
        ("b_two", (CR2,)),
        ("w_three", (3, 3, CR2, CR3)),
        ("b_three", (CR3,)),
        ("w_head", (CR3, ANCH * 8)),
        ("b_head", (ANCH * 8,)),
    ]


def unpack(flat_weights):
    params = {}
    offset = 0
    for entry_name, extent in shapes():
        length = math.prod(extent)
        params[entry_name] = flat_weights[offset : offset + length].reshape(extent)
        offset += length
    return params


def keep_rows(first_row, row_count, all_rows):
    global_row = first_row + jnp.arange(row_count)
    above = global_row % H_SCENE != 0
    below = ((global_row + 1) % H_SCENE != 0) & (global_row + 1 < all_rows)
    return jnp.stack([above, jnp.ones_like(above), below]).astype(jnp.float32)


def mid_taps():
    listing = []
    for out_depth in range(DO):
        first_z = max(0, 2 * out_depth - 1)
        last_z = min(ZD, 2 * out_depth + 2)
        listing.append((first_z, last_z, first_z - 2 * out_depth + 1))
    return listing


def conv_blocks(kernel, layer_name):
    if layer_name != "mid":
        return [(0, kernel.shape[2], kernel)]
    blocks = []
    for first_z, last_z, first_tap in mid_taps():
        tap_block = kernel[first_tap : first_tap + last_z - first_z]
        blocks.append(
            (
                first_z * C2,
                last_z * C2,
                tap_block.transpose(1, 2, 0, 3, 4).reshape(3, 3, (last_z - first_z) * C2, CM),
            )
        )
    return blocks


def fold_kernel(block_grads, layer_name, kernel_shape):
    if layer_name != "mid":
        return block_grads[0]
    folded = jnp.zeros(kernel_shape, jnp.float32)
    for (first_z, last_z, first_tap), block_grad in zip(mid_taps(), block_grads):
        tap_count = last_z - first_z
        folded = folded.at[first_tap : first_tap + tap_count].add(
            block_grad.reshape(3, 3, tap_count, C2, CM).transpose(2, 0, 1, 3, 4)
        )
    return folded


def silu_slope(value):
    sigmoid_value = jax.nn.sigmoid(value)
    return sigmoid_value * (1.0 + value * (1.0 - sigmoid_value))


def anchor_loss(logits, labels, targets):
    class_logits = logits[:ANCH]
    box_out = logits[ANCH:].reshape(ANCH, 7, logits.shape[1], logits.shape[2])
    positive = (labels == 1).astype(jnp.float32)
    negative = (labels == 0).astype(jnp.float32)
    chance = jax.nn.sigmoid(class_logits)
    focal_terms = -FOCAL_ALPHA * positive * (1.0 - chance) ** 2 * jax.nn.log_sigmoid(
        class_logits
    ) - (1.0 - FOCAL_ALPHA) * negative * chance**2 * jax.nn.log_sigmoid(-class_logits)
    residual = box_out - targets.reshape(box_out.shape)
    magnitude = jnp.abs(residual)
    huber_terms = jnp.where(
        magnitude < HUBER_BETA, 0.5 * residual * residual / HUBER_BETA, magnitude - 0.5 * HUBER_BETA
    )
    return jnp.sum(focal_terms) + 2.0 * jnp.sum(huber_terms * positive[:, None])


def adam_outer(gradient, weight, moment, second, momentum):
    moment = FIRST_DECAY * moment + (1.0 - FIRST_DECAY) * gradient
    second = SECOND_DECAY * second + (1.0 - SECOND_DECAY) * gradient * gradient
    moment_fix = moment / (1.0 - FIRST_DECAY**STEP)
    second_fix = second / (1.0 - SECOND_DECAY**STEP)
    inner_weight = weight - INNER_RATE * (
        moment_fix / (jnp.sqrt(second_fix) + ADAM_EPSILON) + WEIGHT_DECAY * weight
    )
    inner_step = weight - inner_weight
    momentum = OUTER_MOMENT * momentum + inner_step
    updated = weight - OUTER_RATE * (inner_step + OUTER_MOMENT * momentum)
    return (moment, second, momentum, updated)


def conv_forward(extended, kernel, row_keep):
    row_count = extended.shape[1] - 2
    col_count = extended.shape[2]
    padded = jnp.pad(extended, ((0, 0), (0, 0), (1, 1)))
    result = jnp.zeros((kernel.shape[3], row_count, col_count), jnp.float32)
    for i in range(3):
        for j in range(3):
            window = padded[:, i : i + row_count, j : j + col_count] * row_keep[i][None, :, None]
            result = result + jnp.einsum(
                "co,crw->orw", kernel[i, j], window, preferred_element_type=jnp.float32
            )
    return result


def conv_backward(extended, kernel, row_keep, grad_pre):
    row_count = extended.shape[1] - 2
    col_count = extended.shape[2]
    padded = jnp.pad(extended, ((0, 0), (0, 0), (1, 1)))
    input_grad = jnp.zeros((extended.shape[0], row_count + 2, col_count + 2), jnp.float32)
    tap_grads = []
    for i in range(3):
        for j in range(3):
            window = padded[:, i : i + row_count, j : j + col_count] * row_keep[i][None, :, None]
            tap_grads.append(
                jnp.einsum("crw,orw->co", window, grad_pre, preferred_element_type=jnp.float32)
            )
            back_tap = jnp.einsum(
                "co,orw->crw", kernel[i, j], grad_pre, preferred_element_type=jnp.float32
            )
            input_grad = input_grad.at[:, i : i + row_count, j : j + col_count].add(
                back_tap * row_keep[i][None, :, None]
            )
    kernel_grad = jnp.stack(tap_grads).reshape(kernel.shape)
    return (kernel_grad, input_grad[:, :, 1 : col_count + 1])


def layer_forward(signal, blocks, bias_vec, row_keep):
    extended = with_halo(signal, (("tile", 1),), 1)
    outputs = [
        conv_forward(extended[first_channel:end_channel], block, row_keep)
        for first_channel, end_channel, block in blocks
    ]
    stacked = jnp.concatenate(outputs, axis=0)
    bias_full = jnp.tile(bias_vec, stacked.shape[0] // bias_vec.shape[0])
    return (extended, stacked + bias_full[:, None, None])


def layer_backward(extended, blocks, row_keep, pre_act, grad_out):
    grad_pre = (grad_out * silu_slope(pre_act)).astype(jnp.bfloat16)
    row_count = extended.shape[1] - 2
    block_grads = []
    out_start = 0
    if len(blocks) == 1:
        kernel_grad, input_grad = conv_backward(extended, blocks[0][2], row_keep, grad_pre)
        block_grads.append(kernel_grad)
    else:
        input_grad = jnp.zeros((extended.shape[0], row_count + 2, extended.shape[2]), jnp.float32)
        for first_channel, end_channel, block in blocks:
            out_width = block.shape[3]
            kernel_grad, block_input = conv_backward(
                extended[first_channel:end_channel],
                block,
                row_keep,
                grad_pre[out_start : out_start + out_width],
            )
            block_grads.append(kernel_grad)
            input_grad = input_grad.at[first_channel:end_channel].add(block_input)
            out_start += out_width
    channel_sums = jnp.sum(grad_pre, axis=(1, 2), dtype=jnp.float32)
    rim_rows = jnp.stack([input_grad[:, 0], input_grad[:, row_count + 1]], axis=1)
    beside = with_halo(rim_rows.astype(jnp.bfloat16), (("tile", 1),), 1).astype(rim_rows.dtype)
    own_rows = input_grad[:, 1 : row_count + 1]
    own_rows = own_rows.at[:, 0].add(beside[:, 0]).at[:, row_count - 1].add(beside[:, 3])
    return (block_grads, channel_sums, own_rows)


def shards(
    points,
    point_counts,
    voxel_cells,
    anchor_labels,
    box_targets,
    weights,
    adam_m,
    adam_v,
    outer_momentum,
):
    flat_weights = lax.all_gather(weights, "tile", axis=0, tiled=True)
    params = unpack(flat_weights)
    point_mask = (jnp.arange(points.shape[1])[:, None] < point_counts[None, :]).astype(jnp.float32)
    counts = point_counts.astype(jnp.float32)
    linear = jnp.einsum("ki,kpv->ipv", params["w_vfe"], points, precision=PRECISE)
    local_total = jnp.sum(point_mask)
    local_positives = jnp.sum((anchor_labels == 1).astype(jnp.float32))
    local_sums = jnp.sum(linear * point_mask, axis=(1, 2))
    channel_sums, point_total, positives = lax.psum(
        (local_sums, local_total, local_positives), "tile"
    )
    channel_mean = channel_sums / point_total
    centered = linear - channel_mean[:, None, None]
    local_squares = jnp.sum(centered * centered * point_mask, axis=(1, 2))
    variance = lax.psum(local_squares, "tile") / point_total
    inverse_scale = lax.rsqrt(variance + NORM_EPSILON)
    normed = centered * inverse_scale[:, None, None]
    gamma = params["gamma"][:, None, None]
    act_in = gamma * normed + params["beta"][:, None, None]
    first_out = jax.nn.silu(act_in) * point_mask
    pooled = jnp.sum(first_out, axis=1) / counts
    joined = jnp.concatenate([first_out, pooled[:, None, :] * point_mask], axis=0).astype(
        jnp.bfloat16
    )
    fc_kernel = params["w_fc"].astype(jnp.bfloat16)
    inner_pre = (
        jnp.einsum("io,ipv->opv", fc_kernel, joined, preferred_element_type=jnp.float32)
        + params["b_fc"][:, None, None]
    )
    feature = jnp.sum(jax.nn.silu(inner_pre) * point_mask, axis=1) / counts
    row_count, col_count = (anchor_labels.shape[1], anchor_labels.shape[2])
    depth_cells = row_count * col_count * ZD
    local_cells = voxel_cells % depth_cells
    canvas = jnp.zeros((C2, depth_cells), jnp.float32).at[:, local_cells].set(feature)
    canvas = (
        canvas.reshape(C2, row_count, col_count, ZD)
        .transpose(3, 0, 1, 2)
        .reshape(ZD * C2, row_count, col_count)
    )
    row_keep = keep_rows(
        lax.axis_index("tile") * row_count, row_count, row_count * lax.axis_size("tile")
    ).astype(jnp.bfloat16)
    signal = canvas.astype(jnp.bfloat16)
    kept = []
    for layer_name in LAYER_NAMES:
        blocks = conv_blocks(params["w_" + layer_name].astype(jnp.bfloat16), layer_name)
        extended, pre_act = layer_forward(signal, blocks, params["b_" + layer_name], row_keep)
        kept.append((extended, blocks, pre_act))
        signal = jax.nn.silu(pre_act).astype(jnp.bfloat16)
    head_kernel = params["w_head"].astype(jnp.bfloat16)
    logits = (
        jnp.einsum("co,crw->orw", head_kernel, signal, preferred_element_type=jnp.float32)
        + params["b_head"][:, None, None]
    )
    divisor = jnp.maximum(positives, 1.0)
    local_loss, loss_pull = jax.vjp(lambda v: anchor_loss(v, anchor_labels, box_targets), logits)
    (grad_logits,) = loss_pull(1.0 / divisor)
    grad_logits = grad_logits.astype(jnp.bfloat16)
    grads = {}
    grads["w_head"] = jnp.einsum(
        "crw,orw->co", signal, grad_logits, preferred_element_type=jnp.float32
    )
    grads["b_head"] = jnp.sum(grad_logits, axis=(1, 2), dtype=jnp.float32)
    grad_signal = jnp.einsum(
        "co,orw->crw", head_kernel, grad_logits, preferred_element_type=jnp.float32
    )
    for position in reversed(range(len(LAYER_NAMES))):
        layer_name = LAYER_NAMES[position]
        extended, blocks, pre_act = kept[position]
        block_grads, channel_sums, grad_signal = layer_backward(
            extended, blocks, row_keep, pre_act, grad_signal
        )
        grads["w_" + layer_name] = fold_kernel(
            block_grads, layer_name, params["w_" + layer_name].shape
        )
        bias_size = params["b_" + layer_name].shape[0]
        grads["b_" + layer_name] = jnp.sum(channel_sums.reshape(-1, bias_size), axis=0)
    grad_cells = (
        grad_signal.reshape(ZD, C2, row_count, col_count)
        .transpose(1, 2, 3, 0)
        .reshape(C2, depth_cells)
    )
    grad_feature = grad_cells[:, local_cells]
    grad_inner = (point_mask * (grad_feature / counts)[:, None, :] * silu_slope(inner_pre)).astype(
        jnp.bfloat16
    )
    grads["w_fc"] = jnp.einsum(
        "ipv,opv->io", joined, grad_inner, preferred_element_type=jnp.float32
    )
    grads["b_fc"] = jnp.sum(grad_inner, axis=(1, 2), dtype=jnp.float32)
    grad_joined = jnp.einsum(
        "io,opv->ipv", fc_kernel, grad_inner, preferred_element_type=jnp.float32
    )
    grad_pooled = jnp.sum(grad_joined[C1:] * point_mask, axis=1)
    grad_first = (grad_joined[:C1] + (grad_pooled / counts)[:, None, :]) * point_mask
    grad_act = grad_first * silu_slope(act_in)
    grads["gamma"] = jnp.sum(grad_act * normed, axis=(1, 2))
    grads["beta"] = jnp.sum(grad_act, axis=(1, 2))
    grad_normed = grad_act * gamma
    sum_plain, sum_scaled, loss_sum = lax.psum(
        (
            jnp.sum(grad_normed * point_mask, axis=(1, 2)),
            jnp.sum(grad_normed * normed * point_mask, axis=(1, 2)),
            local_loss,
        ),
        "tile",
    )
    grad_linear = (
        point_mask
        * inverse_scale[:, None, None]
        * (
            grad_normed
            - sum_plain[:, None, None] / point_total
            - normed * sum_scaled[:, None, None] / point_total
        )
    )
    grads["w_vfe"] = jnp.einsum("kpv,ipv->ki", points, grad_linear, precision=PRECISE)
    pieces = [grads[entry_name].reshape(-1) for entry_name, extent in shapes()]
    used = sum((math.prod(extent) for entry_name, extent in shapes()))
    pieces.append(jnp.zeros((flat_weights.shape[0] - used,), jnp.float32))
    full_grad = jnp.concatenate(pieces)
    shard_grad = lax.psum_scatter(full_grad, "tile", scatter_dimension=0, tiled=True)
    moment, second, momentum, updated = adam_outer(
        shard_grad, weights, adam_m, adam_v, outer_momentum
    )
    return (moment, second, momentum, updated, loss_sum.reshape(1), positives.reshape(1))


def solution(mesh):
    in_specs = (
        P(None, None, ("group", "tile")),
        P(("group", "tile")),
        P(("group", "tile")),
        P(None, ("group", "tile"), None),
        P(None, ("group", "tile"), None),
        P(("group", "tile")),
        P(("group", "tile")),
        P(("group", "tile")),
        P(("group", "tile")),
    )
    out_specs = (
        P(("group", "tile")),
        P(("group", "tile")),
        P(("group", "tile")),
        P(("group", "tile")),
        P("group"),
        P("group"),
    )
    return jax.shard_map(shards, mesh=mesh, in_specs=in_specs, out_specs=out_specs, check_vma=False)
```

profile of v0, /device:TPU:0, one launch (start us, length us, event | category | flops | bytes accessed | tf_op | source)
XLA Modules:
  0.0 1375.9 jit_solution(317905663388805758)
XLA Ops:
  18.2 34.4 %all-gather.3.cloned.1.call-done = f32[8,1,103040]{2,1,0:T(1,128)} async-done(((f32[1,1,103040]{2,1,0:T(1,128)}), f32[8,1,103040]{2,1,0:T(1,128)}) %all-gather.3.cloned.1.call-update) | async-done | bytes 3297296 | tf_op jit(solution)/shard_map/all_gather | solution.py:249
  62.5 15.4 %all-reduce.16 = (f32[32]{0:T(128)S(1)}, f32[]{:T(128)}) all-reduce(f32[32]{0:T(128)S(1)} %get-tuple-element.775, f32[]{:T(128)} %fusion.437), channel_id=1, replica_groups=mesh['group'=4,'tile'=8] {'tile'}, use_global_device_ids=true, to_apply=%region_1.0 | all-reduce | flops 33 | bytes 264 | tf_op jit(solution)/shard_map/psum | solution.py:257
  79.1 13.6 psum.51
  98.3 8.0 fusion.4
  106.2 5.8 scatter_custom_fusion
  122.4 7.3 copy.371
  143.4 7.1 copy.375
  254.4 12.4 fusion.19
  270.0 16.5 %psum.52 = f32[]{:T(128)} all-reduce(f32[]{:T(128)} %get-tuple-element.711), channel_id=1, replica_groups=mesh['group'=4,'tile'=8] {'tile'}, use_global_device_ids=true, to_apply=%region_10.11 | all-reduce | flops 1 | bytes 8 | tf_op jit(solution)/shard_map/psum | solution.py:257
  307.5 15.6 %scatter-add.189 = f32[128,34,130]{2,0,1:T(8,128)} dynamic-update-slice(f32[128,34,130]{2,0,1:T(8,128)} %scatter-add.186, f32[128,32,128]{2,0,1:T(8,128)} %bitcast_add_fusion.4, s32[]{:T(128)} %constant.1398.clone.1, s32[]{:T(128)} %bitcast.119, s32[]{:T(128)} %bitcast.120) | dynamic-update-slice | bytes 4194308 | tf_op jit(solution)/shard_map/scatter-add | solution.py:191
  323.1 6.3 add_select_fusion.4
  329.4 15.5 %scatter-add.190 = f32[128,34,130]{2,0,1:T(8,128)} dynamic-update-slice(f32[128,34,130]{2,0,1:T(8,128)} %scatter-add.189, f32[128,32,128]{2,0,1:T(8,128)} %add_select_fusion.4, s32[]{:T(128)} %constant.1398.clone.1, s32[]{:T(128)} %bitcast.123, s32[]{:T(128)} %bitcast.124) | dynamic-update-slice | bytes 4194308 | tf_op jit(solution)/shard_map/scatter-add | solution.py:191
  353.0 14.3 %scatter-add.194 = f32[128,34,130]{2,0,1:T(8,128)} dynamic-update-slice(f32[128,34,130]{2,0,1:T(8,128)} %fusion.63, f32[128,32,128]{2,0,1:T(8,128)} %slice_add_fusion.30, s32[]{:T(128)} %constant.1398.clone.1, s32[]{:T(128)} %constant.1407.clone.1, s32[]{:T(128)} %constant.1407.clone.1) | dynamic-update-slice | bytes 4194308 | tf_op jit(solution)/shard_map/scatter-add | solution.py:191
  371.8 14.5 %scatter-add.195 = f32[128,34,130]{2,0,1:T(8,128)} dynamic-update-slice(f32[128,34,130]{2,0,1:T(8,128)} %scatter-add.194, f32[128,32,128]{2,0,1:T(8,128)} %slice_add_fusion.29, s32[]{:T(128)} %constant.1398.clone.1, s32[]{:T(128)} %constant.1407.clone.1, s32[]{:T(128)} %constant.1416.clone.1) | dynamic-update-slice | bytes 4194308 | tf_op jit(solution)/shard_map/scatter-add | solution.py:191
  394.5 14.3 %scatter-add.199 = f32[128,34,130]{2,0,1:T(8,128)} dynamic-update-slice(f32[128,34,130]{2,0,1:T(8,128)} %fusion.62, f32[128,32,128]{2,0,1:T(8,128)} %slice_add_fusion.27, s32[]{:T(128)} %constant.1398.clone.1, s32[]{:T(128)} %constant.1416.clone.1, s32[]{:T(128)} %constant.1407.clone.1) | dynamic-update-slice | bytes 4194308 | tf_op jit(solution)/shard_map/scatter-add | solution.py:191
  413.2 14.3 %scatter-add.200 = f32[128,34,130]{2,0,1:T(8,128)} dynamic-update-slice(f32[128,34,130]{2,0,1:T(8,128)} %scatter-add.199, f32[128,32,128]{2,0,1:T(8,128)} %slice_add_fusion.26, s32[]{:T(128)} %constant.1398.clone.1, s32[]{:T(128)} %constant.1416.clone.1, s32[]{:T(128)} %constant.1416.clone.1) | dynamic-update-slice | bytes 4194308 | tf_op jit(solution)/shard_map/scatter-add | solution.py:191
  462.1 15.8 %scatter-add.206 = f32[128,34,130]{2,0,1:T(8,128)} dynamic-update-slice(f32[128,34,130]{2,0,1:T(8,128)} %scatter-add.205, f32[128,32,128]{2,0,1:T(8,128)} %bitcast_add_fusion.3, s32[]{:T(128)} %constant.1398.clone.1, s32[]{:T(128)} %bitcast.119, s32[]{:T(128)} %bitcast.120) | dynamic-update-slice | bytes 4194308 | tf_op jit(solution)/shard_map/scatter-add | solution.py:191
  477.9 6.1 add_select_fusion.3
  484.0 15.5 %scatter-add.209 = f32[128,34,130]{2,0,1:T(8,128)} dynamic-update-slice(f32[128,34,130]{2,0,1:T(8,128)} %scatter-add.206, f32[128,32,128]{2,0,1:T(8,128)} %add_select_fusion.3, s32[]{:T(128)} %constant.1398.clone.1, s32[]{:T(128)} %bitcast.123, s32[]{:T(128)} %bitcast.124) | dynamic-update-slice | bytes 4194308 | tf_op jit(solution)/shard_map/scatter-add | solution.py:191
  507.1 14.3 %scatter-add.211 = f32[128,34,130]{2,0,1:T(8,128)} dynamic-update-slice(f32[128,34,130]{2,0,1:T(8,128)} %fusion.61, f32[128,32,128]{2,0,1:T(8,128)} %slice_add_fusion.24, s32[]{:T(128)} %constant.1398.clone.1, s32[]{:T(128)} %constant.1407.clone.1, s32[]{:T(128)} %constant.1407.clone.1) | dynamic-update-slice | bytes 4194308 | tf_op jit(solution)/shard_map/scatter-add | solution.py:191
  525.6 14.3 %scatter-add.214 = f32[128,34,130]{2,0,1:T(8,128)} dynamic-update-slice(f32[128,34,130]{2,0,1:T(8,128)} %scatter-add.211, f32[128,32,128]{2,0,1:T(8,128)} %slice_add_fusion.23, s32[]{:T(128)} %constant.1398.clone.1, s32[]{:T(128)} %constant.1407.clone.1, s32[]{:T(128)} %constant.1416.clone.1) | dynamic-update-slice | bytes 4194308 | tf_op jit(solution)/shard_map/scatter-add | solution.py:191
  547.6 14.3 %scatter-add.216 = f32[128,34,130]{2,0,1:T(8,128)} dynamic-update-slice(f32[128,34,130]{2,0,1:T(8,128)} %fusion.60, f32[128,32,128]{2,0,1:T(8,128)} %slice_add_fusion.21, s32[]{:T(128)} %constant.1398.clone.1, s32[]{:T(128)} %constant.1416.clone.1, s32[]{:T(128)} %constant.1407.clone.1) | dynamic-update-slice | bytes 4194308 | tf_op jit(solution)/shard_map/scatter-add | solution.py:191
  566.1 14.3 %scatter-add.219 = f32[128,34,130]{2,0,1:T(8,128)} dynamic-update-slice(f32[128,34,130]{2,0,1:T(8,128)} %scatter-add.216, f32[128,32,128]{2,0,1:T(8,128)} %slice_add_fusion.20, s32[]{:T(128)} %constant.1398.clone.1, s32[]{:T(128)} %constant.1416.clone.1, s32[]{:T(128)} %constant.1416.clone.1) | dynamic-update-slice | bytes 4194308 | tf_op jit(solution)/shard_map/scatter-add | solution.py:191
  607.5 15.7 %scatter-add.225 = f32[128,34,130]{2,0,1:T(8,128)} dynamic-update-slice(f32[128,34,130]{2,0,1:T(8,128)} %scatter-add.224, f32[128,32,128]{2,0,1:T(8,128)} %bitcast_add_fusion.2, s32[]{:T(128)} %constant.1398.clone.1, s32[]{:T(128)} %bitcast.119, s32[]{:T(128)} %bitcast.120) | dynamic-update-slice | bytes 4194308 | tf_op jit(solution)/shard_map/scatter-add | solution.py:191
  623.2 6.0 add_select_fusion.2
  629.2 15.5 %scatter-add.226 = f32[128,34,130]{2,0,1:T(8,128)} dynamic-update-slice(f32[128,34,130]{2,0,1:T(8,128)} %scatter-add.225, f32[128,32,128]{2,0,1:T(8,128)} %add_select_fusion.2, s32[]{:T(128)} %constant.1398.clone.1, s32[]{:T(128)} %bitcast.123, s32[]{:T(128)} %bitcast.124) | dynamic-update-slice | bytes 4194308 | tf_op jit(solution)/shard_map/scatter-add | solution.py:191
  652.2 14.3 %scatter-add.230 = f32[128,34,130]{2,0,1:T(8,128)} dynamic-update-slice(f32[128,34,130]{2,0,1:T(8,128)} %fusion.59, f32[128,32,128]{2,0,1:T(8,128)} %slice_add_fusion.18, s32[]{:T(128)} %constant.1398.clone.1, s32[]{:T(128)} %constant.1407.clone.1, s32[]{:T(128)} %constant.1407.clone.1) | dynamic-update-slice | bytes 4194308 | tf_op jit(solution)/shard_map/scatter-add | solution.py:191
  670.7 14.3 %scatter-add.231 = f32[128,34,130]{2,0,1:T(8,128)} dynamic-update-slice(f32[128,34,130]{2,0,1:T(8,128)} %scatter-add.230, f32[128,32,128]{2,0,1:T(8,128)} %slice_add_fusion.17, s32[]{:T(128)} %constant.1398.clone.1, s32[]{:T(128)} %constant.1407.clone.1, s32[]{:T(128)} %constant.1416.clone.1) | dynamic-update-slice | bytes 4194308 | tf_op jit(solution)/shard_map/scatter-add | solution.py:191
  692.6 14.3 %scatter-add.235 = f32[128,34,130]{2,0,1:T(8,128)} dynamic-update-slice(f32[128,34,130]{2,0,1:T(8,128)} %fusion.58, f32[128,32,128]{2,0,1:T(8,128)} %slice_add_fusion.15, s32[]{:T(128)} %constant.1398.clone.1, s32[]{:T(128)} %constant.1416.clone.1, s32[]{:T(128)} %constant.1407.clone.1) | dynamic-update-slice | bytes 4194308 | tf_op jit(solution)/shard_map/scatter-add | solution.py:191
  711.0 14.3 %scatter-add.236 = f32[128,34,130]{2,0,1:T(8,128)} dynamic-update-slice(f32[128,34,130]{2,0,1:T(8,128)} %scatter-add.235, f32[128,32,128]{2,0,1:T(8,128)} %slice_add_fusion.14, s32[]{:T(128)} %constant.1398.clone.1, s32[]{:T(128)} %constant.1416.clone.1, s32[]{:T(128)} %constant.1416.clone.1) | dynamic-update-slice | bytes 4194308 | tf_op jit(solution)/shard_map/scatter-add | solution.py:191
  753.9 5.3 bitcast_add_fusion
  795.3 21.5 %scatter-add.244 = f32[256,34,130]{0,2,1:T(8,128)} dynamic-update-slice(f32[256,34,130]{0,2,1:T(8,128)} %scatter-add.241, f32[256,32,128]{0,2,1:T(8,128)} %bitcast_add_fusion.1, s32[]{:T(128)} %constant.1398.clone.1, s32[]{:T(128)} %bitcast.119, s32[]{:T(128)} %bitcast.120) | dynamic-update-slice | bytes 8388612 | tf_op jit(solution)/shard_map/scatter-add | solution.py:191
  816.8 7.2 add_select_fusion.1
  824.0 21.4 %scatter-add.245 = f32[256,34,130]{0,2,1:T(8,128)} dynamic-update-slice(f32[256,34,130]{0,2,1:T(8,128)} %scatter-add.244, f32[256,32,128]{0,2,1:T(8,128)} %add_select_fusion.1, s32[]{:T(128)} %constant.1398.clone.1, s32[]{:T(128)} %bitcast.123, s32[]{:T(128)} %bitcast.124) | dynamic-update-slice | bytes 8388612 | tf_op jit(solution)/shard_map/scatter-add | solution.py:191
  845.4 5.1 fusion.14
  850.5 5.2 slice_add_fusion.11
  855.8 20.2 %scatter-add.249 = f32[256,34,130]{0,2,1:T(8,128)} dynamic-update-slice(f32[256,34,130]{0,2,1:T(8,128)} %fusion.14, f32[256,32,128]{0,2,1:T(8,128)} %slice_add_fusion.11, s32[]{:T(128)} %constant.1398.clone.1, s32[]{:T(128)} %constant.1407.clone.1, s32[]{:T(128)} %constant.1407.clone.1) | dynamic-update-slice | bytes 8388612 | tf_op jit(solution)/shard_map/scatter-add | solution.py:191
  876.0 5.2 slice_add_fusion.10
  881.2 20.2 %scatter-add.250 = f32[256,34,130]{0,2,1:T(8,128)} dynamic-update-slice(f32[256,34,130]{0,2,1:T(8,128)} %scatter-add.249, f32[256,32,128]{0,2,1:T(8,128)} %slice_add_fusion.10, s32[]{:T(128)} %constant.1398.clone.1, s32[]{:T(128)} %constant.1407.clone.1, s32[]{:T(128)} %constant.1416.clone.1) | dynamic-update-slice | bytes 8388612 | tf_op jit(solution)/shard_map/scatter-add | solution.py:191
  901.4 5.1 fusion.13
  906.5 5.2 slice_add_fusion.8
  911.7 20.2 %scatter-add.254 = f32[256,34,130]{0,2,1:T(8,128)} dynamic-update-slice(f32[256,34,130]{0,2,1:T(8,128)} %fusion.13, f32[256,32,128]{0,2,1:T(8,128)} %slice_add_fusion.8, s32[]{:T(128)} %constant.1398.clone.1, s32[]{:T(128)} %constant.1416.clone.1, s32[]{:T(128)} %constant.1407.clone.1) | dynamic-update-slice | bytes 8388612 | tf_op jit(solution)/shard_map/scatter-add | solution.py:191
  931.9 5.2 slice_add_fusion.7
  937.2 20.2 %scatter-add.255 = f32[256,34,130]{0,2,1:T(8,128)} dynamic-update-slice(f32[256,34,130]{0,2,1:T(8,128)} %scatter-add.254, f32[256,32,128]{0,2,1:T(8,128)} %slice_add_fusion.7, s32[]{:T(128)} %constant.1398.clone.1, s32[]{:T(128)} %constant.1416.clone.1, s32[]{:T(128)} %constant.1416.clone.1) | dynamic-update-slice | bytes 8388612 | tf_op jit(solution)/shard_map/scatter-add | solution.py:191
  964.8 24.4 %scatter-add.260 = f32[384,34,130]{0,2,1:T(8,128)} dynamic-update-slice(f32[384,34,130]{0,2,1:T(8,128)} %scatter-add.259, f32[384,32,128]{0,2,1:T(8,128)} %bitcast_add_fusion, s32[]{:T(128)} %constant.1398.clone.1, s32[]{:T(128)} %bitcast.119, s32[]{:T(128)} %bitcast.120) | dynamic-update-slice | bytes 12582916 | tf_op jit(solution)/shard_map/scatter-add | solution.py:191
  989.2 8.8 add_select_fusion
  998.0 24.5 %scatter-add.261 = f32[384,34,130]{0,2,1:T(8,128)} dynamic-update-slice(f32[384,34,130]{0,2,1:T(8,128)} %scatter-add.260, f32[384,32,128]{0,2,1:T(8,128)} %add_select_fusion, s32[]{:T(128)} %constant.1398.clone.1, s32[]{:T(128)} %bitcast.123, s32[]{:T(128)} %bitcast.124) | dynamic-update-slice | bytes 12582916 | tf_op jit(solution)/shard_map/scatter-add | solution.py:191
  1022.5 6.6 fusion.11
  1029.1 6.7 slice_add_fusion.5
  1035.9 23.1 %scatter-add.265 = f32[384,34,130]{0,2,1:T(8,128)} dynamic-update-slice(f32[384,34,130]{0,2,1:T(8,128)} %fusion.11, f32[384,32,128]{0,2,1:T(8,128)} %slice_add_fusion.5, s32[]{:T(128)} %constant.1398.clone.1, s32[]{:T(128)} %constant.1407.clone.1, s32[]{:T(128)} %constant.1407.clone.1) | dynamic-update-slice | bytes 12582916 | tf_op jit(solution)/shard_map/scatter-add | solution.py:191
  1058.9 6.7 slice_add_fusion.4
  1065.7 23.1 %scatter-add.266 = f32[384,34,130]{0,2,1:T(8,128)} dynamic-update-slice(f32[384,34,130]{0,2,1:T(8,128)} %scatter-add.265, f32[384,32,128]{0,2,1:T(8,128)} %slice_add_fusion.4, s32[]{:T(128)} %constant.1398.clone.1, s32[]{:T(128)} %constant.1407.clone.1, s32[]{:T(128)} %constant.1416.clone.1) | dynamic-update-slice | bytes 12582916 | tf_op jit(solution)/shard_map/scatter-add | solution.py:191
  1088.7 6.6 fusion.10
  1095.3 6.7 slice_add_fusion.2
  1102.1 23.0 %scatter-add.270 = f32[384,34,130]{0,2,1:T(8,128)} dynamic-update-slice(f32[384,34,130]{0,2,1:T(8,128)} %fusion.10, f32[384,32,128]{0,2,1:T(8,128)} %slice_add_fusion.2, s32[]{:T(128)} %constant.1398.clone.1, s32[]{:T(128)} %constant.1416.clone.1, s32[]{:T(128)} %constant.1407.clone.1) | dynamic-update-slice | bytes 12582916 | tf_op jit(solution)/shard_map/scatter-add | solution.py:191
  1125.1 6.7 slice_add_fusion.1
  1131.9 23.0 %scatter-add.271 = f32[384,34,130]{0,2,1:T(8,128)} dynamic-update-slice(f32[384,34,130]{0,2,1:T(8,128)} %scatter-add.270, f32[384,32,128]{0,2,1:T(8,128)} %slice_add_fusion.1, s32[]{:T(128)} %constant.1398.clone.1, s32[]{:T(128)} %constant.1416.clone.1, s32[]{:T(128)} %constant.1416.clone.1) | dynamic-update-slice | bytes 12582916 | tf_op jit(solution)/shard_map/scatter-add | solution.py:191
  1154.9 8.6 fusion.9
  1187.3 9.9 reshape.2052
  1201.8 8.7 convert_reduce_fusion
  1219.9 17.3 %all-reduce.15 = (f32[32]{0:T(128)}, f32[32]{0:T(128)S(1)}, f32[1]{0:T(128)}) all-reduce(f32[32]{0:T(128)S(1)} %get-tuple-element.707, f32[32]{0:T(128)S(1)} %get-tuple-element.708, f32[1]{0:T(128)} %bitcast.312), channel_id=1, replica_groups=mesh['group'=4,'tile'=8] {'tile'}, use_global_device_ids=true, to_apply=%region_16.18 | all-reduce | flops 65 | bytes 520 | tf_op jit(solution)/shard_map/psum | solution.py:348
  1237.8 5.6 fusion.233
  1244.2 43.2 %concatenate.205 = f32[824320]{0:T(1024)} concatenate(f32[224]{0:T(256)S(1)} %reshape.2054, f32[32]{0:T(128)} %get-tuple-element.706, f32[32]{0:T(128)} %get-tuple-element.709, f32[8192]{0:T(1024)} %fusion.232, f32[128]{0:T(128)} %get-tuple-element.729, f32[221184]{0:T(1024)} %reshape.2056, f32[64]{0:T(128)} %reduce_sum.205, f32[147456]{0:T(1024)S(1)} %bitcast.941, ...), dimensions={0} | concatenate | bytes 6594560 | tf_op jit(solution)/shard_map/concatenate | solution.py:369
  1289.3 76.6 %all-reduce.19.cloned.1.call-done = f32[824320]{0:T(1024)} async-done(((f32[824320]{0:T(1024)}), f32[824320]{0:T(1024)}) %all-reduce.19.cloned.1.call-update) | async-done | bytes 3297296
  (536 shorter events, 425.2 us)
Async XLA Ops:
  7.2 53.1 %copy-start = (f32[7,35,512]{2,1,0:T(8,128)S(1)}, f32[7,35,512]{2,1,0:T(8,128)}, u32[]{:S(2)}) copy-start(f32[7,35,512]{2,1,0:T(8,128)} %param.126) | copy-start | bytes 1505284
  7.2 45.3 %all-gather.3.cloned.1.call-start = ((), (), s32[]{:S(2)}) async-start(), calls=%async_computation | async-start | bytes 3709440 | tf_op jit(solution)/shard_map/all_gather | solution.py:249
  9.3 1356.6 %all-reduce.19.cloned.1.call-start = ((), (), s32[]{:S(2)}) async-start(), calls=%async_computation.1 | async-start | bytes 6594560
  10.1 96.2 %copy-start.111 = (f32[512]{0:T(512)}, f32[512]{0:T(512)S(1)}, u32[]{:S(2)}) copy-start(f32[512]{0:T(512)S(1)} %convert_element_type.202) | copy-start | bytes 6148
  18.2 80.1 %copy-start.39 = (f32[35,512]{1,0:T(8,128)}, f32[35,512]{1,0:T(8,128)S(1)}, u32[]{:S(2)}) copy-start(f32[35,512]{1,0:T(8,128)S(1)} %fusion.407) | copy-start | bytes 215044
  54.0 39.3 %copy-start.116 = (f32[32]{0:T(128)}, f32[32]{0:T(128)S(1)}, u32[]{:S(2)}) copy-start(f32[32]{0:T(128)S(1)} %get-tuple-element.745) | copy-start | bytes 388
  54.0 39.3 %copy-start.118 = (f32[32]{0:T(128)}, f32[32]{0:T(128)S(1)}, u32[]{:S(2)}) copy-start(f32[32]{0:T(128)S(1)} %get-tuple-element.744) | copy-start | bytes 388
  55.3 42.9 %copy-start.121 = (f32[128]{0:T(128)}, f32[128]{0:T(128)S(1)}, u32[]{:S(2)}) copy-start(f32[128]{0:T(128)S(1)} %get-tuple-element.743) | copy-start | bytes 1540
  62.5 33.5 %copy-start.6 = (f32[32,35,512]{2,0,1:T(8,128)}, f32[32,35,512]{2,0,1:T(8,128)S(1)}, u32[]{:S(2)}) copy-start(f32[32,35,512]{2,0,1:T(8,128)S(1)} %get-tuple-element.776) | copy-start | bytes 6881284
  78.5 17.5 %copy-start.114 = (f32[32]{0:T(128)}, f32[32]{0:T(128)S(1)}, u32[]{:S(2)}) copy-start(f32[32]{0:T(128)S(1)} %broadcast_divide_fusion.3) | copy-start | bytes 388
  98.2 8.0 copy-start.55
  134.3 24.3 %copy-start.45 = (bf16[3,3,384,64]{2,3,1,0:T(8,128)(2,1)}, bf16[3,3,384,64]{2,3,1,0:T(8,128)(2,1)S(1)}, u32[]{:S(2)}) copy-start(bf16[3,3,384,64]{2,3,1,0:T(8,128)(2,1)S(1)} %reshape.2047) | copy-start | bytes 1327108
  139.7 53.5 %copy-start.49 = (bf16[3,3,256,64]{2,3,1,0:T(8,128)(2,1)}, bf16[3,3,256,64]{2,3,1,0:T(8,128)(2,1)S(1)}, u32[]{:S(2)}) copy-start(bf16[3,3,256,64]{2,3,1,0:T(8,128)(2,1)S(1)} %reshape.2046) | copy-start | bytes 884740
  143.4 7.1 copy-start.36
  143.4 7.1 copy-start.92
  152.4 6.8 copy-start.27
  152.8 6.4 copy-start.8
  154.8 13.9 %collective-permute-start = (bf16[512,1,128]{2,0,1:T(8,128)(2,1)}, bf16[512,1,128]{2,0,1:T(8,128)(2,1)}, u32[]{:S(2)}, u32[]{:S(2)}) collective-permute-start(bf16[512,1,128]{2,0,1:T(8,128)(2,1)} %get-tuple-element.739), channel_id=1, source_target_pairs={{0,1},{1,2},{2,3},{3,4},{4,5},{5,6},{6,7},{8,9},{9,10},{10,11},{11... | collective-permute-start | bytes 393224 | tf_op jit(solution)/shard_map/ppermute | solution.py:43
  157.3 11.5 collective-permute-start.1
  172.0 21.2 %copy-start.25 = (bf16[256,34,128]{2,0,1:T(8,128)(2,1)}, bf16[256,34,128]{2,0,1:T(8,128)(2,1)S(1)}, u32[]{:S(2)}) copy-start(bf16[256,34,128]{2,0,1:T(8,128)(2,1)S(1)} %slice.2478) | copy-start | bytes 6684676
  173.3 14.1 %copy-start.16 = (bf16[384,34,128]{2,0,1:T(8,128)(2,1)}, bf16[384,34,128]{2,0,1:T(8,128)(2,1)S(1)}, u32[]{:S(2)}) copy-start(bf16[384,34,128]{2,0,1:T(8,128)(2,1)S(1)} %slice.2490) | copy-start | bytes 10027012
  195.0 10.8 copy-start.19
  195.0 4.9 collective-permute-start.2
  198.1 3.2 collective-permute-start.3
  199.9 5.9 copy-start.66
  206.4 9.3 copy-start.43
  209.6 12.1 copy-start.21
  209.6 6.6 collective-permute-start.4
  214.2 3.1 collective-permute-start.5
  225.7 25.6 %copy-start.23 = (bf16[128,32,128]{2,0,1:T(8,128)(2,1)}, bf16[128,32,128]{2,0,1:T(8,128)(2,1)S(1)}, u32[]{:S(2)}) copy-start(bf16[128,32,128]{2,0,1:T(8,128)(2,1)S(1)} %get-tuple-element.781) | copy-start | bytes 3145732
  225.7 6.8 collective-permute-start.6
  229.7 3.1 collective-permute-start.7
  232.5 18.7 %copy-start.74 = (bf16[128,1,128]{2,0,1:T(8,128)(2,1)}, bf16[128,1,128]{2,0,1:T(8,128)(2,1)S(1)}, u32[]{:S(2)}) copy-start(bf16[128,1,128]{2,0,1:T(8,128)(2,1)S(1)} %collective-permute-done.6) | copy-start | bytes 98308
  232.8 15.4 %copy-start.72 = (bf16[128,1,128]{2,0,1:T(8,128)(2,1)}, bf16[128,1,128]{2,0,1:T(8,128)(2,1)S(1)}, u32[]{:S(2)}) copy-start(bf16[128,1,128]{2,0,1:T(8,128)(2,1)S(1)} %collective-permute-done.7) | copy-start | bytes 98308
  234.0 20.4 %copy-start.10 = (bf16[128,34,130]{2,0,1:T(8,128)(2,1)}, bf16[128,34,130]{2,0,1:T(8,128)(2,1)S(1)}, u32[]{:S(2)}) copy-start(bf16[128,34,130]{2,0,1:T(8,128)(2,1)S(1)} %select_maximum_fusion) | copy-start | bytes 3394564
  254.4 12.5 copy-start.62
  266.8 20.5 %copy-start.63 = (f32[14,32,128]{2,1,0:T(8,128)S(1)}, f32[14,32,128]{2,1,0:T(8,128)}, u32[]{:S(2)}) copy-start(f32[14,32,128]{2,1,0:T(8,128)} %param.130) | copy-start | bytes 688132
  266.8 20.5 %copy-start.76 = (f32[2,32,128]{2,1,0:T(8,128)S(1)}, f32[2,32,128]{2,1,0:T(8,128)}, u32[]{:S(2)}) copy-start(f32[2,32,128]{2,1,0:T(8,128)} %get-tuple-element.731) | copy-start | bytes 98308
  430.3 11.1 collective-permute-start.8
  431.6 9.8 collective-permute-start.9
  484.0 15.5 %copy-start.89 = (f32[32]{0:T(128)S(1)}, f32[32]{0:T(128)}, u32[]{:S(2)}) copy-start(f32[32]{0:T(128)} %get-tuple-element.766) | copy-start | bytes 388
  525.6 14.3 %copy-start.85 = (f32[32]{0:T(128)S(1)}, f32[32]{0:T(128)}, u32[]{:S(2)}) copy-start(f32[32]{0:T(128)} %get-tuple-element.765) | copy-start | bytes 388
  580.4 7.5 copy-start.69
  583.1 11.7 collective-permute-start.10
  586.1 8.6 collective-permute-start.11
  725.3 7.2 copy-start.65
  725.3 7.3 copy-start.110
  728.0 10.3 collective-permute-start.12
  731.0 7.3 collective-permute-start.13
  824.0 21.4 %copy-start.91 = (f32[32]{0:T(128)S(1)}, f32[32]{0:T(128)}, u32[]{:S(2)}) copy-start(f32[32]{0:T(128)} %get-tuple-element.766) | copy-start | bytes 388
  881.2 20.2 %copy-start.87 = (f32[32]{0:T(128)S(1)}, f32[32]{0:T(128)}, u32[]{:S(2)}) copy-start(f32[32]{0:T(128)} %get-tuple-element.765) | copy-start | bytes 388
  1163.6 11.0 copy-start.48
  1163.6 12.5 copy-start.1
  1168.7 15.1 %collective-permute-start.14 = (bf16[512,1,128]{0,2,1:T(8,128)(2,1)}, bf16[512,1,128]{0,2,1:T(8,128)(2,1)}, u32[]{:S(2)}, u32[]{:S(2)}) collective-permute-start(bf16[512,1,128]{0,2,1:T(8,128)(2,1)} %get-tuple-element.737), channel_id=1, source_target_pairs={{0,1},{1,2},{2,3},{3,4},{4,5},{5,6},{6,7},{8,9},{9,10},{10,11},{11... | collective-permute-start | bytes 393224 | tf_op jit(solution)/shard_map/ppermute | solution.py:43
  1173.2 10.6 collective-permute-start.15
  1187.3 9.9 copy-start.113
  1201.8 8.7 copy-start.54
  1201.8 8.7 copy-start.56
  1237.8 6.4 copy-start.58
  1237.8 6.4 copy-start.104
  1287.4 78.5 %copy-start.51 = (f32[103040]{0:T(1024)S(1)}, f32[103040]{0:T(1024)}, u32[]{:S(2)}) copy-start(f32[103040]{0:T(1024)} %param.131) | copy-start | bytes 1236484
  1287.4 78.5 %copy-start.59 = (f32[103040]{0:T(1024)S(1)}, f32[103040]{0:T(1024)}, u32[]{:S(2)}) copy-start(f32[103040]{0:T(1024)} %param.134) | copy-start | bytes 1236484
  1287.4 78.5 %copy-start.60 = (f32[103040]{0:T(1024)S(1)}, f32[103040]{0:T(1024)}, u32[]{:S(2)}) copy-start(f32[103040]{0:T(1024)} %param.133) | copy-start | bytes 1236484
  1287.4 78.5 %copy-start.61 = (f32[103040]{0:T(1024)S(1)}, f32[103040]{0:T(1024)}, u32[]{:S(2)}) copy-start(f32[103040]{0:T(1024)} %param.132) | copy-start | bytes 1236484
  (85 other events, 224.6 us)
Sparse Core Ops, SparseCore 0:
  10.2 42.2 all-gather.2
  1287.6 78.2 all-reduce.18
where the time goes:
time: 1400 us; the launch traced here: 1380 us
  local copies, waits for them, and re-layouts  700 us (50%)
  matrix products  354 us (25%)
  waiting for transfers between devices  114 us (8%)
  other arithmetic  87.9 us (6%)
  blocking collectives  62.8 us (4%)
  starting transfers between devices  37.7 us (3%)
  between operations  19.2 us (1%)
    scatter-add x35, local copies, waits for them, and re-layouts, conv_backward(): input_grad.at[:, i:i + row_count, j:j + col_count]  544 us
    dot_general x45, matrix products, conv_backward(): jnp.einsum('co,orw->crw', kernel[i, j], grad_pre, preferred_element_type=...  201 us
    unnamed x3, waiting for transfers between devices  76.7 us
    dot_general x45, matrix products, conv_forward(): jnp.einsum('co,crw->orw', kernel[i, j], window, preferred_element_type=jn...  70.4 us
    dot_general x45, matrix products, conv_backward(): jnp.einsum('crw,orw->co', window, grad_pre, preferred_element_type=jnp.fl...  54.9 us
    concatenate x1, local copies, waits for them, and re-layouts, shards(): full_grad = jnp.concatenate(pieces)  43.2 us
    all_gather x1, waiting for transfers between devices, shards(): flat_weights = lax.all_gather(weights, 'tile', axis=0, tiled=True)  34.4 us
    psum x2, blocking collectives, shards(): lax.psum((local_sums, local_total, local_positives), 'tile')  31.9 us
  transfers between devices with their start and end apart: 18, of which 5 were waited for; matrix products, arithmetic and copies ran while one was open for 4% of the time, Pallas kernels for 0%

commit v1 on v0

v1 whole, which is shorter than its diff:
```python
import functools
import math

import jax
import jax.numpy as jnp
from jax import lax
from jax.experimental import pallas as pl
from jax.experimental.pallas import tpu as pltpu
from jax.sharding import PartitionSpec as P

MESH = pl.DeviceIdType.MESH
F32 = jnp.float32
BF16 = jnp.bfloat16
HIGH = lax.Precision.HIGHEST

C1, C2, CM, CR1, CR2, CR3, ANCH, ZD = 32, 128, 64, 128, 128, 256, 2, 4
H_SCENE = 200
STEP = 10
LANES = 128
NORM_EPSILON = 1e-05
INNER_RATE = 0.05
FIRST_DECAY = 0.9
SECOND_DECAY = 0.999
ADAM_EPSILON = 1e-08
WEIGHT_DECAY = 0.01
OUTER_RATE = 0.7
OUTER_MOMENT = 0.9
FOCAL_ALPHA = 0.25
HUBER_BETA = 1.0 / 9.0

SMALL = 80
FC_ROW, FC_LANE = 2, 32
BIAS_ROWS = (1795, 2947, 2948, 4100, 4101, 6405, 6406, 6407, 6439)
RUN_A = (2, 32)
RUN_B = (1795, 96)
A_MID = 65
B_ONE, B_TWO, B_THREE, B_HEAD = 0, 1153, 2306, 4612
MSG = 48


def vmem():
    return pl.BlockSpec(memory_space=pltpu.VMEM)


def anywhere():
    return pl.BlockSpec(memory_space=pl.ANY)


def smem():
    return pl.BlockSpec(memory_space=pltpu.SMEM)


def ceil_to(value, step):
    return (value + step - 1) // step * step


def sigmoid(value):
    return 0.5 * jnp.tanh(0.5 * value) + 0.5


def slope(value):
    s = sigmoid(value)
    return s * (1.0 + value * (1.0 - s))


def nt(a, b, precision=None):
    return lax.dot_general(a, b, (((1,), (1,)), ((), ())), precision=precision, preferred_element_type=F32)


def tn(a, b, precision=None):
    return lax.dot_general(a, b, (((0,), (0,)), ((), ())), precision=precision, preferred_element_type=F32)


def nn(a, b, precision=None):
    return lax.dot_general(a, b, (((1,), (0,)), ((), ())), precision=precision, preferred_element_type=F32)


def lane_of(shape):
    return lax.broadcasted_iota(jnp.int32, shape, len(shape) - 1)


def row_of(shape):
    return lax.broadcasted_iota(jnp.int32, shape, len(shape) - 2)


def enter(n, me):
    sem = pltpu.get_barrier_semaphore()

    def greet(k, carry):
        pl.semaphore_signal(
            sem, inc=1, device_id={"tile": lax.rem(me + k, n)}, device_id_type=MESH
        )
        return carry

    lax.fori_loop(1, n, greet, 0)
    pl.semaphore_wait(sem, n - 1)


def remote(src, dst, send, recv, peer):
    return pltpu.make_async_remote_copy(
        src_ref=src,
        dst_ref=dst,
        send_sem=send,
        recv_sem=recv,
        device_id={"tile": peer},
        device_id_type=MESH,
    )


def even_first():
    out = row_of((LANES, LANES))
    source = jnp.where(out < 64, 2 * out, 2 * out - 127)
    return lane_of((LANES, LANES)) == source


def first_layer(small_ref):
    turned = jnp.transpose(small_ref[0:LANES_PAD, :])
    columns = [turned[(k % 4) * 32 : (k % 4) * 32 + 32, k // 4 : k // 4 + 1] for k in range(7)]
    return columns, turned[96:128, 1:2], turned[0:32, 2:3]


LANES_PAD = 8


def voxel_rows(small_ref):
    here, after = small_ref[2:74, :], small_ref[3:75, :]
    mixed = jnp.where(lane_of((72, LANES)) >= FC_LANE, here, after)
    return pltpu.roll(mixed, LANES - FC_LANE, axis=1)


def front_kernel(
    n, points_hbm, counts_ref, labels_ref, shard_ref,
    wall, small, stat, linear, joined, feature,
    points, own, mine, msgs, sem_p, sem_small_s, sem_small_r, sem_msg_s, sem_msg_r, sem_w_s, sem_w_r, sem_f_s,
):
    me = lax.axis_index("tile")
    rows = shard_ref.shape[0]
    slots, voxels = points_hbm.shape[1], points_hbm.shape[2]
    sibling = me + 1 - 2 * lax.rem(me, 2)
    loads = [
        pltpu.make_async_copy(points_hbm.at[k], points.at[:, k, :], sem_p.at[k]) for k in range(7)
    ]
    for load in loads:
        load.start()
    own[...] = jnp.zeros_like(own)
    own[0:rows, :] = shard_ref[...].astype(BF16)
    enter(n, me)

    def small_copy(k):
        peer = lax.rem(me + k, n)
        return remote(small, small, sem_small_s.at[k], sem_small_r.at[0], peer)

    @pl.when(me == 0)
    def _():
        small[...] = shard_ref[0:SMALL, :]

        def send(k, carry):
            small_copy(k).start()
            return carry

        lax.fori_loop(1, n, send, 0)

    def shard_copy(k):
        return remote(own, wall.at[me], sem_w_s.at[k], sem_w_r.at[me], lax.rem(me + 2 * k, n))

    half = n // 2
    for k in range(1, half):
        shard_copy(k).start()
    to_sibling = remote(own, wall.at[me], sem_w_s.at[0], sem_w_r.at[me], sibling)
    to_sibling.start()
    wall[me] = own[...]

    counts = counts_ref[...]
    slot_no = row_of((slots, voxels))
    mask_all = (slot_no < counts).astype(F32)
    for load in loads:
        load.wait()
    point_sums = jnp.zeros((32, 1), F32)
    row32 = row_of((32, 1))
    for k in range(7):
        total = jnp.sum(jnp.sum(points[:, k, :] * mask_all, axis=1, keepdims=True), axis=0, keepdims=True)
        point_sums = point_sums + jnp.where(row32 == k, total, 0.0)
    positives = jnp.zeros((1, 1), F32)
    for a in range(ANCH):
        hits = (labels_ref[a] == 1).astype(F32)
        positives += jnp.sum(jnp.sum(hits, axis=1, keepdims=True), axis=0, keepdims=True)
    held = jnp.sum(jnp.sum(mask_all, axis=1, keepdims=True), axis=0, keepdims=True)
    for a, row in enumerate(BIAS_ROWS):
        owner, place = row // rows, row % rows
        mine[32 + a : 33 + a, :] = jnp.where(me == owner, shard_ref[place : place + 1, :], 0.0)
    for a in range(len(BIAS_ROWS), MSG - 32):
        mine[32 + a : 33 + a, :] = jnp.zeros((1, LANES), F32)

    @pl.when(me > 0)
    def _():
        small_copy(0).wait_recv()

    columns, gamma, beta = first_layer(small)
    wide = [jnp.broadcast_to(c, (32, voxels)) for c in columns]

    def pass_a(p, total):
        value = wide[0] * points[p, 0:1, :]
        for k in range(1, 7):
            value += wide[k] * points[p, k : k + 1, :]
        linear[p] = value
        return total + jnp.where(p < counts, value, 0.0)

    total = lax.fori_loop(0, slots, pass_a, jnp.zeros((32, voxels), F32), unroll=5)
    local_sum = jnp.sum(total, axis=1, keepdims=True)
    local_mean = local_sum / held

    def pass_b(p, total):
        off = linear[p] - local_mean
        return total + jnp.where(p < counts, off * off, 0.0)

    total = lax.fori_loop(0, slots, pass_b, jnp.zeros((32, voxels), F32), unroll=5)
    local_square = jnp.sum(total, axis=1, keepdims=True)
    lane = lane_of((32, LANES))
    packed = jnp.where(lane == 0, local_sum, 0.0)
    packed = jnp.where(lane == 1, local_square, packed)
    packed = jnp.where(lane == 2, held, packed)
    packed = jnp.where(lane == 3, positives, packed)
    packed = jnp.where(lane == 4, point_sums, packed)
    mine[0:32, :] = packed

    def message(k):
        return remote(mine, msgs.at[me], sem_msg_s.at[k], sem_msg_r.at[me], lax.rem(me + k, n))

    for k in range(1, n):
        message(k).start()
    msgs[me] = mine[...]
    for k in range(1, n):
        sender = lax.rem(me + n - k, n)
        remote(mine, msgs.at[sender], sem_msg_s.at[k], sem_msg_r.at[sender], sender).wait_recv()
    sums = msgs[0]
    for d in range(1, n):
        sums += msgs[d]
    held_all = sums[0:32, 2:3]
    mean = sums[0:32, 0:1] / held_all
    square = sums[0:32, 1:2]
    for d in range(n):
        held_d = msgs[d, 0:32, 2:3]
        off = msgs[d, 0:32, 0:1] / held_d - mean
        square += held_d * off * off
    inverse = lax.rsqrt(square / held_all + NORM_EPSILON)
    columns_out = jnp.where(lane == 0, mean, 0.0)
    columns_out = jnp.where(lane == 1, inverse, columns_out)
    columns_out = jnp.where(lane == 2, held_all, columns_out)
    columns_out = jnp.where(lane == 3, sums[0:32, 3:4], columns_out)
    columns_out = jnp.where(lane == 4, sums[0:32, 4:5] / held_all, columns_out)
    stat[0:32, :] = columns_out
    stat[32:MSG, :] = sums[32:MSG, :]

    inverse_counts = 1.0 / counts.astype(F32)

    def pass_c(p, pooled):
        act = gamma * ((linear[p] - mean) * inverse) + beta
        out = jnp.where(p < counts, act * sigmoid(act), 0.0)
        joined[p, 0:32, :] = out.astype(BF16)
        return pooled + out

    pooled = lax.fori_loop(0, slots, pass_c, jnp.zeros((32, voxels), F32), unroll=5)
    pooled = (pooled / counts.astype(F32)).astype(BF16)
    order = even_first()
    rows_fc = voxel_rows(small)
    kernel_t = nt(order.astype(BF16), rows_fc[0:64, :].astype(BF16)).astype(BF16)
    bias = jnp.sum(jnp.where(order, rows_fc[64:65, :], 0.0), axis=1, keepdims=True)
    tail = jnp.where(row_of((16, voxels)) == 0, 1.0, 0.0).astype(BF16)

    def pass_d(p, total):
        inside = p < counts
        joined[p, 32:64, :] = jnp.where(inside, pooled.astype(F32), 0.0).astype(BF16)
        joined[p, 64:80, :] = tail
        inner = nn(kernel_t, joined[p, 0:64, :]) + bias
        return total + jnp.where(inside, inner * sigmoid(inner), 0.0)

    total = lax.fori_loop(0, slots, pass_d, jnp.zeros((LANES, voxels), F32))
    feature[...] = jnp.transpose(total / counts.astype(F32))

    for k in range(1, half):
        source = lax.rem(me + n - 2 * k, n)
        remote(own, wall.at[source], sem_w_s.at[k], sem_w_r.at[source], source).wait_recv()
        remote(wall.at[source], wall.at[source], sem_f_s.at[k], sem_w_r.at[source], sibling).start()
    for k in range(half):
        source = lax.rem(sibling + n - 2 * k, n)
        remote(own, wall.at[source], sem_w_s.at[k], sem_w_r.at[source], source).wait_recv()
    for k in range(1, half):
        source = lax.rem(me + n - 2 * k, n)
        remote(wall.at[source], wall.at[source], sem_f_s.at[k], sem_w_r.at[source], sibling).wait_send()
        shard_copy(k).wait_send()
    to_sibling.wait_send()
    for k in range(1, n):
        message(k).wait_send()

    @pl.when(me == 0)
    def _():
        def done(k, carry):
            small_copy(k).wait_send()
            return carry

        lax.fori_loop(1, n, done, 0)


def front(n, points, counts, labels, shard):
    slots, voxels = points.shape[1:]
    rows = shard.shape[0]
    padded = ceil_to(rows, 16)
    shape = jax.ShapeDtypeStruct
    dma = pltpu.SemaphoreType.DMA
    return pl.pallas_call(
        functools.partial(front_kernel, n),
        name="front",
        out_shape=(
            shape((n, padded, LANES), BF16),
            shape((SMALL, LANES), F32),
            shape((MSG, LANES), F32),
            shape((slots, 32, voxels), F32),
            shape((slots, 80, voxels), BF16),
            shape((voxels, LANES), F32),
        ),
        in_specs=[anywhere(), vmem(), vmem(), vmem()],
        out_specs=(vmem(),) * 6,
        scratch_shapes=[
            pltpu.VMEM((slots, 8, voxels), F32),
            pltpu.VMEM((padded, LANES), BF16),
            pltpu.VMEM((MSG, LANES), F32),
            pltpu.VMEM((n, MSG, LANES), F32),
            dma((7,)), dma((n,)), dma((1,)), dma((n,)), dma((n,)), dma((n,)), dma((n,)), dma((n,)),
        ],
        compiler_params=pltpu.CompilerParams(
            collective_id=1, has_side_effects=True, vmem_limit_bytes=56 << 20
        ),
    )(points, counts, labels, shard)


def layout(n, row_count):
    first = lax.axis_index("tile") * row_count
    ahead = (first // H_SCENE + 1) * H_SCENE - first
    split = jnp.where(ahead < row_count, 1, 0)
    edge = jnp.where(ahead < row_count, ahead, row_count)
    top = jnp.where(lax.rem(first, H_SCENE) != 0, 1, 0)
    last = first + row_count
    bottom = jnp.where((lax.rem(last, H_SCENE) != 0) & (last < n * row_count), 1, 0)
    return edge, split, top, bottom


def place_ok(place, edge, split, row_count):
    return (place >= 1) & (place <= row_count + split) & ((place != edge + 1) | (split == 0))


def place_row(place, edge, row_count):
    row = jnp.where(place <= edge, place - 1, place - 2)
    return jnp.clip(row, 0, row_count - 1)


PITCH = 136


def voxel_base(cell, depth_cells, columns, edge, split):
    local = lax.rem(cell, depth_cells)
    spot = local // ZD
    row = spot // columns
    column = spot - row * columns
    place = row + 1 + jnp.where((row >= edge) & (split == 1), 1, 0)
    return place * PITCH + column + 7


def z_columns(cells_row):
    z = lax.rem(cells_row, ZD).astype(F32)
    return jnp.transpose(jnp.broadcast_to(z, (8, z.shape[1])))[:, 0:1]


def spread_z(feature, z_column, out_ref):
    for z in range(ZD):
        out_ref[:, z * C2 : (z + 1) * C2] = jnp.where(z_column == z, feature, 0.0).astype(BF16)


def middle_kernel(
    n, rows, row_count,
    cells_smem, cells_row, feature, wall,
    pre, w_mid, f_one, f_two, f_three, d_one, d_two, d_three, head_t,
    flat, run, spread, parts0, parts1, parts2, sum0, sum1, sum2,
):
    edge, split, _, _ = layout(n, row_count)
    voxels = feature.shape[0]
    columns = LANES
    parts, sums = (parts0, parts1, parts2), (sum0, sum1, sum2)
    for s in range(n):
        flat[s * rows : s * rows + wall.shape[1], :] = wall[s].astype(F32)

    def aligned(begin, start, count):
        row, lane = begin
        here = flat[pl.ds(row + start, count), :]
        after = flat[pl.ds(row + start + 1, count), :]
        mixed = jnp.where(lane_of((count, LANES)) >= lane, here, after)
        return pltpu.roll(mixed, LANES - lane, axis=1)

    low = lane_of((64, LANES)) < 64
    for ij in range(9):
        taps = [aligned(RUN_A, A_MID + (t * 9 + ij) * 64, 64) for t in range(3)]
        turned = [pltpu.roll(tap, 64, axis=1) for tap in taps]
        none = jnp.zeros((64, LANES), F32)
        for z in range(ZD):
            first, second = z + 1, z - 1
            a, a_t = (taps[first], turned[first]) if first < 3 else (none, none)
            b, b_t = (taps[second], turned[second]) if second >= 0 else (none, none)
            lanes = slice(ij * LANES, (ij + 1) * LANES)
            w_mid[z * C2 : z * C2 + 64, lanes] = jnp.where(low, a, b_t).astype(BF16)
            w_mid[z * C2 + 64 : (z + 1) * C2, lanes] = jnp.where(low, a_t, b).astype(BF16)

    spread_z(feature[...], z_columns(cells_row[...]), spread)
    for i in range(3):
        product = nn(spread[...], w_mid[:, i * 384 : (i + 1) * 384])
        for j in range(3):
            parts[i][pl.ds(2 - j, voxels, 4), :] = product[:, j * LANES : (j + 1) * LANES]
        sums[i][...] = jnp.zeros_like(sums[i])

    depth_cells = row_count * columns * ZD

    def add(v, carry):
        base = voxel_base(cells_smem[v], depth_cells, columns, edge, split)
        for i in range(3):
            spot = pl.ds(base + (1 - i) * PITCH, 3)
            sums[i][spot, :] = sums[i][spot, :] + parts[i][pl.ds(4 * v, 3), :]
        return carry

    lax.fori_loop(0, voxels, add, 0, unroll=4)

    def gather(p, carry):
        spot = pl.ds(pl.multiple_of(p * PITCH + 8, 8), columns)
        pre[p] = sum0[spot, :] + sum1[spot, :] + sum2[spot, :]
        return carry

    lax.fori_loop(0, row_count + 5, gather, 0)

    def zero_half(ref, row, column, height, width):
        ref[row : row + height, column : column + width] = jnp.zeros((height, width), BF16)

    for begin, f_ref, d_ref in ((B_ONE, f_one, d_one), (B_TWO, f_two, d_two)):
        for j in range(3):
            for e in range(2):
                outside = 3 if e == 0 else 0
                zero_half(f_ref, outside * 384 + j * LANES, e * LANES, LANES, LANES)
                zero_half(d_ref, e * LANES, outside * 384 + j * LANES, LANES, LANES)

        def tap(i, j, begin=begin, f_ref=f_ref, d_ref=d_ref):
            block = aligned(RUN_B, begin + (i * 3 + j) * LANES, LANES).astype(BF16)
            for e in range(2):
                t = i + e
                f_ref[t * 384 + j * LANES : t * 384 + (j + 1) * LANES, e * LANES : (e + 1) * LANES] = block
                t = 2 + e - i
                lane = t * 384 + (2 - j) * LANES
                d_ref[e * LANES : (e + 1) * LANES, lane : lane + LANES] = block

        for i in range(3):
            for j in range(3):
                tap(i, j)
    for j in range(3):
        for e in range(2):
            outside = 3 if e == 0 else 0
            zero_half(d_three, e * LANES, outside * 768 + j * 256, LANES, 256)
    for i in range(3):
        for j in range(3):
            run[...] = aligned(RUN_B, B_THREE + (i * 3 + j) * 256, 256)
            for h in range(2):
                block = run[pl.ds(h, LANES, 2), :].astype(BF16)
                row = (i * 3 + j) * LANES
                f_three[row : row + LANES, h * LANES : (h + 1) * LANES] = block
                for e in range(2):
                    lane = (2 + e - i) * 768 + (2 - j) * 256 + h * LANES
                    d_three[e * LANES : (e + 1) * LANES, lane : lane + LANES] = block
    head_rows = aligned(RUN_B, B_HEAD, 32).astype(BF16)
    chosen = nn(eighths(), head_rows)
    chosen = jnp.where(same_eighth(), chosen, 0.0).astype(BF16)
    head_t[...] = nt(fold16(), chosen).astype(BF16)


def eighths():
    return (row_of((CR3, 32)) // 8 == lane_of((CR3, 32))).astype(F32).astype(BF16)


def same_eighth():
    return lane_of((CR3, LANES)) // 16 == lax.rem(row_of((CR3, LANES)), 8)


def fold16():
    return (lax.rem(lane_of((16, LANES)), 16) == row_of((16, LANES))).astype(F32).astype(BF16)


def middle(n, rows, row_count, cells, feature, wall):
    shape = jax.ShapeDtypeStruct
    voxels = feature.shape[0]
    cells_all = (row_count + 6) * PITCH
    return pl.pallas_call(
        functools.partial(middle_kernel, n, rows, row_count),
        name="middle",
        out_shape=(
            shape((row_count + 5, LANES, LANES), F32),
            shape((512, 1152), BF16),
            shape((1536, 256), BF16),
            shape((1536, 256), BF16),
            shape((1152, 256), BF16),
            shape((256, 1536), BF16),
            shape((256, 1536), BF16),
            shape((256, 3072), BF16),
            shape((16, 256), BF16),
        ),
        in_specs=[smem(), vmem(), vmem(), vmem()],
        out_specs=(vmem(),) * 9,
        scratch_shapes=[
            pltpu.VMEM((n * rows + 24, LANES), F32),
            pltpu.VMEM((256, LANES), F32),
            pltpu.VMEM((voxels, ZD * C2), BF16),
            pltpu.VMEM((voxels * 4, LANES), F32),
            pltpu.VMEM((voxels * 4, LANES), F32),
            pltpu.VMEM((voxels * 4, LANES), F32),
            pltpu.VMEM((cells_all, LANES), F32),
            pltpu.VMEM((cells_all, LANES), F32),
            pltpu.VMEM((cells_all, LANES), F32),
        ],
        compiler_params=pltpu.CompilerParams(vmem_limit_bytes=56 << 20),
    )(cells, cells.reshape(1, -1), feature, wall)


PAIRS = 18
QB = 9
STEPS = PAIRS // QB
SPAN = QB * LANES
GRID = PAIRS * LANES
A_ROWS, B_ROWS = 1800, 4656


def conv_kernel(
    n, row_count,
    cells_smem, cells_row, feature, stat, pre_in, w_mid, f_one, f_two, f_three, d_one, d_two, d_three, head_t,
    labels_hbm, boxes_hbm,
    grad_a, grad_b, grad_feature, loss_out,
    x_one, x_two, x_three, pre_mid, pre_one, pre_two, back, spread,
    acc0, acc1, acc2,
    labels, boxes, logit_grads, loss_mine, loss_all,
    up_f, down_f, from_up_f, from_down_f, send_up, send_down, from_up, from_down,
    send_up_w, send_down_w, from_up_w, from_down_w,
    sem_t, sem_fs, sem_fr, sem_s, sem_r, sem_ws, sem_wr, sem_ls, sem_lr,
):
    me = lax.axis_index("tile")
    edge, split, top, bottom = layout(n, row_count)
    has_up, has_down = me > 0, me < n - 1
    above, below = jnp.maximum(me - 1, 0), jnp.minimum(me + 1, n - 1)
    loads = [pltpu.make_async_copy(labels_hbm.at[a], labels.at[:, a, :], sem_t.at[a]) for a in range(2)]
    loads += [
        pltpu.make_async_copy(boxes_hbm.at[a], boxes.at[:, 2 + a, :], sem_t.at[2 + a]) for a in range(14)
    ]
    for load in loads:
        load.start()
    enter(n, me)

    def ok(place):
        return place_ok(place, edge, split, row_count)

    def halo_copies(s, up_src, down_src, up_dst, down_dst, sem_send, sem_recv):
        up = remote(up_src, down_dst, sem_send.at[2 * s], sem_recv.at[2 * s], above)
        down = remote(down_src, up_dst, sem_send.at[2 * s + 1], sem_recv.at[2 * s + 1], below)
        return up, down

    def halo_start(copies):
        up, down = copies

        @pl.when(has_up)
        def _():
            up.start()

        @pl.when(has_down)
        def _():
            down.start()

    def halo_wait(copies):
        up, down = copies

        @pl.when(has_up)
        def _():
            up.wait_send()
            down.wait_recv()

        @pl.when(has_down)
        def _():
            down.wait_send()
            up.wait_recv()

    def thin(s):
        return halo_copies(
            s, send_up.at[s], send_down.at[s], from_up.at[s], from_down.at[s], sem_s, sem_r
        )

    def pick(condition, a, b):
        return jnp.where(condition, a, b)

    column = row_of((LANES, LANES))

    def shifted(value):
        left = jnp.where(column > 0, pltpu.roll(value, 1, axis=0), 0.0)
        right = jnp.where(column < LANES - 1, pltpu.roll(value, LANES - 1, axis=0), 0.0)
        return left.astype(BF16), value.astype(BF16), right.astype(BF16)

    def put(ref, pair, parity, value, part, parts):
        rows = pl.ds(pl.multiple_of(pair * LANES, LANES), LANES)
        width = 3 * parts * LANES
        for j, shift in enumerate(shifted(value)):
            lane = parity * width + (j * parts + part) * LANES
            ref[rows, lane : lane + LANES] = shift

    def put_edges(ref, s, parts, up_halo, down_halo):
        for part in range(parts):
            lanes = slice(part * LANES, (part + 1) * LANES)
            halo = pick((top == 1) & has_up, up_halo[:, lanes].astype(F32), 0.0)
            put(ref, 0, 0, halo, part, parts)
            halo = pick((bottom == 1) & has_down, down_halo[:, lanes].astype(F32), 0.0)
            width = 3 * parts * LANES
            row = pl.ds(16 * LANES, LANES)
            for j, shift in enumerate(shifted(halo)):
                lane = width + (j * parts + part) * LANES
                ref[row, lane : lane + LANES] = pick(split == 1, ref[row, lane : lane + LANES], shift)
            put(ref, 17, 0, pick(split == 1, halo, 0.0), part, parts)

    grad_b[B_HEAD + 32 :, :] = jnp.zeros((B_ROWS - B_HEAD - 32, LANES), F32)
    up_f[...] = pre_in[0]
    down_f[...] = pick(split == 1, pre_in[row_count + 2], pre_in[row_count + 1])
    copies = halo_copies(0, up_f, down_f, from_up_f, from_down_f, sem_fs, sem_fr)
    halo_start(copies)
    for ref, wide in ((x_one, 768), (x_two, 768), (x_three, 768)):
        ref[0:LANES, 0:384] = jnp.zeros((LANES, 384), BF16)
        ref[18 * LANES : 20 * LANES, :] = jnp.zeros((2 * LANES, wide), BF16)
    spread_z(feature[...], z_columns(cells_row[...]), spread)
    halo_wait(copies)

    bias_mid = stat[32:33, :]
    b_mid = jnp.concatenate([bias_mid[:, 32:96], bias_mid[:, 32:96]], axis=1)
    last = row_count

    def fold(q, carry):
        for e in range(2):
            p = 2 * q + 1 + e
            value = pre_in[p] + b_mid
            value += pick((p == 1) & (top == 1) & has_up, from_up_f[...], 0.0)
            value += pick((p == last + split) & (bottom == 1) & has_down, from_down_f[...], 0.0)
            pre_mid[pl.ds(pl.multiple_of(q * LANES, LANES), LANES), e * LANES : (e + 1) * LANES] = value
        return carry

    lax.fori_loop(0, PAIRS, fold, 0)

    def activate(pre_ref, x_ref, s):
        def step(q, carry):
            rows = pl.ds(pl.multiple_of(q * LANES, LANES), LANES)
            for e in range(2):
                value = pre_ref[rows, e * LANES : (e + 1) * LANES]
                value = pick(ok(2 * q + 1 + e), value * sigmoid(value), 0.0)
                put(x_ref, q + e, 1 - e, value, 0, 1)
            return carry

        lax.fori_loop(0, PAIRS, step, 0)
        exchange(x_ref, s)
        copies = thin(s)
        halo_wait(copies)
        put_edges(x_ref, s, 1, from_up[s], from_down[s])

    def exchange(x_ref, s):
        send_up[s] = x_ref[0:LANES, 512:640]
        send_down[s] = pick(split == 1, x_ref[16 * LANES : 17 * LANES, 512:640], x_ref[16 * LANES : 17 * LANES, 128:256])
        halo_start(thin(s))

    def banded(x_ref, f_ref, bias, out_ref):
        def step(b, carry):
            start = pl.multiple_of(b * SPAN, LANES)
            total = nn(x_ref[pl.ds(start, SPAN), :], f_ref[0:768, :])
            total += nn(x_ref[pl.ds(start + LANES, SPAN), :], f_ref[768:1536, :])
            out_ref[pl.ds(start, SPAN), :] = total + bias
            return carry

        lax.fori_loop(0, STEPS, step, 0)

    def banded_back(g_ref, d_ref, out_ref):
        width = g_ref.shape[1]

        def step(b, carry):
            start = pl.multiple_of(b * SPAN, LANES)
            total = nt(g_ref[pl.ds(start, SPAN), :], d_ref[:, 0:width])
            total += nt(g_ref[pl.ds(start + LANES, SPAN), :], d_ref[:, width : 2 * width])
            out_ref[pl.ds(start, SPAN), :] = total
            return carry

        lax.fori_loop(0, STEPS, step, 0)

    def bias_row(first, lane):
        mixed = jnp.where(lane_of((1, LANES)) >= lane, stat[first : first + 1, :], stat[first + 1 : first + 2, :])
        return pltpu.roll(jnp.broadcast_to(mixed, (8, LANES)), LANES - lane, axis=1)[0:1, :]

    def twice(row):
        return jnp.concatenate([row, row], axis=1)

    activate(pre_mid, x_one, 0)
    banded(x_one, f_one, twice(bias_row(33, 96)), pre_one)
    activate(pre_one, x_two, 1)
    banded(x_two, f_two, twice(bias_row(35, 96)), pre_two)
    activate(pre_two, x_three, 2)

    def weight_grads(g_ref, x_ref, parts, write):
        width, wide = parts * LANES, 3 * parts * LANES
        middle0 = slice(width, 2 * width)
        middle1 = slice(wide + width, wide + 2 * width)
        acc0[0 : 2 * width, :] = jnp.zeros((2 * width, 768), F32)
        acc1[0:width, :] = jnp.zeros((width, 384), F32)
        acc2[0:width, :] = jnp.zeros((width, 384), F32)

        def step(b, carry):
            start = pl.multiple_of(b * SPAN, LANES)
            rows = pl.ds(start, SPAN)
            g0, g1 = g_ref[rows, middle0], g_ref[rows, middle1]
            both = jnp.concatenate([g0, g1], axis=1)
            acc0[0 : 2 * width, :] += tn(both, x_ref[rows, :])
            acc2[0:width, :] += tn(g1, x_ref[pl.ds(start + LANES, SPAN), 0:384])
            after = g_ref[pl.ds(start + LANES, SPAN), middle0]
            acc1[0:width, :] += tn(after, x_ref[rows, 384:768])
            return carry

        lax.fori_loop(0, STEPS, step, 0)
        for i in range(3):
            if i == 0:
                total = acc0[width : 2 * width, 0:384] + acc1[0:width, :]
            elif i == 1:
                total = acc0[0:width, 0:384] + acc0[width : 2 * width, 384:768]
            else:
                total = acc0[0:width, 384:768] + acc2[0:width, :]
            for j in range(3):
                for part in range(parts):
                    block = total[part * LANES : (part + 1) * LANES, j * LANES : (j + 1) * LANES]
                    write(i, j, part, jnp.transpose(block))

    def bias_grads(g_ref, parts):
        width, wide = parts * LANES, 3 * parts * LANES
        ones = jnp.ones((16, SPAN), BF16)

        def step(b, total):
            rows = pl.ds(pl.multiple_of(b * SPAN, LANES), SPAN)
            total += nn(ones, g_ref[rows, width : 2 * width])
            return total + nn(ones, g_ref[rows, wide + width : wide + 2 * width])

        return lax.fori_loop(0, STEPS, step, jnp.zeros((16, width), F32))[0:1, :]

    def last_layers(pre_three, x_head, g_three):
        bias = jnp.concatenate([bias_row(37, 96), bias_row(38, 96)], axis=1)

        def conv_step(b, carry):
            start = pl.multiple_of(b * SPAN, LANES)
            rows, more = pl.ds(start, SPAN), pl.ds(start + LANES, SPAN)
            total = nn(x_ref3[rows, :], f_three[0:768, :]) + nn(x_ref3[more, 0:384], f_three[768:1152, :])
            pre_three[rows, 0:256] = total + bias
            total = nn(x_ref3[rows, 384:768], f_three[0:384, :]) + nn(x_ref3[more, :], f_three[384:1152, :])
            pre_three[rows, 256:512] = total + bias
            return carry

        x_ref3 = x_three
        lax.fori_loop(0, STEPS, conv_step, 0)

        def head_step(q, carry):
            rows = pl.ds(pl.multiple_of(q * LANES, LANES), LANES)
            value = pre_three[rows, :]
            x_head[rows, :] = (value * sigmoid(value)).astype(BF16)
            return carry

        lax.fori_loop(0, PAIRS, head_step, 0)
        for load in loads:
            load.wait()
        head_row = jnp.broadcast_to(stat[40:41, :], (LANES, LANES))
        b_head = jnp.sum(jnp.where(lane_of((16, LANES)) == row_of((16, LANES)) + 96, head_row[0:16, :], 0.0), axis=1, keepdims=True)
        divisor = jnp.maximum(stat[0:1, 3:4], 1.0)
        inverse = 1.0 / divisor
        row16 = row_of((16, LANES))

        def loss_tile(logits, place):
            row = place_row(place, edge, row_count)
            label = labels[row]
            kind = jnp.concatenate([label, jnp.zeros((14, LANES), jnp.int32)], axis=0)
            is_class = row16 < 2
            anchor0, anchor1 = label[0:1, :] == 1, label[1:2, :] == 1
            box_on = ((row16 < 9) & anchor0) | ((row16 >= 9) & anchor1)
            positive = (kind == 1).astype(F32)
            negative = (kind == 0).astype(F32)
            q = 1.0 / (1.0 + jnp.exp(-logits))
            rest = jnp.log(1.0 + jnp.exp(-jnp.abs(logits)))
            log_q = jnp.minimum(logits, 0.0) - rest
            log_not = jnp.minimum(-logits, 0.0) - rest
            short = 1.0 - q
            focal = -FOCAL_ALPHA * positive * short * short * log_q
            focal -= (1.0 - FOCAL_ALPHA) * negative * q * q * log_not
            slope_p = FOCAL_ALPHA * (2.0 * q * short * short * log_q - short * short * short)
            slope_n = (1.0 - FOCAL_ALPHA) * (q * q * q - 2.0 * q * q * short * log_not)
            residual = logits - boxes[row]
            size = jnp.abs(residual)
            huber = jnp.where(size < HUBER_BETA, (0.5 / HUBER_BETA) * residual * residual, size - 0.5 * HUBER_BETA)
            bent = jnp.clip(residual * (1.0 / HUBER_BETA), -1.0, 1.0)
            value = jnp.where(is_class, focal, jnp.where(box_on, 2.0 * huber, 0.0))
            grad = jnp.where(is_class, positive * slope_p + negative * slope_n, jnp.where(box_on, 2.0 * bent, 0.0))
            good = ok(place)
            return pick(good, value, 0.0), pick(good, grad * inverse, 0.0)

        def loss_step(q, total):
            rows = pl.ds(pl.multiple_of(q * LANES, LANES), LANES)
            for e in range(2):
                logits = nt(head_t[...], x_head[rows, e * 256 : (e + 1) * 256]) + b_head
                value, grad = loss_tile(logits, 2 * q + 1 + e)
                logit_grads[e, :, rows] = grad.astype(BF16)
                total = total + value
            return total

        total = lax.fori_loop(0, PAIRS, loss_step, jnp.zeros((16, LANES), F32), unroll=3)
        total = jnp.sum(jnp.sum(total, axis=1, keepdims=True), axis=0, keepdims=True)
        loss_mine[...] = jnp.broadcast_to(total, (8, LANES))
        for k in range(1, n):
            loss_copy(k).start()
        g_head = jnp.zeros((16, CR3), F32)
        g_bias = jnp.zeros((16, 1), F32)
        for e in range(2):
            g_head += nn(logit_grads[e], x_head[0:GRID, e * 256 : (e + 1) * 256])
            g_bias += jnp.sum(logit_grads[e].astype(F32), axis=1, keepdims=True)
        back_rows = jnp.where(same_eighth(), tn(g_head, fold16().astype(F32), HIGH), 0.0)
        grad_b[B_HEAD : B_HEAD + 32, :] = tn(eighths().astype(F32), back_rows, HIGH)
        spots = (lane_of((16, LANES)) == row_of((16, LANES))).astype(F32)
        grad_b[B_HEAD + 32 : B_HEAD + 33, :] = jnp.sum(spots * g_bias, axis=0, keepdims=True)

        def back_step(q, carry):
            rows = pl.ds(pl.multiple_of(q * LANES, LANES), LANES)
            for e in range(2):
                grad = tn(logit_grads[e, :, rows], head_t[...])
                grad = grad * slope(pre_three[rows, e * 256 : (e + 1) * 256])
                for part in range(2):
                    put(g_three, q + e, 1 - e, grad[:, part * LANES : (part + 1) * LANES], part, 2)
            return carry

        g_three[0:LANES, 0:768] = jnp.zeros((LANES, 768), BF16)
        g_three[18 * LANES : 20 * LANES, :] = jnp.zeros((2 * LANES, 1536), BF16)
        lax.fori_loop(0, PAIRS, back_step, 0)
        last_row = slice(16 * LANES, 17 * LANES)
        send_up_w[...] = g_three[0:LANES, 1024:1280]
        send_down_w[...] = pick(split == 1, g_three[last_row, 1024:1280], g_three[last_row, 256:512])
        copies = halo_copies(0, send_up_w, send_down_w, from_up_w, from_down_w, sem_ws, sem_wr)
        halo_start(copies)

        def write(i, j, part, block):
            start = B_THREE + 2 * (i * 3 + j) * LANES + part
            grad_b[pl.ds(start, LANES, 2), :] = block

        weight_grads(g_three, x_three, 2, write)
        sums = bias_grads(g_three, 2)
        grad_b[B_HEAD - 2 : B_HEAD - 1, :] = sums[:, 0:LANES]
        grad_b[B_HEAD - 1 : B_HEAD, :] = sums[:, LANES : 2 * LANES]
        halo_wait(copies)
        put_edges(g_three, 0, 2, from_up_w[...], from_down_w[...])
        banded_back(g_three, d_three, back)

    def loss_copy(k):
        return remote(loss_mine, loss_all.at[me], sem_ls.at[k], sem_lr.at[me], lax.rem(me + k, n))

    pl.run_scoped(
        last_layers,
        pltpu.VMEM((GRID, 512), F32),
        pltpu.VMEM((GRID, 512), BF16),
        pltpu.VMEM((20 * LANES, 1536), BF16),
    )

    def lower_layers(g_ref, g_map, win0, win1, win2, gathered):
        def grads_in(pre_ref):
            def step(q, carry):
                rows = pl.ds(pl.multiple_of(q * LANES, LANES), LANES)
                for e in range(2):
                    lanes = slice(e * LANES, (e + 1) * LANES)
                    value = back[rows, lanes] * slope(pre_ref[rows, lanes])
                    put(g_ref, q + e, 1 - e, pick(ok(2 * q + 1 + e), value, 0.0), 0, 1)
                return carry

            lax.fori_loop(0, PAIRS, step, 0)

        def layer(pre_ref, x_ref, d_ref, begin, s):
            g_ref[0:LANES, 0:384] = jnp.zeros((LANES, 384), BF16)
            grads_in(pre_ref)
            exchange(g_ref, s)

            def write(i, j, part, block):
                start = begin + (i * 3 + j) * LANES
                grad_b[start : start + LANES, :] = block

            weight_grads(g_ref, x_ref, 1, write)
            grad_b[begin + 1152 : begin + 1153, :] = bias_grads(g_ref, 1)
            halo_wait(thin(s))
            put_edges(g_ref, s, 1, from_up[s], from_down[s])
            banded_back(g_ref, d_ref, back)

        g_ref[18 * LANES : 20 * LANES, :] = jnp.zeros((2 * LANES, 768), BF16)
        layer(pre_two, x_two, d_two, B_TWO, 3)
        layer(pre_one, x_one, d_one, B_ONE, 4)

        g_map[...] = jnp.zeros_like(g_map)

        def to_map(q, total):
            rows = pl.ds(pl.multiple_of(q * LANES, LANES), LANES)
            for e in range(2):
                p = 2 * q + 1 + e
                lanes = slice(e * LANES, (e + 1) * LANES)
                value = back[rows, lanes] * slope(pre_mid[rows, lanes])
                value = pick(ok(p), value, 0.0).astype(BF16).astype(F32)
                g_map[pl.ds(pl.multiple_of(p * PITCH + 8, 8), LANES), :] = value
                total += jnp.sum(value, axis=0, keepdims=True)
            return total

        total = lax.fori_loop(0, PAIRS, to_map, jnp.zeros((1, LANES), F32))
        total = total[:, 0:CM] + total[:, CM : 2 * CM]
        grad_a[0:A_MID, :] = jnp.zeros((A_MID, LANES), F32)
        grad_a[A_MID + 1728 : A_ROWS, :] = jnp.zeros((A_ROWS - A_MID - 1728, LANES), F32)
        grad_a[A_MID + 1728 : A_MID + 1729, 0:CM] = total

        def map_row(place):
            return slice(place * PITCH + 8, place * PITCH + 8 + LANES)

        send_up[5] = g_map[map_row(1), :].astype(BF16)
        send_down[5] = pick(split == 1, g_map[map_row(row_count + 1), :], g_map[map_row(row_count), :]).astype(BF16)
        halo_start(thin(5))
        halo_wait(thin(5))
        g_map[map_row(0), :] = pick((top == 1) & has_up, from_up[5].astype(F32), 0.0)
        halo = pick((bottom == 1) & has_down, from_down[5].astype(F32), 0.0)
        g_map[map_row(row_count + 1), :] = pick(split == 1, g_map[map_row(row_count + 1), :], halo)
        g_map[map_row(row_count + 2), :] = pick(split == 1, halo, 0.0)

        wins = (win0, win1, win2)
        voxels = feature.shape[0]
        depth_cells = row_count * LANES * ZD

        def fetch(v, carry):
            base = voxel_base(cells_smem[v], depth_cells, LANES, edge, split)
            for i in range(3):
                wins[i][pl.ds(4 * v, 3), :] = g_map[pl.ds(base + (1 - i) * PITCH, 3), :]
            return carry

        lax.fori_loop(0, voxels, fetch, 0, unroll=8)
        for i in range(3):
            for j in range(3):
                lanes = slice((i * 3 + j) * LANES, (i * 3 + j + 1) * LANES)
                gathered[:, lanes] = wins[i][pl.ds(2 - j, voxels, 4), :].astype(BF16)
        low = lane_of((64, LANES)) < 64
        for i in range(3):
            block = tn(spread[...], gathered[:, i * 384 : (i + 1) * 384])
            for j in range(3):
                part = block[:, j * LANES : (j + 1) * LANES]
                even = [part[z * LANES : z * LANES + 64] for z in range(ZD)]
                odd = [part[z * LANES + 64 : (z + 1) * LANES] for z in range(ZD)]

                def flip(x):
                    return pltpu.roll(x, 64, axis=1)

                taps = (
                    jnp.where(low, flip(even[1]), odd[1]),
                    jnp.where(low, even[0] + flip(even[2]), flip(odd[0]) + odd[2]),
                    jnp.where(low, even[1] + flip(even[3]), flip(odd[1]) + odd[3]),
                )
                for t in range(3):
                    start = A_MID + (t * 9 + i * 3 + j) * 64
                    grad_a[start : start + 64, :] = taps[t]
        z_column = z_columns(cells_row[...])
        total = jnp.zeros((voxels, C2), F32)
        for z in range(ZD):
            total += jnp.where(z_column == z, nt(gathered[...], w_mid[z * C2 : (z + 1) * C2, :]), 0.0)
        grad_feature[...] = total

    voxels = feature.shape[0]
    pl.run_scoped(
        lower_layers,
        pltpu.VMEM((20 * LANES, 768), BF16),
        pltpu.VMEM(((row_count + 6) * PITCH, LANES), F32),
        pltpu.VMEM((voxels * 4, LANES), F32),
        pltpu.VMEM((voxels * 4, LANES), F32),
        pltpu.VMEM((voxels * 4, LANES), F32),
        pltpu.VMEM((voxels, 1152), BF16),
    )
    for k in range(1, n):
        sender = lax.rem(me + n - k, n)
        remote(loss_mine, loss_all.at[sender], sem_ls.at[k], sem_lr.at[sender], sender).wait_recv()
    loss_all[me] = loss_mine[...]
    total = loss_all[0]
    for d in range(1, n):
        total += loss_all[d]
    loss_out[...] = total
    for k in range(1, n):
        loss_copy(k).wait_send()


def convs(n, row_count, cells, feature, stat, middle_out, labels, boxes):
    shape = jax.ShapeDtypeStruct
    dma = pltpu.SemaphoreType.DMA
    voxels = feature.shape[0]
    row = (LANES, LANES)
    return pl.pallas_call(
        functools.partial(conv_kernel, n, row_count),
        name="convs",
        out_shape=(
            shape((A_ROWS, LANES), F32),
            shape((B_ROWS, LANES), F32),
            shape((voxels, LANES), F32),
            shape((8, LANES), F32),
        ),
        in_specs=[smem()] + [vmem()] * 12 + [anywhere()] * 2,
        out_specs=(vmem(),) * 4,
        scratch_shapes=[
            pltpu.VMEM((20 * LANES, 768), BF16),
            pltpu.VMEM((20 * LANES, 768), BF16),
            pltpu.VMEM((20 * LANES, 768), BF16),
            pltpu.VMEM((GRID, 256), F32),
            pltpu.VMEM((GRID, 256), F32),
            pltpu.VMEM((GRID, 256), F32),
            pltpu.VMEM((GRID, 256), F32),
            pltpu.VMEM((voxels, ZD * C2), BF16),
            pltpu.VMEM((512, 768), F32),
            pltpu.VMEM((256, 384), F32),
            pltpu.VMEM((256, 384), F32),
            pltpu.VMEM((row_count, 2, LANES), jnp.int32),
            pltpu.VMEM((row_count, 16, LANES), F32),
            pltpu.VMEM((2, 16, GRID), BF16),
            pltpu.VMEM((8, LANES), F32),
            pltpu.VMEM((n, 8, LANES), F32),
            pltpu.VMEM(row, F32),
            pltpu.VMEM(row, F32),
            pltpu.VMEM(row, F32),
            pltpu.VMEM(row, F32),
            pltpu.VMEM((6,) + row, BF16),
            pltpu.VMEM((6,) + row, BF16),
            pltpu.VMEM((6,) + row, BF16),
            pltpu.VMEM((6,) + row, BF16),
            pltpu.VMEM((LANES, 256), BF16),
            pltpu.VMEM((LANES, 256), BF16),
            pltpu.VMEM((LANES, 256), BF16),
            pltpu.VMEM((LANES, 256), BF16),
            dma((16,)), dma((2,)), dma((2,)), dma((12,)), dma((12,)), dma((2,)), dma((2,)), dma((n,)), dma((n,)),
        ],
        compiler_params=pltpu.CompilerParams(
            collective_id=2, has_side_effects=True, vmem_limit_bytes=62 << 20
        ),
    )(cells, cells.reshape(1, -1), feature, stat, *middle_out, labels, boxes)


def adam_outer(gradient, weight, moment, second, momentum):
    moment = FIRST_DECAY * moment + (1.0 - FIRST_DECAY) * gradient
    second = SECOND_DECAY * second + (1.0 - SECOND_DECAY) * gradient * gradient
    moment_fix = moment / (1.0 - FIRST_DECAY**STEP)
    second_fix = second / (1.0 - SECOND_DECAY**STEP)
    inner_weight = weight - INNER_RATE * (
        moment_fix / (jnp.sqrt(second_fix) + ADAM_EPSILON) + WEIGHT_DECAY * weight
    )
    inner_step = weight - inner_weight
    momentum = OUTER_MOMENT * momentum + inner_step
    updated = weight - OUTER_RATE * (inner_step + OUTER_MOMENT * momentum)
    return (moment, second, momentum, updated)


def flat_pieces(rows, slot):
    begin, end = slot * rows, (slot + 1) * rows
    spans = ((0, 67, None, 0), (67, 1795, "a", 2), (1795, 1796, "both", 0), (1796, 6440, "b", 1795), (6440, 1 << 30, None, 0))
    pieces = []
    for low, high, run, shift in spans:
        first, last = max(begin, low), min(end, high)
        if first < last:
            pieces.append((first - begin, last - first, run, first - shift))
    return pieces


NOTE = 112


def finish_kernel(
    n, points_hbm, counts_ref, small, stat, linear, joined, grad_feature, grad_a, grad_b,
    weight, moment, second, momentum,
    moment_out, second_out, momentum_out, weight_out,
    points, first, slots, pair, line, mine, notes, fc_rows, small_grad,
    sem_p, sem_ps, sem_pr, sem_zs, sem_zr, sem_ns, sem_nr,
):
    me = lax.axis_index("tile")
    rows = weight.shape[0]
    half = n // 2
    parity, chip = lax.rem(me, 2), me // 2
    sibling = me + 1 - 2 * parity
    count_p, voxels = points_hbm.shape[1], points_hbm.shape[2]
    points[...] = jnp.ones_like(points)
    loads = [
        pltpu.make_async_copy(points_hbm.at[k], points.at[:, k, :], sem_p.at[k]) for k in range(7)
    ]
    for load in loads:
        load.start()
    enter(n, me)

    def realigned(ref, start, count, lane):
        here, before = ref[pl.ds(start, count), :], ref[pl.ds(start - 1, count), :]
        mixed = jnp.where(lane_of((count, LANES)) >= LANES - lane, before, here)
        return pltpu.roll(mixed, lane, axis=1)

    for s in range(n):
        for row, count, run, start in flat_pieces(rows, s):
            if run is None:
                value = jnp.zeros((count, LANES), F32)
            elif run == "a":
                value = realigned(grad_a, start, count, 32)
            elif run == "b":
                value = realigned(grad_b, start, count, 96)
            else:
                lane = lane_of((8, LANES))
                part_a = jnp.where(lane[0:1] >= 96, grad_a[1792:1793, :], grad_a[1793:1794, :])
                part_b = jnp.where(lane[0:1] >= 32, 0.0, grad_b[0:1, :])
                part_a = pltpu.roll(jnp.broadcast_to(part_a, (8, LANES)), 32, axis=1)
                part_b = pltpu.roll(jnp.broadcast_to(part_b, (8, LANES)), 96, axis=1)
                value = (jnp.where(lane < 96, part_a, part_b))[0:1]
            slots[s, row : row + count, :] = value

    def pair_copy(k):
        return remote(slots.at[2 * k + 1 - parity], pair.at[k], sem_ps.at[k], sem_pr.at[k], sibling)

    for k in range(half):
        pair_copy(k).start()

    def line_copy(k):
        target = lax.rem(me + 2 * k, n)
        return remote(slots.at[target], line.at[chip], sem_zs.at[k], sem_zr.at[chip], target)

    for k in range(half):
        pair_copy(k).wait()
        slots[2 * k + parity] = slots[2 * k + parity] + pair[k]
    for k in range(1, half):
        line_copy(k).start()

    counts = counts_ref[...]
    columns, gamma, beta = first_layer(small)
    mean, scale, held = stat[0:32, 0:1], stat[0:32, 1:2], stat[0:32, 2:3]
    centre = stat[0:8, 4:5]
    order = even_first()
    rows_fc = voxel_rows(small)
    kernel = rows_fc[0:64, :].astype(BF16)
    kernel_t = nt(order.astype(BF16), kernel).astype(BF16)
    kernel = nt(kernel, order.astype(BF16)).astype(BF16)
    bias = jnp.sum(jnp.where(order, rows_fc[64:65, :], 0.0), axis=1, keepdims=True)
    counts_f = counts.astype(F32)
    grad_pre = jnp.transpose(grad_feature[...]) / counts_f

    def pass_e(p, carry):
        fc, pooled = carry
        inner = nn(kernel_t, joined[p, 0:64, :]) + bias
        grad = jnp.where(p < counts, grad_pre * slope(inner), 0.0).astype(BF16)
        fc += nt(joined[p], grad)
        down = nn(kernel, grad)
        first[p] = down[0:32]
        return fc, pooled + down[32:64]

    fc, pooled = lax.fori_loop(
        0, count_p, pass_e, (jnp.zeros((80, LANES), F32), jnp.zeros((32, voxels), F32))
    )
    pooled = pooled / counts_f
    for load in loads:
        load.wait()

    def halves(value):
        high = value.astype(BF16)
        return high, (value - high.astype(F32)).astype(BF16)

    def pass_f(p, carry):
        moments, g_gamma, centred = carry
        inside = p < counts
        normed = jnp.where(inside, (linear[p] - mean) * scale, 0.0)
        act = gamma * normed + beta
        grad = jnp.where(inside, (first[p] + pooled) * slope(act), 0.0)
        off = points[p] - centre
        off_high, off_low = halves(off)
        grad_high, grad_low = halves(grad)
        norm_high, norm_low = halves(normed)
        left = jnp.concatenate([grad_high, grad_low, norm_high, norm_low], axis=0)
        right = jnp.concatenate([off_high, off_low], axis=0)
        return (
            moments + nt(left, right),
            g_gamma + grad * normed,
            centred + jnp.where(inside, off, 0.0),
        )

    moments, g_gamma, centred = lax.fori_loop(
        0,
        count_p,
        pass_f,
        (jnp.zeros((LANES, 16), F32), jnp.zeros((32, voxels), F32), jnp.zeros((8, voxels), F32)),
    )
    by_grad = moments[0:32] + moments[32:64]
    by_grad = by_grad[:, 0:8] + by_grad[:, 8:16]
    by_norm = moments[64:96] + moments[96:128]
    by_norm = by_norm[:, 0:8] + by_norm[:, 8:16]
    mine[...] = jnp.zeros_like(mine)
    mine[0:72, :] = fc[0:72]
    mine[72:104, 0:8] = by_grad
    mine[72:104, 8:16] = by_norm
    mine[72:104, 16:17] = jnp.sum(g_gamma, axis=1, keepdims=True)
    mine[104:112, 0:1] = jnp.sum(centred, axis=1, keepdims=True)
    small_grad[...] = jnp.zeros_like(small_grad)

    def note(sender):
        return remote(mine, notes.at[sender], sem_ns.at[0], sem_nr.at[sender], 0)

    @pl.when(me > 0)
    def _():
        note(me).start()

    @pl.when(me == 0)
    def _():
        notes[0] = mine[...]
        for d in range(1, n):
            note(d).wait_recv()
        total = notes[0]
        for d in range(1, n):
            total += notes[d]
        by_grad, by_norm = total[72:104, 0:8], total[72:104, 8:16]
        g_gamma, g_beta = total[72:104, 16:17], total[72:104, 7:8]
        off_sums = jnp.transpose(jnp.broadcast_to(total[104:112, 0:1], (8, LANES)))[0:32, 0:8]
        g_vfe = scale * gamma * (
            by_grad - g_beta / held * off_sums - g_gamma / held * by_norm
        )
        tall0 = jnp.concatenate([g_vfe[:, k : k + 1] for k in range(4)], axis=0)
        tall1 = jnp.concatenate([g_vfe[:, 4:5], g_vfe[:, 5:6], g_vfe[:, 6:7], g_gamma], axis=0)
        tall2 = jnp.concatenate([g_beta, jnp.zeros((96, 1), F32)], axis=0)
        lane = lane_of((LANES, LANES))
        tall = jnp.where(lane == 0, tall0, 0.0) + jnp.where(lane == 1, tall1, 0.0) + jnp.where(lane == 2, tall2, 0.0)
        head = jnp.transpose(tall)[0:8]
        fc_rows[...] = jnp.zeros_like(fc_rows)
        fc_rows[8:80, :] = nn(total[0:72], order.astype(F32), HIGH)
        small_grad[2:74, :] = realigned(fc_rows, 8, 72, 32)
        small_grad[0:8, :] = small_grad[0:8, :] + head

    total = slots[me, 0:rows, :]
    for k in range(1, half):
        source = lax.rem(chip + half - k, half)
        remote(slots.at[0], line.at[source], sem_zs.at[k], sem_zr.at[source], sibling).wait_recv()
        total += line[source, 0:rows, :]
    slots[me, 0:rows, :] = total
    slots[me, 0:SMALL, :] = slots[me, 0:SMALL, :] + small_grad[...]
    outs = adam_outer(slots[me, 0:rows, :], weight[...], moment[...], second[...], momentum[...])
    moment_out[...], second_out[...], momentum_out[...], weight_out[...] = outs
    for k in range(1, half):
        line_copy(k).wait_send()

    @pl.when(me > 0)
    def _():
        note(me).wait_send()


def finish(n, points, counts, small, stat, linear, joined, grad_feature, grad_a, grad_b, shards):
    shape = jax.ShapeDtypeStruct
    dma = pltpu.SemaphoreType.DMA
    slots, voxels = points.shape[1:]
    rows = shards[0].shape[0]
    padded = ceil_to(rows, 8)
    half = n // 2
    return pl.pallas_call(
        functools.partial(finish_kernel, n),
        name="finish",
        out_shape=(shape((rows, LANES), F32),) * 4,
        in_specs=[anywhere()] + [vmem()] * 12,
        out_specs=(vmem(),) * 4,
        scratch_shapes=[
            pltpu.VMEM((slots, 8, voxels), F32),
            pltpu.VMEM((slots, 32, voxels), F32),
            pltpu.VMEM((n, padded, LANES), F32),
            pltpu.VMEM((half, padded, LANES), F32),
            pltpu.VMEM((half, padded, LANES), F32),
            pltpu.VMEM((NOTE, LANES), F32),
            pltpu.VMEM((n, NOTE, LANES), F32),
            pltpu.VMEM((88, LANES), F32),
            pltpu.VMEM((SMALL, LANES), F32),
            dma((7,)), dma((half,)), dma((half,)), dma((half,)), dma((half,)), dma((1,)), dma((n,)),
        ],
        compiler_params=pltpu.CompilerParams(
            collective_id=3, has_side_effects=True, vmem_limit_bytes=58 << 20
        ),
    )(points, counts, small, stat, linear, joined, grad_feature, grad_a, grad_b, *shards)


def shards(
    points, point_counts, voxel_cells, anchor_labels, box_targets, weights, adam_m, adam_v, outer_momentum
):
    n = lax.axis_size("tile")
    rows = weights.shape[0] // LANES
    row_count = anchor_labels.shape[1]
    held = [x.reshape(rows, LANES) for x in (weights, adam_m, adam_v, outer_momentum)]
    counts = point_counts.reshape(1, -1)
    wall, small, stat, linear, joined, feature = front(n, points, counts, anchor_labels, held[0])
    ready = middle(n, rows, row_count, voxel_cells, feature, wall)
    grad_a, grad_b, grad_feature, loss = convs(
        n, row_count, voxel_cells, feature, stat, ready, anchor_labels, box_targets
    )
    outs = finish(
        n, points, counts, small, stat, linear, joined, grad_feature, grad_a, grad_b, held
    )
    moment, second, momentum, updated = [x.reshape(weights.shape) for x in outs]
    return (moment, second, momentum, updated, loss[0, 0:1], stat[0, 3:4])


def solution(mesh):
    split = ("group", "tile")
    in_specs = (
        P(None, None, split), P(split), P(split), P(None, split, None), P(None, split, None),
        P(split), P(split), P(split), P(split),
    )
    out_specs = (P(split), P(split), P(split), P(split), P("group"), P("group"))
    return jax.shard_map(shards, mesh=mesh, in_specs=in_specs, out_specs=out_specs, check_vma=False)
```

time: 1400 us -> 202 us (0.14); the launches traced: 1380 us -> 202 us
  local copies, waits for them, and re-layouts: 700 us -> 8.63 us
  matrix products: 354 us -> 0 us
  Pallas kernels: 0 us -> 193 us
  waiting for transfers between devices: 114 us -> 0 us
  other arithmetic: 87.9 us -> 0 us
  blocking collectives: 62.8 us -> 0 us
  starting transfers between devices: 37.7 us -> 0 us
  between operations: 19.2 us -> 0.67 us
    scatter-add x36 -> x0, local copies, waits for them, and re-layouts: 549 us -> none  [the longest x35 544 us: conv_backward(): input_grad.at[:, i:i + row_count, j:j + col_count]]
    dot_general x143 -> x0, matrix products: 354 us -> none  [the longest x45 201 us: conv_backward(): jnp.einsum('co,orw->crw', kernel[i, j], grad_pre, preferred_element_type=...]
    pallas_call x0 -> x4, Pallas kernels: none -> 193 us  [the longest x1 78.2 us: convs(): pl.pallas_call(functools.partial(conv_kernel, n, row_count), name='convs'...]
    unnamed x3 -> x0, waiting for transfers between devices: 76.7 us -> none
    psum x4 -> x0, blocking collectives: 62.8 us -> none  [the longest x2 31.9 us: shards(): lax.psum((local_sums, local_total, local_positives), 'tile')]
    slice x30 -> x2, local copies, waits for them, and re-layouts: 50.9 us -> 2.5 us  [shards(): return (moment, second, momentum, updated, loss[0, 0:1], stat[0, 3:4])]
    concatenate x1 -> x0, local copies, waits for them, and re-layouts: 43.2 us -> none  [shards(): full_grad = jnp.concatenate(pieces)]
    ppermute x16 -> x0, starting transfers between devices: 37.6 us -> none  [the longest x8 26 us: with_halo(): lax.ppermute(tail, axis, [(i, (i + 1) % count) for i in range(ends)])]
  transfers between devices with their start and end apart: 18 -> 0, of which waited for: 5 -> 0; matrix products, arithmetic and copies ran while one was open for 4% -> 0% of each run, Pallas kernels for 0% -> 0%
where the time goes in v1:
time: 202 us
  Pallas kernels  193 us (96%)
  local copies, waits for them, and re-layouts  8.63 us (4%)
    pallas_call x1, Pallas kernels, convs(): pl.pallas_call(functools.partial(conv_kernel, n, row_count), name='convs'...  78.2 us
    pallas_call x1, Pallas kernels, finish(): pl.pallas_call(functools.partial(finish_kernel, n), name='finish', out_sh...  54.4 us
    pallas_call x1, Pallas kernels, front(): pl.pallas_call(functools.partial(front_kernel, n), name='front', out_shap...  43.8 us
    pallas_call x1, Pallas kernels, middle(): pl.pallas_call(functools.partial(middle_kernel, n, rows, row_count), name...  16.1 us
    unnamed x6, local copies, waits for them, and re-layouts  6.13 us

profile of v1, /device:TPU:0, one launch (start us, length us, event | category | flops | bytes accessed | tf_op | source)
XLA Modules:
  0.0 201.9 jit_solution(10221316906165162951)
XLA Ops:
  0.6 43.8 %front.1 = (bf16[8,816,128]{2,1,0:T(8,128)(2,1)}, f32[80,128]{1,0:T(8,128)}, f32[48,128]{1,0:T(8,128)}, f32[35,32,512]{2,1,0:T(8,128)}, bf16[35,80,512]{2,1,0:T(8,128)(2,1)}, /*index=5*/f32[512,128]{1,0:T(8,128)}) custom-call(f32[7,35,512]{2,1,0:T(8,128)} %points_hbm.3, s32[1,512]{1,0:T(1,128)} %bitcast.23, s32[2,32,128]{2,1,0:T(8,128)} %labels_hbm.1, ...), custom_call_target="tpu_custom_call" | custom-call | tf_op jit(solution)/shard_map/front/pallas_call | solution.py:310
  44.5 16.1 %middle.1 = (f32[37,128,128]{2,1,0:T(8,128)}, bf16[512,1152]{1,0:T(8,128)(2,1)}, bf16[1536,256]{1,0:T(8,128)(2,1)}, bf16[1536,256]{1,0:T(8,128)(2,1)}, bf16[1152...) custom-call(s32[512]{0:T(512)} %cells_smem.3, ...), custom_call_target="tpu_custom_call" | custom-call | tf_op jit(solution)/shard_map/middle/pallas_call | solution.py:494
  60.6 78.2 %convs.1 = (f32[1800,128]{1,0:T(8,128)}, f32[4656,128]{1,0:T(8,128)}, f32[512,128]{1,0:T(8,128)}, f32[8,128]{1,0:T(8,128)}) custom-call(s32[512]{0:T(512)} %cells_smem.3, s32[1,512]{1,0:T(1,128)} %bitcast.22, f32[512,128]{1,0:T(8,128)} %get-tuple-element.33.feature, f32[48,128]{1,0:T(8,128)} %get-tuple-element.30.stat, ...), custom_call_target="tpu_custom_call" | custom-call | tf_op jit(solution)/shard_map/convs/pallas_call | solution.py:998
  138.9 54.4 %finish.1 = (f32[805,128]{1,0:T(8,128)}, f32[805,128]{1,0:T(8,128)}, f32[805,128]{1,0:T(8,128)}, f32[805,128]{1,0:T(8,128)}) custom-call(f32[7,35,512]{2,1,0:T(8,128)} %points_hbm.3, s32[1,512]{1,0:T(1,128)} %bitcast.24, f32[80,128]{1,0:T(8,128)} %get-tuple-element.29.small, f32[48,128]{1,0:T(8,128)} %get-tuple-element.30.stat, ...), custom_call_target="tpu_custom_call" | custom-call | tf_op jit(solution)/shard_map/finish/pallas_call | solution.py:1258
  193.3 0.0 copy-start
  193.3 1.2 slice.6
  194.5 1.3 slice.7
  195.8 1.8 copy.19
  197.6 1.8 copy.20
  199.3 1.8 copy.21
  201.1 0.0 copy-done
  201.1 0.8 copy.22
Async XLA Ops:
  193.3 7.9 %copy-start = (f32[805,128]{1,0:T(8,128)S(1)}, f32[805,128]{1,0:T(8,128)}, u32[]{:S(2)}) copy-start(f32[805,128]{1,0:T(8,128)} %get-tuple-element.50) | copy-start | bytes 1236484

commit v2 on v1

--- a/solution.py
+++ b/solution.py
@@ -35,7 +35,9 @@
 RUN_B = (1795, 96)
 A_MID = 65
 B_ONE, B_TWO, B_THREE, B_HEAD = 0, 1153, 2306, 4612
-MSG = 48
+PAIRS_OF = tuple((a, b) for a in range(7) for b in range(a, 7))
+DIAGONAL = tuple(r for r, (a, b) in enumerate(PAIRS_OF) if a == b)
+CHUNK = 256
 
 
 def vmem():
@@ -83,7 +85,7 @@
     return lax.broadcasted_iota(jnp.int32, shape, len(shape) - 2)
 
 
-def enter(n, me):
+def enter(n, me, between=None):
     sem = pltpu.get_barrier_semaphore()
 
     def greet(k, carry):
@@ -93,6 +95,8 @@
         return carry
 
     lax.fori_loop(1, n, greet, 0)
+    if between is not None:
+        between()
     pl.semaphore_wait(sem, n - 1)
 
 
@@ -128,27 +132,115 @@
     return pltpu.roll(mixed, LANES - FC_LANE, axis=1)
 
 
+def linear_row(wide, points, p):
+    value = wide[0] * points[0, pl.ds(p, 1), :]
+    for k in range(1, 7):
+        value += wide[k] * points[k, pl.ds(p, 1), :]
+    return value
+
+
+def local_moments(points, counts, labels_ref, sums, message):
+    slots, voxels = points.shape[1:]
+    inside = row_of((slots, voxels)) < counts
+
+    def folded(value):
+        total = value[:, 0:LANES]
+        for c in range(1, voxels // LANES):
+            total = total + value[:, c * LANES : (c + 1) * LANES]
+        return jnp.sum(total, axis=0, keepdims=True)
+
+    def whole(row):
+        return jnp.sum(row, axis=1, keepdims=True)
+
+    held = whole(folded(inside.astype(F32)))
+    masked = [jnp.where(inside, points[k], 0.0) for k in range(7)]
+    rows = [folded(value) for value in masked]
+    means = [whole(row) / held for row in rows]
+    centred = [jnp.where(inside, points[k] - means[k], 0.0) for k in range(7)]
+    for r, (a, b) in enumerate(PAIRS_OF):
+        sums[0, r : r + 1, :] = folded(centred[a] * centred[b])
+        sums[1, r : r + 1, :] = rows[a]
+        sums[2, r : r + 1, :] = rows[b]
+    spare = len(PAIRS_OF)
+    for c in range(3):
+        sums[c, spare:LANES, :] = jnp.zeros((LANES - spare, LANES), F32)
+    lane = lane_of((LANES, LANES))
+    columns = jnp.zeros((LANES, LANES), F32)
+    for c in range(3):
+        columns = jnp.where(lane == c, jnp.sum(sums[c], axis=1, keepdims=True), columns)
+    positives = jnp.zeros((1, 1), F32)
+    for a in range(ANCH):
+        positives += whole(jnp.sum((labels_ref[a] == 1).astype(F32), axis=0, keepdims=True))
+    packed = jnp.transpose(columns)[0:8]
+    row = row_of((8, LANES))
+    packed = jnp.where(row == 3, held, packed)
+    message[...] = jnp.where(row == 4, positives, packed)
+
+
+def joint_moments(n, messages):
+    total = messages[0]
+    for d in range(1, n):
+        total += messages[d]
+    held = total[3:4]
+    mean_a, mean_b = total[1:2] / held, total[2:3] / held
+    product = total[0:1]
+    for d in range(n):
+        held_d = messages[d, 3:4, :]
+        product += held_d * (messages[d, 1:2, :] / held_d - mean_a) * (messages[d, 2:3, :] / held_d - mean_b)
+    return mean_a, product, held, total[4:5]
+
+
+def channel_statistics(columns, mean_row, product, held):
+    lane = lane_of((32, LANES))
+    once, twice = jnp.zeros((32, LANES), F32), jnp.zeros((32, LANES), F32)
+    for r, (a, b) in enumerate(PAIRS_OF):
+        if a == b:
+            once = jnp.where(lane == r, columns[a], once)
+        twice = jnp.where(lane == r, (1.0 if a == b else 2.0) * columns[a] * columns[b], twice)
+    mean = jnp.sum(once * mean_row, axis=1, keepdims=True)
+    variance = jnp.sum(twice * (product / held), axis=1, keepdims=True)
+    return mean, lax.rsqrt(variance + NORM_EPSILON)
+
+
 def front_kernel(
-    n, points_hbm, counts_ref, labels_ref, shard_ref,
-    wall, small, stat, linear, joined, feature,
-    points, own, mine, msgs, sem_p, sem_small_s, sem_small_r, sem_msg_s, sem_msg_r, sem_w_s, sem_w_r, sem_f_s,
+    n, points, counts_ref, labels_ref, shard_ref,
+    wall, small, stat, first_out, pooled_out, feature,
+    own, sums, mine, messages, my_bias, biases,
+    sem_small_s, sem_small_r, sem_msg_s, sem_msg_r, sem_b_s, sem_b_r, sem_w_s, sem_w_r, sem_f_s,
 ):
     me = lax.axis_index("tile")
     rows = shard_ref.shape[0]
-    slots, voxels = points_hbm.shape[1], points_hbm.shape[2]
+    slots, voxels = points.shape[1:]
     sibling = me + 1 - 2 * lax.rem(me, 2)
-    loads = [
-        pltpu.make_async_copy(points_hbm.at[k], points.at[:, k, :], sem_p.at[k]) for k in range(7)
-    ]
-    for load in loads:
-        load.start()
-    own[...] = jnp.zeros_like(own)
-    own[0:rows, :] = shard_ref[...].astype(BF16)
-    enter(n, me)
+    half = n // 2
+    counts = counts_ref[...]
+
+    def prepare():
+        local_moments(points, counts, labels_ref, sums, mine)
+        own[...] = jnp.zeros_like(own)
+        own[0:rows, :] = shard_ref[...].astype(BF16)
+        for a, row in enumerate(BIAS_ROWS):
+            owner, place = row // rows, row % rows
+            my_bias[a : a + 1, :] = jnp.where(me == owner, shard_ref[place : place + 1, :], 0.0)
+        for a in range(len(BIAS_ROWS), 16):
+            my_bias[a : a + 1, :] = jnp.zeros((1, LANES), F32)
+
+    enter(n, me, prepare)
+
+    def message(k):
+        return remote(mine, messages.at[me], sem_msg_s.at[k], sem_msg_r.at[me], lax.rem(me + k, n))
+
+    def bias_message(k):
+        return remote(my_bias, biases.at[me], sem_b_s.at[k], sem_b_r.at[me], lax.rem(me + k, n))
 
     def small_copy(k):
-        peer = lax.rem(me + k, n)
-        return remote(small, small, sem_small_s.at[k], sem_small_r.at[0], peer)
+        return remote(small, small, sem_small_s.at[k], sem_small_r.at[0], lax.rem(me + k, n))
+
+    def shard_copy(k):
+        return remote(own, wall.at[me], sem_w_s.at[k], sem_w_r.at[me], lax.rem(me + 2 * k, n))
+
+    for k in range(1, n):
+        message(k).start()
 
     @pl.when(me == 0)
     def _():
@@ -160,127 +252,74 @@
 
         lax.fori_loop(1, n, send, 0)
 
-    def shard_copy(k):
-        return remote(own, wall.at[me], sem_w_s.at[k], sem_w_r.at[me], lax.rem(me + 2 * k, n))
-
-    half = n // 2
+    for k in range(1, n):
+        bias_message(k).start()
     for k in range(1, half):
         shard_copy(k).start()
     to_sibling = remote(own, wall.at[me], sem_w_s.at[0], sem_w_r.at[me], sibling)
     to_sibling.start()
     wall[me] = own[...]
-
-    counts = counts_ref[...]
-    slot_no = row_of((slots, voxels))
-    mask_all = (slot_no < counts).astype(F32)
-    for load in loads:
-        load.wait()
-    point_sums = jnp.zeros((32, 1), F32)
-    row32 = row_of((32, 1))
-    for k in range(7):
-        total = jnp.sum(jnp.sum(points[:, k, :] * mask_all, axis=1, keepdims=True), axis=0, keepdims=True)
-        point_sums = point_sums + jnp.where(row32 == k, total, 0.0)
-    positives = jnp.zeros((1, 1), F32)
-    for a in range(ANCH):
-        hits = (labels_ref[a] == 1).astype(F32)
-        positives += jnp.sum(jnp.sum(hits, axis=1, keepdims=True), axis=0, keepdims=True)
-    held = jnp.sum(jnp.sum(mask_all, axis=1, keepdims=True), axis=0, keepdims=True)
-    for a, row in enumerate(BIAS_ROWS):
-        owner, place = row // rows, row % rows
-        mine[32 + a : 33 + a, :] = jnp.where(me == owner, shard_ref[place : place + 1, :], 0.0)
-    for a in range(len(BIAS_ROWS), MSG - 32):
-        mine[32 + a : 33 + a, :] = jnp.zeros((1, LANES), F32)
+    messages[me] = mine[...]
+    biases[me] = my_bias[...]
 
     @pl.when(me > 0)
     def _():
         small_copy(0).wait_recv()
 
     columns, gamma, beta = first_layer(small)
-    wide = [jnp.broadcast_to(c, (32, voxels)) for c in columns]
-
-    def pass_a(p, total):
-        value = wide[0] * points[p, 0:1, :]
-        for k in range(1, 7):
-            value += wide[k] * points[p, k : k + 1, :]
-        linear[p] = value
-        return total + jnp.where(p < counts, value, 0.0)
-
-    total = lax.fori_loop(0, slots, pass_a, jnp.zeros((32, voxels), F32), unroll=5)
-    local_sum = jnp.sum(total, axis=1, keepdims=True)
-    local_mean = local_sum / held
-
-    def pass_b(p, total):
-        off = linear[p] - local_mean
-        return total + jnp.where(p < counts, off * off, 0.0)
-
-    total = lax.fori_loop(0, slots, pass_b, jnp.zeros((32, voxels), F32), unroll=5)
-    local_square = jnp.sum(total, axis=1, keepdims=True)
-    lane = lane_of((32, LANES))
-    packed = jnp.where(lane == 0, local_sum, 0.0)
-    packed = jnp.where(lane == 1, local_square, packed)
-    packed = jnp.where(lane == 2, held, packed)
-    packed = jnp.where(lane == 3, positives, packed)
-    packed = jnp.where(lane == 4, point_sums, packed)
-    mine[0:32, :] = packed
-
-    def message(k):
-        return remote(mine, msgs.at[me], sem_msg_s.at[k], sem_msg_r.at[me], lax.rem(me + k, n))
-
-    for k in range(1, n):
-        message(k).start()
-    msgs[me] = mine[...]
-    for k in range(1, n):
-        sender = lax.rem(me + n - k, n)
-        remote(mine, msgs.at[sender], sem_msg_s.at[k], sem_msg_r.at[sender], sender).wait_recv()
-    sums = msgs[0]
-    for d in range(1, n):
-        sums += msgs[d]
-    held_all = sums[0:32, 2:3]
-    mean = sums[0:32, 0:1] / held_all
-    square = sums[0:32, 1:2]
-    for d in range(n):
-        held_d = msgs[d, 0:32, 2:3]
-        off = msgs[d, 0:32, 0:1] / held_d - mean
-        square += held_d * off * off
-    inverse = lax.rsqrt(square / held_all + NORM_EPSILON)
-    columns_out = jnp.where(lane == 0, mean, 0.0)
-    columns_out = jnp.where(lane == 1, inverse, columns_out)
-    columns_out = jnp.where(lane == 2, held_all, columns_out)
-    columns_out = jnp.where(lane == 3, sums[0:32, 3:4], columns_out)
-    columns_out = jnp.where(lane == 4, sums[0:32, 4:5] / held_all, columns_out)
-    stat[0:32, :] = columns_out
-    stat[32:MSG, :] = sums[32:MSG, :]
-
-    inverse_counts = 1.0 / counts.astype(F32)
-
-    def pass_c(p, pooled):
-        act = gamma * ((linear[p] - mean) * inverse) + beta
-        out = jnp.where(p < counts, act * sigmoid(act), 0.0)
-        joined[p, 0:32, :] = out.astype(BF16)
-        return pooled + out
-
-    pooled = lax.fori_loop(0, slots, pass_c, jnp.zeros((32, voxels), F32), unroll=5)
-    pooled = (pooled / counts.astype(F32)).astype(BF16)
     order = even_first()
     rows_fc = voxel_rows(small)
     kernel_t = nt(order.astype(BF16), rows_fc[0:64, :].astype(BF16)).astype(BF16)
     bias = jnp.sum(jnp.where(order, rows_fc[64:65, :], 0.0), axis=1, keepdims=True)
-    tail = jnp.where(row_of((16, voxels)) == 0, 1.0, 0.0).astype(BF16)
-
-    def pass_d(p, total):
-        inside = p < counts
-        joined[p, 32:64, :] = jnp.where(inside, pooled.astype(F32), 0.0).astype(BF16)
-        joined[p, 64:80, :] = tail
-        inner = nn(kernel_t, joined[p, 0:64, :]) + bias
-        return total + jnp.where(inside, inner * sigmoid(inner), 0.0)
-
-    total = lax.fori_loop(0, slots, pass_d, jnp.zeros((LANES, voxels), F32))
-    feature[...] = jnp.transpose(total / counts.astype(F32))
+    for k in range(1, n):
+        sender = lax.rem(me + n - k, n)
+        remote(mine, messages.at[sender], sem_msg_s.at[k], sem_msg_r.at[sender], sender).wait_recv()
+    mean_row, product, held, positives = joint_moments(n, messages)
+    mean, inverse = channel_statistics(columns, mean_row, product, held)
+    lane, row = lane_of((32, LANES)), row_of((32, LANES))
+    columns_out = jnp.where(lane == 0, mean, 0.0)
+    columns_out = jnp.where(lane == 1, inverse, columns_out)
+    columns_out = jnp.where(lane == 2, held, columns_out)
+    columns_out = jnp.where(lane == 3, positives, columns_out)
+    for k, r in enumerate(DIAGONAL):
+        columns_out = jnp.where((lane == 4) & (row == k), mean_row[:, r : r + 1], columns_out)
+    stat[0:32, :] = columns_out
+
+    for c in range(voxels // CHUNK):
+        part = slice(c * CHUNK, (c + 1) * CHUNK)
+        wide = [jnp.broadcast_to(column, (32, CHUNK)) for column in columns]
+        held_c = counts[:, part]
+        view = points.at[:, :, part]
+
+        def pass_c(p, pooled, wide=wide, held_c=held_c, view=view, part=part):
+            act = gamma * ((linear_row(wide, view, p) - mean) * inverse) + beta
+            out = jnp.where(p < held_c, act * sigmoid(act), 0.0)
+            first_out[p, :, part] = out.astype(BF16)
+            return pooled + out
+
+        pooled = lax.fori_loop(0, slots, pass_c, jnp.zeros((32, CHUNK), F32), unroll=5)
+        pooled = (pooled / held_c.astype(F32)).astype(BF16)
+        pooled_out[:, part] = pooled
+        fixed = nn(kernel_t[:, 32:64], pooled) + bias
+
+        def pass_d(p, total, fixed=fixed, held_c=held_c, part=part):
+            inner = nn(kernel_t[:, 0:32], first_out[p, :, part]) + fixed
+            return total + jnp.where(p < held_c, inner * sigmoid(inner), 0.0)
+
+        total = lax.fori_loop(0, slots, pass_d, jnp.zeros((LANES, CHUNK), F32), unroll=5)
+        feature[part, :] = jnp.transpose(total / held_c.astype(F32))
 
     for k in range(1, half):
         source = lax.rem(me + n - 2 * k, n)
         remote(own, wall.at[source], sem_w_s.at[k], sem_w_r.at[source], source).wait_recv()
         remote(wall.at[source], wall.at[source], sem_f_s.at[k], sem_w_r.at[source], sibling).start()
+    for k in range(1, n):
+        sender = lax.rem(me + n - k, n)
+        remote(my_bias, biases.at[sender], sem_b_s.at[k], sem_b_r.at[sender], sender).wait_recv()
+    total = biases[0]
+    for d in range(1, n):
+        total += biases[d]
+    stat[32:48, :] = total
     for k in range(half):
         source = lax.rem(sibling + n - 2 * k, n)
         remote(own, wall.at[source], sem_w_s.at[k], sem_w_r.at[source], source).wait_recv()
@@ -291,6 +330,7 @@
     to_sibling.wait_send()
     for k in range(1, n):
         message(k).wait_send()
+        bias_message(k).wait_send()
 
     @pl.when(me == 0)
     def _():
@@ -313,19 +353,21 @@
         out_shape=(
             shape((n, padded, LANES), BF16),
             shape((SMALL, LANES), F32),
-            shape((MSG, LANES), F32),
-            shape((slots, 32, voxels), F32),
-            shape((slots, 80, voxels), BF16),
+            shape((48, LANES), F32),
+            shape((slots, 32, voxels), BF16),
+            shape((32, voxels), BF16),
             shape((voxels, LANES), F32),
         ),
-        in_specs=[anywhere(), vmem(), vmem(), vmem()],
+        in_specs=[vmem()] * 4,
         out_specs=(vmem(),) * 6,
         scratch_shapes=[
-            pltpu.VMEM((slots, 8, voxels), F32),
             pltpu.VMEM((padded, LANES), BF16),
-            pltpu.VMEM((MSG, LANES), F32),
-            pltpu.VMEM((n, MSG, LANES), F32),
-            dma((7,)), dma((n,)), dma((1,)), dma((n,)), dma((n,)), dma((n,)), dma((n,)), dma((n,)),
+            pltpu.VMEM((3, LANES, LANES), F32),
+            pltpu.VMEM((8, LANES), F32),
+            pltpu.VMEM((n, 8, LANES), F32),
+            pltpu.VMEM((16, LANES), F32),
+            pltpu.VMEM((n, 16, LANES), F32),
+            dma((n,)), dma((1,)), dma((n,)), dma((n,)), dma((n,)), dma((n,)), dma((n,)), dma((n,)), dma((n,)),
         ],
         compiler_params=pltpu.CompilerParams(
             collective_id=1, has_side_effects=True, vmem_limit_bytes=56 << 20
@@ -1072,14 +1114,12 @@
 
 
 def finish_kernel(
-    n, points_hbm, counts_ref, small, stat, linear, joined, grad_feature, grad_a, grad_b,
-    weight, moment, second, momentum,
-    moment_out, second_out, momentum_out, weight_out,
+    n, rows, points_hbm, points_in, counts_ref, small, stat, first_out, pooled_in, grad_feature, grad_a, grad_b,
+    gradient,
     points, first, slots, pair, line, mine, notes, fc_rows, small_grad,
     sem_p, sem_ps, sem_pr, sem_zs, sem_zr, sem_ns, sem_nr,
 ):
     me = lax.axis_index("tile")
-    rows = weight.shape[0]
     half = n // 2
     parity, chip = lax.rem(me, 2), me // 2
     sibling = me + 1 - 2 * parity
@@ -1140,22 +1180,6 @@
     kernel_t = nt(order.astype(BF16), kernel).astype(BF16)
     kernel = nt(kernel, order.astype(BF16)).astype(BF16)
     bias = jnp.sum(jnp.where(order, rows_fc[64:65, :], 0.0), axis=1, keepdims=True)
-    counts_f = counts.astype(F32)
-    grad_pre = jnp.transpose(grad_feature[...]) / counts_f
-
-    def pass_e(p, carry):
-        fc, pooled = carry
-        inner = nn(kernel_t, joined[p, 0:64, :]) + bias
-        grad = jnp.where(p < counts, grad_pre * slope(inner), 0.0).astype(BF16)
-        fc += nt(joined[p], grad)
-        down = nn(kernel, grad)
-        first[p] = down[0:32]
-        return fc, pooled + down[32:64]
-
-    fc, pooled = lax.fori_loop(
-        0, count_p, pass_e, (jnp.zeros((80, LANES), F32), jnp.zeros((32, voxels), F32))
-    )
-    pooled = pooled / counts_f
     for load in loads:
         load.wait()
 
@@ -1163,30 +1187,51 @@
         high = value.astype(BF16)
         return high, (value - high.astype(F32)).astype(BF16)
 
-    def pass_f(p, carry):
-        moments, g_gamma, centred = carry
-        inside = p < counts
-        normed = jnp.where(inside, (linear[p] - mean) * scale, 0.0)
-        act = gamma * normed + beta
-        grad = jnp.where(inside, (first[p] + pooled) * slope(act), 0.0)
-        off = points[p] - centre
-        off_high, off_low = halves(off)
-        grad_high, grad_low = halves(grad)
-        norm_high, norm_low = halves(normed)
-        left = jnp.concatenate([grad_high, grad_low, norm_high, norm_low], axis=0)
-        right = jnp.concatenate([off_high, off_low], axis=0)
-        return (
-            moments + nt(left, right),
-            g_gamma + grad * normed,
-            centred + jnp.where(inside, off, 0.0),
-        )
-
-    moments, g_gamma, centred = lax.fori_loop(
-        0,
-        count_p,
-        pass_f,
-        (jnp.zeros((LANES, 16), F32), jnp.zeros((32, voxels), F32), jnp.zeros((8, voxels), F32)),
-    )
+    tail = jnp.where(row_of((16, CHUNK)) == 0, 1.0, 0.0).astype(BF16)
+    fc = jnp.zeros((80, LANES), F32)
+    moments, g_gamma, centred = jnp.zeros((LANES, 16), F32), jnp.zeros((32, CHUNK), F32), jnp.zeros((8, CHUNK), F32)
+    for c in range(voxels // CHUNK):
+        part = slice(c * CHUNK, (c + 1) * CHUNK)
+        held_c = counts[:, part]
+        counts_f = held_c.astype(F32)
+        grad_pre = jnp.transpose(grad_feature[part, :]) / counts_f
+        pooled_c = pooled_in[:, part]
+        fixed = nn(kernel_t[:, 32:64], pooled_c) + bias
+
+        def pass_e(p, carry, part=part, held_c=held_c, grad_pre=grad_pre, pooled_c=pooled_c, fixed=fixed):
+            fc, pooled = carry
+            start = first_out[p, :, part]
+            inner = nn(kernel_t[:, 0:32], start) + fixed
+            grad = jnp.where(p < held_c, grad_pre * slope(inner), 0.0).astype(BF16)
+            fc += nt(jnp.concatenate([start, pooled_c, tail], axis=0), grad)
+            down = nn(kernel, grad)
+            first[p] = down[0:32]
+            return fc, pooled + down[32:64]
+
+        fc, pooled = lax.fori_loop(0, count_p, pass_e, (fc, jnp.zeros((32, CHUNK), F32)), unroll=5)
+        pooled = pooled / counts_f
+        wide = [jnp.broadcast_to(column, (32, CHUNK)) for column in columns]
+        view = points_in.at[:, :, part]
+
+        def pass_f(p, carry, part=part, held_c=held_c, pooled=pooled, wide=wide, view=view):
+            moments, g_gamma, centred = carry
+            inside = p < held_c
+            normed = jnp.where(inside, (linear_row(wide, view, p) - mean) * scale, 0.0)
+            act = gamma * normed + beta
+            grad = jnp.where(inside, (first[p] + pooled) * slope(act), 0.0)
+            off = points[p, :, part] - centre
+            off_high, off_low = halves(off)
+            grad_high, grad_low = halves(grad)
+            norm_high, norm_low = halves(normed)
+            left = jnp.concatenate([grad_high, grad_low, norm_high, norm_low], axis=0)
+            right = jnp.concatenate([off_high, off_low], axis=0)
+            return (
+                moments + nt(left, right),
+                g_gamma + grad * normed,
+                centred + jnp.where(inside, off, 0.0),
+            )
+
+        moments, g_gamma, centred = lax.fori_loop(0, count_p, pass_f, (moments, g_gamma, centred), unroll=5)
     by_grad = moments[0:32] + moments[32:64]
     by_grad = by_grad[:, 0:8] + by_grad[:, 8:16]
     by_norm = moments[64:96] + moments[96:128]
@@ -1236,10 +1281,8 @@
         source = lax.rem(chip + half - k, half)
         remote(slots.at[0], line.at[source], sem_zs.at[k], sem_zr.at[source], sibling).wait_recv()
         total += line[source, 0:rows, :]
-    slots[me, 0:rows, :] = total
-    slots[me, 0:SMALL, :] = slots[me, 0:SMALL, :] + small_grad[...]
-    outs = adam_outer(slots[me, 0:rows, :], weight[...], moment[...], second[...], momentum[...])
-    moment_out[...], second_out[...], momentum_out[...], weight_out[...] = outs
+    gradient[...] = total
+    gradient[0:SMALL, :] = total[0:SMALL, :] + small_grad[...]
     for k in range(1, half):
         line_copy(k).wait_send()
 
@@ -1248,22 +1291,21 @@
         note(me).wait_send()
 
 
-def finish(n, points, counts, small, stat, linear, joined, grad_feature, grad_a, grad_b, shards):
+def finish(n, rows, points, counts, small, stat, first_out, pooled, grad_feature, grad_a, grad_b):
     shape = jax.ShapeDtypeStruct
     dma = pltpu.SemaphoreType.DMA
     slots, voxels = points.shape[1:]
-    rows = shards[0].shape[0]
     padded = ceil_to(rows, 8)
     half = n // 2
     return pl.pallas_call(
-        functools.partial(finish_kernel, n),
+        functools.partial(finish_kernel, n, rows),
         name="finish",
-        out_shape=(shape((rows, LANES), F32),) * 4,
-        in_specs=[anywhere()] + [vmem()] * 12,
-        out_specs=(vmem(),) * 4,
+        out_shape=shape((rows, LANES), F32),
+        in_specs=[anywhere()] + [vmem()] * 9,
+        out_specs=vmem(),
         scratch_shapes=[
             pltpu.VMEM((slots, 8, voxels), F32),
-            pltpu.VMEM((slots, 32, voxels), F32),
+            pltpu.VMEM((slots, 32, CHUNK), F32),
             pltpu.VMEM((n, padded, LANES), F32),
             pltpu.VMEM((half, padded, LANES), F32),
             pltpu.VMEM((half, padded, LANES), F32),
@@ -1276,7 +1318,29 @@
         compiler_params=pltpu.CompilerParams(
             collective_id=3, has_side_effects=True, vmem_limit_bytes=58 << 20
         ),
-    )(points, counts, small, stat, linear, joined, grad_feature, grad_a, grad_b, *shards)
+    )(points, points, counts, small, stat, first_out, pooled, grad_feature, grad_a, grad_b)
+
+
+def update_kernel(
+    gradient, weight, moment, second, momentum, loss, stat,
+    moment_out, second_out, momentum_out, weight_out, loss_out, positives_out,
+):
+    outs = adam_outer(gradient[...], weight[...], moment[...], second[...], momentum[...])
+    moment_out[...], second_out[...], momentum_out[...], weight_out[...] = outs
+    loss_out[0] = loss[0, 0]
+    positives_out[0] = stat[0, 3]
+
+
+def update(gradient, held, loss, stat):
+    shape = jax.ShapeDtypeStruct
+    return pl.pallas_call(
+        update_kernel,
+        name="update",
+        out_shape=(shape(gradient.shape, F32),) * 4 + (shape((1,), F32),) * 2,
+        in_specs=[vmem()] * 7,
+        out_specs=(vmem(),) * 4 + (smem(),) * 2,
+        compiler_params=pltpu.CompilerParams(vmem_limit_bytes=32 << 20),
+    )(gradient, *held, loss, stat)
 
 
 def shards(
@@ -1287,16 +1351,17 @@
     row_count = anchor_labels.shape[1]
     held = [x.reshape(rows, LANES) for x in (weights, adam_m, adam_v, outer_momentum)]
     counts = point_counts.reshape(1, -1)
-    wall, small, stat, linear, joined, feature = front(n, points, counts, anchor_labels, held[0])
+    wall, small, stat, first_out, pooled, feature = front(n, points, counts, anchor_labels, held[0])
     ready = middle(n, rows, row_count, voxel_cells, feature, wall)
     grad_a, grad_b, grad_feature, loss = convs(
         n, row_count, voxel_cells, feature, stat, ready, anchor_labels, box_targets
     )
-    outs = finish(
-        n, points, counts, small, stat, linear, joined, grad_feature, grad_a, grad_b, held
+    gradient = finish(
+        n, rows, points, counts, small, stat, first_out, pooled, grad_feature, grad_a, grad_b
     )
+    *outs, loss_sum, positives = update(gradient, held, loss, stat)
     moment, second, momentum, updated = [x.reshape(weights.shape) for x in outs]
-    return (moment, second, momentum, updated, loss[0, 0:1], stat[0, 3:4])
+    return (moment, second, momentum, updated, loss_sum, positives)
 
 
 def solution(mesh):

time: 202 us -> 181 us (0.90)
  Pallas kernels: 193 us -> 178 us
  local copies, waits for them, and re-layouts: 8.63 us -> 1.03 us
    pallas_call x1, Pallas kernels: 43.8 us -> 27.2 us  [front(): pl.pallas_call(functools.partial(front_kernel, n), name='front', out_shap...]
    unnamed x6 -> x14, local copies, waits for them, and re-layouts: 6.13 us -> 1.03 us
    pallas_call x1, Pallas kernels: 78.2 us -> 81.6 us  [convs(): pl.pallas_call(functools.partial(conv_kernel, n, row_count), name='convs'...]
    slice x2 -> x0, local copies, waits for them, and re-layouts: 2.5 us -> none  [shards(): return (moment, second, momentum, updated, loss[0, 0:1], stat[0, 3:4])]
    pallas_call x1 -> x2, Pallas kernels: 54.4 us -> 53.5 us  [the longest x1 51.9 us: finish(): pl.pallas_call(functools.partial(finish_kernel, n, rows), name='finish',...]
where the time goes in v2:
time: 181 us; the launch traced here: 180 us
  Pallas kernels  178 us (98%)
    pallas_call x1, Pallas kernels, convs(): pl.pallas_call(functools.partial(conv_kernel, n, row_count), name='convs'...  81.6 us
    pallas_call x1, Pallas kernels, finish(): pl.pallas_call(functools.partial(finish_kernel, n, rows), name='finish',...  51.9 us
    pallas_call x1, Pallas kernels, front(): pl.pallas_call(functools.partial(front_kernel, n), name='front', out_shap...  27.2 us
    pallas_call x1, Pallas kernels, middle(): pl.pallas_call(functools.partial(middle_kernel, n, rows, row_count), name...  16.2 us

profile of v2, /device:TPU:0, one launch (start us, length us, event | category | flops | bytes accessed | tf_op | source)
XLA Modules:
  0.0 180.4 jit_solution(16303271552212100516)
XLA Ops:
  0.6 27.2 %front.1 = (bf16[8,816,128]{2,1,0:T(8,128)(2,1)}, f32[80,128]{1,0:T(8,128)}, f32[48,128]{1,0:T(8,128)}, bf16[35,32,512]{2,1,0:T(8,128)(2,1)}, bf16[32,512]{1,0:T(8,128)(2,1)}, /*index=5*/f32[512,128]{1,0:T(8,128)}) custom-call(f32[7,35,512]{2,1,0:T(8,128)} %points_in.1, s32[1,512]{1,0:T(1,128)} %bitcast.17, s32[2,32,128]{2,1,0:T(8,128)} %labels_hbm.1, ...), custom_call_target="tpu_custom_call" | custom-call | tf_op jit(solution)/shard_map/front/pallas_call | solution.py:350
  27.8 16.2 %middle.1 = (f32[37,128,128]{2,1,0:T(8,128)}, bf16[512,1152]{1,0:T(8,128)(2,1)}, bf16[1536,256]{1,0:T(8,128)(2,1)}, bf16[1536,256]{1,0:T(8,128)(2,1)}, bf16[1152...) custom-call(s32[512]{0:T(512)} %cells_smem.3, ...), custom_call_target="tpu_custom_call" | custom-call | tf_op jit(solution)/shard_map/middle/pallas_call | solution.py:536
  44.0 81.6 %convs.1 = (f32[1800,128]{1,0:T(8,128)}, f32[4656,128]{1,0:T(8,128)}, f32[512,128]{1,0:T(8,128)}, f32[8,128]{1,0:T(8,128)}) custom-call(s32[512]{0:T(512)} %cells_smem.3, s32[1,512]{1,0:T(1,128)} %bitcast.16, f32[512,128]{1,0:T(8,128)} %get-tuple-element.35.feature, f32[48,128]{1,0:T(8,128)} %get-tuple-element.32.stat, ...), custom_call_target="tpu_custom_call" | custom-call | tf_op jit(solution)/shard_map/convs/pallas_call | solution.py:1040
  125.6 0.0 copy-start
  125.6 0.0 copy-start.2
  125.6 0.0 copy-start.3
  125.6 0.0 copy-start.4
  125.6 0.0 copy-start.5
  125.6 0.0 copy-start.6
  125.6 51.9 %finish.1.gradient = f32[805,128]{1,0:T(8,128)} custom-call(f32[7,35,512]{2,1,0:T(8,128)} %points_in.1, f32[7,35,512]{2,1,0:T(8,128)} %points_in.1, s32[1,512]{1,0:T(1,128)} %bitcast.18, f32[80,128]{1,0:T(8,128)} %get-tuple-element.31.small, f32[48,128]{1,0:T(8,128)} %get-tuple-element.32.stat, bf16[35,32,512]{2,1,0:T(8,128)(2,1)} %get-tuple-element.33.first_out, ...), custom_call_target="tpu_custom_call" | custom-call | tf_op jit(solution)/shard_map/finish/pallas_call | solution.py:1300
  177.5 0.0 copy-done
  177.6 0.0 copy-done.2
  177.6 0.0 copy-done.3
  177.6 0.0 copy-done.4
  177.6 0.0 copy-done.5
  177.6 0.0 copy-done.6
  177.6 0.0 copy-start.1
  177.6 1.0 copy-done.1
  178.6 1.7 update.1
Async XLA Ops:
  125.6 52.0 %copy-start = (f32[103040]{0:T(1024)S(1)}, f32[103040]{0:T(1024)}, u32[]{:S(2)}) copy-start(f32[103040]{0:T(1024)} %param.14) | copy-start | bytes 1236484
  125.6 52.0 %copy-start.2 = (f32[103040]{0:T(1024)S(1)}, f32[103040]{0:T(1024)}, u32[]{:S(2)}) copy-start(f32[103040]{0:T(1024)} %param.15) | copy-start | bytes 1236484
  125.6 52.0 %copy-start.3 = (f32[103040]{0:T(1024)S(1)}, f32[103040]{0:T(1024)}, u32[]{:S(2)}) copy-start(f32[103040]{0:T(1024)} %param.16) | copy-start | bytes 1236484
  125.6 52.0 %copy-start.4 = (f32[103040]{0:T(1024)S(1)}, f32[103040]{0:T(1024)}, u32[]{:S(2)}) copy-start(f32[103040]{0:T(1024)} %param.17) | copy-start | bytes 1236484
  125.6 52.0 %copy-start.5 = (f32[48,128]{1,0:T(8,128)S(1)}, f32[48,128]{1,0:T(8,128)}, u32[]{:S(2)}) copy-start(f32[48,128]{1,0:T(8,128)} %get-tuple-element.32.stat) | copy-start | bytes 73732
  125.6 52.0 %copy-start.6 = (f32[8,128]{1,0:T(8,128)S(1)}, f32[8,128]{1,0:T(8,128)}, u32[]{:S(2)}) copy-start(f32[8,128]{1,0:T(8,128)} %get-tuple-element.49.loss) | copy-start | bytes 12292
  177.6 1.0 copy-start.1

commit v3 on v2

--- a/solution.py
+++ b/solution.py
@@ -65,6 +65,15 @@
     return s * (1.0 + value * (1.0 - s))
 
 
+def half_silu(half):
+    return half * (1.0 + jnp.tanh(half))
+
+
+def half_slope(half):
+    t = jnp.tanh(half)
+    return (1.0 + t) * (1.0 + half * (1.0 - t))
+
+
 def nt(a, b, precision=None):
     return lax.dot_general(a, b, (((1,), (1,)), ((), ())), precision=precision, preferred_element_type=F32)
 
@@ -130,6 +139,38 @@
     here, after = small_ref[2:74, :], small_ref[3:75, :]
     mixed = jnp.where(lane_of((72, LANES)) >= FC_LANE, here, after)
     return pltpu.roll(mixed, LANES - FC_LANE, axis=1)
+
+
+def layout(n, row_count):
+    first = lax.axis_index("tile") * row_count
+    ahead = (first // H_SCENE + 1) * H_SCENE - first
+    split = jnp.where(ahead < row_count, 1, 0)
+    edge = jnp.where(ahead < row_count, ahead, row_count)
+    top = jnp.where(lax.rem(first, H_SCENE) != 0, 1, 0)
+    last = first + row_count
+    bottom = jnp.where((lax.rem(last, H_SCENE) != 0) & (last < n * row_count), 1, 0)
+    return edge, split, top, bottom
+
+
+def place_ok(place, edge, split, row_count):
+    return (place >= 1) & (place <= row_count + split) & ((place != edge + 1) | (split == 0))
+
+
+def place_row(place, edge, row_count):
+    row = jnp.where(place <= edge, place - 1, place - 2)
+    return jnp.clip(row, 0, row_count - 1)
+
+
+PITCH = 136
+
+
+def voxel_bases(cells, n, row_count, columns):
+    edge, split, _, _ = layout(n, row_count)
+    local = lax.rem(cells, row_count * columns * ZD)
+    row = local // (columns * ZD)
+    column = lax.rem(local, columns * ZD) // ZD
+    place = row + 1 + jnp.where((row >= edge) & (split == 1), 1, 0)
+    return (place - 1) * PITCH + column + 7
 
 
 def linear_row(wide, points, p):
@@ -203,8 +244,8 @@
 
 
 def front_kernel(
-    n, points, counts_ref, labels_ref, shard_ref,
-    wall, small, stat, first_out, pooled_out, feature,
+    n, points, counts_ref, cells_ref, labels_ref, shard_ref,
+    wall, small, stat, first_out, pooled_out, feature, bases,
     own, sums, mine, messages, my_bias, biases,
     sem_small_s, sem_small_r, sem_msg_s, sem_msg_r, sem_b_s, sem_b_r, sem_w_s, sem_w_r, sem_f_s,
 ):
@@ -217,6 +258,7 @@
 
     def prepare():
         local_moments(points, counts, labels_ref, sums, mine)
+        bases[...] = voxel_bases(cells_ref[...], n, labels_ref.shape[1], labels_ref.shape[2])
         own[...] = jnp.zeros_like(own)
         own[0:rows, :] = shard_ref[...].astype(BF16)
         for a, row in enumerate(BIAS_ROWS):
@@ -269,8 +311,8 @@
     columns, gamma, beta = first_layer(small)
     order = even_first()
     rows_fc = voxel_rows(small)
-    kernel_t = nt(order.astype(BF16), rows_fc[0:64, :].astype(BF16)).astype(BF16)
-    bias = jnp.sum(jnp.where(order, rows_fc[64:65, :], 0.0), axis=1, keepdims=True)
+    kernel_t = (0.5 * nt(order.astype(BF16), rows_fc[0:64, :].astype(BF16))).astype(BF16)
+    bias = 0.5 * jnp.sum(jnp.where(order, rows_fc[64:65, :], 0.0), axis=1, keepdims=True)
     for k in range(1, n):
         sender = lax.rem(me + n - k, n)
         remote(mine, messages.at[sender], sem_msg_s.at[k], sem_msg_r.at[sender], sender).wait_recv()
@@ -285,6 +327,7 @@
         columns_out = jnp.where((lane == 4) & (row == k), mean_row[:, r : r + 1], columns_out)
     stat[0:32, :] = columns_out
 
+    half_gamma, half_beta = 0.5 * gamma, 0.5 * beta
     for c in range(voxels // CHUNK):
         part = slice(c * CHUNK, (c + 1) * CHUNK)
         wide = [jnp.broadcast_to(column, (32, CHUNK)) for column in columns]
@@ -292,8 +335,8 @@
         view = points.at[:, :, part]
 
         def pass_c(p, pooled, wide=wide, held_c=held_c, view=view, part=part):
-            act = gamma * ((linear_row(wide, view, p) - mean) * inverse) + beta
-            out = jnp.where(p < held_c, act * sigmoid(act), 0.0)
+            half_act = half_gamma * ((linear_row(wide, view, p) - mean) * inverse) + half_beta
+            out = jnp.where(p < held_c, half_silu(half_act), 0.0)
             first_out[p, :, part] = out.astype(BF16)
             return pooled + out
 
@@ -303,10 +346,10 @@
         fixed = nn(kernel_t[:, 32:64], pooled) + bias
 
         def pass_d(p, total, fixed=fixed, held_c=held_c, part=part):
-            inner = nn(kernel_t[:, 0:32], first_out[p, :, part]) + fixed
-            return total + jnp.where(p < held_c, inner * sigmoid(inner), 0.0)
-
-        total = lax.fori_loop(0, slots, pass_d, jnp.zeros((LANES, CHUNK), F32), unroll=5)
+            half_inner = nn(kernel_t[:, 0:32], first_out[p, :, part]) + fixed
+            return total + jnp.where(p < held_c, half_silu(half_inner), 0.0)
+
+        total = lax.fori_loop(0, slots, pass_d, jnp.zeros((LANES, CHUNK), F32), unroll=7)
         feature[part, :] = jnp.transpose(total / held_c.astype(F32))
 
     for k in range(1, half):
@@ -341,7 +384,7 @@
         lax.fori_loop(1, n, done, 0)
 
 
-def front(n, points, counts, labels, shard):
+def front(n, points, counts, cells, labels, shard):
     slots, voxels = points.shape[1:]
     rows = shard.shape[0]
     padded = ceil_to(rows, 16)
@@ -357,9 +400,10 @@
             shape((slots, 32, voxels), BF16),
             shape((32, voxels), BF16),
             shape((voxels, LANES), F32),
+            shape((1, voxels), jnp.int32),
         ),
-        in_specs=[vmem()] * 4,
-        out_specs=(vmem(),) * 6,
+        in_specs=[vmem()] * 5,
+        out_specs=(vmem(),) * 7,
         scratch_shapes=[
             pltpu.VMEM((padded, LANES), BF16),
             pltpu.VMEM((3, LANES, LANES), F32),
@@ -372,39 +416,75 @@
         compiler_params=pltpu.CompilerParams(
             collective_id=1, has_side_effects=True, vmem_limit_bytes=56 << 20
         ),
-    )(points, counts, labels, shard)
-
-
-def layout(n, row_count):
-    first = lax.axis_index("tile") * row_count
-    ahead = (first // H_SCENE + 1) * H_SCENE - first
-    split = jnp.where(ahead < row_count, 1, 0)
-    edge = jnp.where(ahead < row_count, ahead, row_count)
-    top = jnp.where(lax.rem(first, H_SCENE) != 0, 1, 0)
-    last = first + row_count
-    bottom = jnp.where((lax.rem(last, H_SCENE) != 0) & (last < n * row_count), 1, 0)
-    return edge, split, top, bottom
-
-
-def place_ok(place, edge, split, row_count):
-    return (place >= 1) & (place <= row_count + split) & ((place != edge + 1) | (split == 0))
-
-
-def place_row(place, edge, row_count):
-    row = jnp.where(place <= edge, place - 1, place - 2)
-    return jnp.clip(row, 0, row_count - 1)
-
-
-PITCH = 136
-
-
-def voxel_base(cell, depth_cells, columns, edge, split):
-    local = lax.rem(cell, depth_cells)
-    spot = local // ZD
-    row = spot // columns
-    column = spot - row * columns
-    place = row + 1 + jnp.where((row >= edge) & (split == 1), 1, 0)
-    return place * PITCH + column + 7
+    )(points, counts, cells, labels, shard)
+
+
+def flat_pieces(rows, slot):
+    begin, end = slot * rows, (slot + 1) * rows
+    spans = ((0, 67, None, 0), (67, 1795, "a", 2), (1795, 1796, "both", 0), (1796, 6440, "b", 1795), (6440, 1 << 30, None, 0))
+    pieces = []
+    for low, high, run, shift in spans:
+        first, last = max(begin, low), min(end, high)
+        if first < last:
+            pieces.append((first - begin, last - first, run, first - shift))
+    return pieces
+
+
+def flat_slot(slot, rows, low, high, grad_a, grad_b, out_ref):
+    def realigned(ref, start, count, lane):
+        here, before = ref[pl.ds(start, count), :], ref[pl.ds(start - 1, count), :]
+        mixed = jnp.where(lane_of((count, LANES)) >= LANES - lane, before, here)
+        return pltpu.roll(mixed, lane, axis=1)
+
+    for row, count, run, start in flat_pieces(rows, slot):
+        first, last = max(row, low), min(row + count, high)
+        if first >= last:
+            continue
+        start, row, count = start + first - row, first, last - first
+        if run is None:
+            value = jnp.zeros((count, LANES), F32)
+        elif run == "a":
+            value = realigned(grad_a, start, count, 32)
+        elif run == "b":
+            value = realigned(grad_b, start, count, 96)
+        else:
+            lane = lane_of((1, LANES))
+            part_a = jnp.where(lane >= 96, grad_a[1792:1793, :], grad_a[1793:1794, :])
+            part_b = jnp.where(lane >= 32, 0.0, grad_b[0:1, :])
+            part_a = pltpu.roll(jnp.broadcast_to(part_a, (8, LANES)), 32, axis=1)
+            part_b = pltpu.roll(jnp.broadcast_to(part_b, (8, LANES)), 96, axis=1)
+            value = jnp.where(lane < 96, part_a[0:1], part_b[0:1])
+        out_ref[row : row + count, :] = value
+
+
+class Piece:
+    def __init__(self, chip, row, count, stage, order):
+        self.chip, self.group, self.side = chip, chip // 2, chip % 2
+        self.row, self.count, self.stage, self.order = row, count, stage, order
+        self.rows = pl.ds(row, count)
+
+
+def shard_pieces(n, rows):
+    padded = ceil_to(rows, 8)
+    early, late = [], []
+    for chip in range(n // 2):
+        first = 2 * chip * rows
+        cut = min(ceil_to(min(max(1796 - first, 0), rows), 8), padded)
+        spans = [(0, cut)] if cut else []
+        if cut >= 400:
+            half = ceil_to(cut // 2, 8)
+            spans = [(0, half), (half, cut)]
+        for order, (low, high) in enumerate(spans):
+            late.append(Piece(chip, low, high - low, 3, order))
+        if cut < padded:
+            begin = first + cut
+            stage = 0 if begin >= 4102 else 1 if begin >= 2949 else 2
+            early.append(Piece(chip, cut, padded - cut, stage, 2))
+    return early, late
+
+
+def late_chips(n, rows):
+    return max(piece.chip for piece in shard_pieces(n, rows)[1]) + 1
 
 
 def z_columns(cells_row):
@@ -419,11 +499,10 @@
 
 def middle_kernel(
     n, rows, row_count,
-    cells_smem, cells_row, feature, wall,
+    bases, cells_row, feature, wall,
     pre, w_mid, f_one, f_two, f_three, d_one, d_two, d_three, head_t,
     flat, run, spread, parts0, parts1, parts2, sum0, sum1, sum2,
 ):
-    edge, split, _, _ = layout(n, row_count)
     voxels = feature.shape[0]
     columns = LANES
     parts, sums = (parts0, parts1, parts2), (sum0, sum1, sum2)
@@ -457,16 +536,14 @@
             parts[i][pl.ds(2 - j, voxels, 4), :] = product[:, j * LANES : (j + 1) * LANES]
         sums[i][...] = jnp.zeros_like(sums[i])
 
-    depth_cells = row_count * columns * ZD
-
     def add(v, carry):
-        base = voxel_base(cells_smem[v], depth_cells, columns, edge, split)
+        base = bases[0, v]
         for i in range(3):
-            spot = pl.ds(base + (1 - i) * PITCH, 3)
+            spot = pl.ds(base + (2 - i) * PITCH, 3)
             sums[i][spot, :] = sums[i][spot, :] + parts[i][pl.ds(4 * v, 3), :]
         return carry
 
-    lax.fori_loop(0, voxels, add, 0, unroll=4)
+    lax.fori_loop(0, voxels, add, 0, unroll=8)
 
     def gather(p, carry):
         spot = pl.ds(pl.multiple_of(p * PITCH + 8, 8), columns)
@@ -529,7 +606,7 @@
     return (lax.rem(lane_of((16, LANES)), 16) == row_of((16, LANES))).astype(F32).astype(BF16)
 
 
-def middle(n, rows, row_count, cells, feature, wall):
+def middle(n, rows, row_count, bases, cells, feature, wall):
     shape = jax.ShapeDtypeStruct
     voxels = feature.shape[0]
     cells_all = (row_count + 6) * PITCH
@@ -561,7 +638,7 @@
             pltpu.VMEM((cells_all, LANES), F32),
         ],
         compiler_params=pltpu.CompilerParams(vmem_limit_bytes=56 << 20),
-    )(cells, cells.reshape(1, -1), feature, wall)
+    )(bases, cells, feature, wall)
 
 
 PAIRS = 18
@@ -573,16 +650,17 @@
 
 
 def conv_kernel(
-    n, row_count,
-    cells_smem, cells_row, feature, stat, pre_in, w_mid, f_one, f_two, f_three, d_one, d_two, d_three, head_t,
+    n, rows_dev, row_count,
+    bases, cells_row, feature, stat, pre_in, w_mid, f_one, f_two, f_three, d_one, d_two, d_three, head_t,
     labels_hbm, boxes_hbm,
-    grad_a, grad_b, grad_feature, loss_out,
+    late, early_part, grad_feature, loss_out,
+    grad_a, grad_b, slots, core_in, chip_in,
     x_one, x_two, x_three, pre_mid, pre_one, pre_two, back, spread,
     acc0, acc1, acc2,
     labels, boxes, logit_grads, loss_mine, loss_all,
     up_f, down_f, from_up_f, from_down_f, send_up, send_down, from_up, from_down,
     send_up_w, send_down_w, from_up_w, from_down_w,
-    sem_t, sem_fs, sem_fr, sem_s, sem_r, sem_ws, sem_wr, sem_ls, sem_lr,
+    sem_t, sem_fs, sem_fr, sem_s, sem_r, sem_ws, sem_wr, sem_ls, sem_lr, sem_cs, sem_cr, sem_zs, sem_zr,
 ):
     me = lax.axis_index("tile")
     edge, split, top, bottom = layout(n, row_count)
@@ -596,6 +674,57 @@
         load.start()
     enter(n, me)
 
+    early, late_list = shard_pieces(n, rows_dev)
+    core, side = lax.rem(me, 2), lax.rem(me // 2, 2)
+    sibling, other = me + 1 - 2 * core, me + 2 - 4 * side
+
+    def core_copy(i):
+        piece = early[i]
+        return remote(
+            slots.at[2 * piece.chip + 1 - core, piece.rows],
+            core_in.at[piece.chip, piece.rows],
+            sem_cs.at[i], sem_cr.at[i], sibling,
+        )
+
+    def chip_copy(i):
+        piece = early[i]
+        return remote(
+            slots.at[2 * piece.chip + core, piece.rows],
+            chip_in.at[piece.group, piece.rows],
+            sem_zs.at[i], sem_zr.at[i], other,
+        )
+
+    def ship(stage):
+        for i, piece in enumerate(early):
+            if piece.stage == stage:
+                for s in (2 * piece.chip, 2 * piece.chip + 1):
+                    flat_slot(s, rows_dev, piece.row, piece.row + piece.count, grad_a, grad_b, slots.at[s])
+                core_copy(i).start()
+
+    def ship_on(stage):
+        for i, piece in enumerate(early):
+            if piece.stage == stage:
+                core_copy(i).wait()
+                spot = 2 * piece.chip + core
+                slots[spot, piece.rows, :] = slots[spot, piece.rows, :] + core_in[piece.chip, piece.rows, :]
+
+                @pl.when(side != piece.side)
+                def _(i=i):
+                    chip_copy(i).start()
+
+    def ship_end():
+        for i, piece in enumerate(early):
+
+            @pl.when(side != piece.side)
+            def _(i=i):
+                chip_copy(i).wait_send()
+
+            @pl.when(side == piece.side)
+            def _(i=i, piece=piece):
+                chip_copy(i).wait_recv()
+                own = slots[2 * piece.chip + core, piece.rows, :]
+                early_part[piece.group, piece.rows, :] = own + chip_in[piece.group, piece.rows, :]
+
     def ok(place):
         return place_ok(place, edge, split, row_count)
 
@@ -650,20 +779,29 @@
             lane = parity * width + (j * parts + part) * LANES
             ref[rows, lane : lane + LANES] = shift
 
-    def put_edges(ref, s, parts, up_halo, down_halo):
-        for part in range(parts):
-            lanes = slice(part * LANES, (part + 1) * LANES)
-            halo = pick((top == 1) & has_up, up_halo[:, lanes].astype(F32), 0.0)
-            put(ref, 0, 0, halo, part, parts)
-            halo = pick((bottom == 1) & has_down, down_halo[:, lanes].astype(F32), 0.0)
-            width = 3 * parts * LANES
-            row = pl.ds(16 * LANES, LANES)
-            for j, shift in enumerate(shifted(halo)):
-                lane = width + (j * parts + part) * LANES
-                ref[row, lane : lane + LANES] = pick(split == 1, ref[row, lane : lane + LANES], shift)
-            put(ref, 17, 0, pick(split == 1, halo, 0.0), part, parts)
-
-    grad_b[B_HEAD + 32 :, :] = jnp.zeros((B_ROWS - B_HEAD - 32, LANES), F32)
+    def edges(parts, up_halo, down_halo):
+        rows = []
+        for good, halo in (((top == 1) & has_up, up_halo), ((bottom == 1) & has_down, down_halo)):
+            pieces = [shifted(pick(good, halo[:, p * LANES : (p + 1) * LANES].astype(F32), 0.0)) for p in range(parts)]
+            rows.append(jnp.concatenate([pieces[p][j] for j in range(3) for p in range(parts)], axis=1))
+        return rows
+
+    def put_edges(ref, top_row, bottom_row):
+        width = top_row.shape[1]
+        ref[0:LANES, 0:width] = top_row
+        rows = slice(16 * LANES, 17 * LANES)
+        ref[rows, width : 2 * width] = pick(split == 1, ref[rows, width : 2 * width], bottom_row)
+        rows = slice(17 * LANES, 18 * LANES)
+        ref[rows, 0:width] = pick(split == 1, bottom_row, jnp.zeros_like(bottom_row))
+
+    def add_edges(ref, at_top, at_bottom):
+        width = at_top.shape[1]
+        ref[0:LANES, 0:width] += at_top
+        rows = slice(15 * LANES, 16 * LANES)
+        ref[rows, width : 2 * width] += pick(split == 1, 0.0, at_bottom)
+        rows = slice(16 * LANES, 17 * LANES)
+        ref[rows, 0:width] += pick(split == 1, at_bottom, 0.0)
+
     up_f[...] = pre_in[0]
     down_f[...] = pick(split == 1, pre_in[row_count + 2], pre_in[row_count + 1])
     copies = halo_copies(0, up_f, down_f, from_up_f, from_down_f, sem_fs, sem_fr)
@@ -672,37 +810,37 @@
         ref[0:LANES, 0:384] = jnp.zeros((LANES, 384), BF16)
         ref[18 * LANES : 20 * LANES, :] = jnp.zeros((2 * LANES, wide), BF16)
     spread_z(feature[...], z_columns(cells_row[...]), spread)
-    halo_wait(copies)
-
     bias_mid = stat[32:33, :]
     b_mid = jnp.concatenate([bias_mid[:, 32:96], bias_mid[:, 32:96]], axis=1)
-    last = row_count
-
-    def fold(q, carry):
+
+    def activated(value, x_ref, q, e):
+        value = pick(ok(2 * q + 1 + e), value * sigmoid(value), 0.0)
+        put(x_ref, q + e, 1 - e, value, 0, 1)
+
+    def mid_step(q, carry):
+        rows = pl.ds(pl.multiple_of(q * LANES, LANES), LANES)
         for e in range(2):
-            p = 2 * q + 1 + e
-            value = pre_in[p] + b_mid
-            value += pick((p == 1) & (top == 1) & has_up, from_up_f[...], 0.0)
-            value += pick((p == last + split) & (bottom == 1) & has_down, from_down_f[...], 0.0)
-            pre_mid[pl.ds(pl.multiple_of(q * LANES, LANES), LANES), e * LANES : (e + 1) * LANES] = value
+            value = pre_in[2 * q + 1 + e] + b_mid
+            pre_mid[rows, e * LANES : (e + 1) * LANES] = value
+            activated(value, x_one, q, e)
         return carry
 
-    lax.fori_loop(0, PAIRS, fold, 0)
-
-    def activate(pre_ref, x_ref, s):
+    lax.fori_loop(0, PAIRS, mid_step, 0)
+    halo_wait(copies)
+    at_top = pick((top == 1) & has_up, from_up_f[...], 0.0)
+    at_bottom = pick((bottom == 1) & has_down, from_down_f[...], 0.0)
+    add_edges(pre_mid, at_top, at_bottom)
+    for q, e in ((0, 0), (15, 1), (16, 0)):
+        activated(pre_mid[q * LANES : (q + 1) * LANES, e * LANES : (e + 1) * LANES], x_one, q, e)
+
+    def activate(pre_ref, x_ref):
         def step(q, carry):
             rows = pl.ds(pl.multiple_of(q * LANES, LANES), LANES)
             for e in range(2):
-                value = pre_ref[rows, e * LANES : (e + 1) * LANES]
-                value = pick(ok(2 * q + 1 + e), value * sigmoid(value), 0.0)
-                put(x_ref, q + e, 1 - e, value, 0, 1)
+                activated(pre_ref[rows, e * LANES : (e + 1) * LANES], x_ref, q, e)
             return carry
 
         lax.fori_loop(0, PAIRS, step, 0)
-        exchange(x_ref, s)
-        copies = thin(s)
-        halo_wait(copies)
-        put_edges(x_ref, s, 1, from_up[s], from_down[s])
 
     def exchange(x_ref, s):
         send_up[s] = x_ref[0:LANES, 512:640]
@@ -738,11 +876,18 @@
     def twice(row):
         return jnp.concatenate([row, row], axis=1)
 
-    activate(pre_mid, x_one, 0)
-    banded(x_one, f_one, twice(bias_row(33, 96)), pre_one)
-    activate(pre_one, x_two, 1)
-    banded(x_two, f_two, twice(bias_row(35, 96)), pre_two)
-    activate(pre_two, x_three, 2)
+    def layer_forward(x_ref, f_ref, bias, out_ref, s):
+        exchange(x_ref, s)
+        banded(x_ref, f_ref, twice(bias), out_ref)
+        halo_wait(thin(s))
+        top_row, bottom_row = edges(1, from_up[s], from_down[s])
+        put_edges(x_ref, top_row, bottom_row)
+        add_edges(out_ref, nn(top_row, f_ref[0:384, 0:LANES]), nn(bottom_row, f_ref[768:1152, 0:LANES]))
+
+    layer_forward(x_one, f_one, bias_row(33, 96), pre_one, 0)
+    activate(pre_one, x_two)
+    layer_forward(x_two, f_two, bias_row(35, 96), pre_two, 1)
+    activate(pre_two, x_three)
 
     def weight_grads(g_ref, x_ref, parts, write):
         width, wide = parts * LANES, 3 * parts * LANES
@@ -800,7 +945,12 @@
             return carry
 
         x_ref3 = x_three
+        exchange(x_three, 2)
         lax.fori_loop(0, STEPS, conv_step, 0)
+        halo_wait(thin(2))
+        top_row, bottom_row = edges(1, from_up[2], from_down[2])
+        put_edges(x_three, top_row, bottom_row)
+        add_edges(pre_three, nn(top_row, f_three[0:384, :]), nn(bottom_row, f_three[768:1152, :]))
 
         def head_step(q, carry):
             rows = pl.ds(pl.multiple_of(q * LANES, LANES), LANES)
@@ -890,13 +1040,18 @@
             start = B_THREE + 2 * (i * 3 + j) * LANES + part
             grad_b[pl.ds(start, LANES, 2), :] = block
 
+        banded_back(g_three, d_three, back)
         weight_grads(g_three, x_three, 2, write)
         sums = bias_grads(g_three, 2)
         grad_b[B_HEAD - 2 : B_HEAD - 1, :] = sums[:, 0:LANES]
         grad_b[B_HEAD - 1 : B_HEAD, :] = sums[:, LANES : 2 * LANES]
+        ship(0)
         halo_wait(copies)
-        put_edges(g_three, 0, 2, from_up_w[...], from_down_w[...])
-        banded_back(g_three, d_three, back)
+        add_back(d_three, *edges(2, from_up_w[...], from_down_w[...]))
+
+    def add_back(d_ref, top_row, bottom_row):
+        width = top_row.shape[1]
+        add_edges(back, nt(top_row, d_ref[0:LANES, 0:width]), nt(bottom_row, d_ref[0:LANES, 2 * width : 3 * width]))
 
     def loss_copy(k):
         return remote(loss_mine, loss_all.at[me], sem_ls.at[k], sem_lr.at[me], lax.rem(me + k, n))
@@ -920,24 +1075,32 @@
 
             lax.fori_loop(0, PAIRS, step, 0)
 
-        def layer(pre_ref, x_ref, d_ref, begin, s):
-            g_ref[0:LANES, 0:384] = jnp.zeros((LANES, 384), BF16)
-            grads_in(pre_ref)
-            exchange(g_ref, s)
-
+        def weights_of(x_ref, begin):
             def write(i, j, part, block):
                 start = begin + (i * 3 + j) * LANES
                 grad_b[start : start + LANES, :] = block
 
             weight_grads(g_ref, x_ref, 1, write)
             grad_b[begin + 1152 : begin + 1153, :] = bias_grads(g_ref, 1)
+
+        def from_edges(d_ref, s):
             halo_wait(thin(s))
-            put_edges(g_ref, s, 1, from_up[s], from_down[s])
-            banded_back(g_ref, d_ref, back)
-
+            add_back(d_ref, *edges(1, from_up[s], from_down[s]))
+
+        g_ref[0:LANES, 0:384] = jnp.zeros((LANES, 384), BF16)
         g_ref[18 * LANES : 20 * LANES, :] = jnp.zeros((2 * LANES, 768), BF16)
-        layer(pre_two, x_two, d_two, B_TWO, 3)
-        layer(pre_one, x_one, d_one, B_ONE, 4)
+        grads_in(pre_two)
+        exchange(g_ref, 3)
+        ship_on(0)
+        banded_back(g_ref, d_two, back)
+        weights_of(x_two, B_TWO)
+        ship(1)
+        from_edges(d_two, 3)
+        grads_in(pre_one)
+        exchange(g_ref, 4)
+        ship_on(1)
+        banded_back(g_ref, d_one, back)
+        from_edges(d_one, 4)
 
         g_map[...] = jnp.zeros_like(g_map)
 
@@ -964,6 +1127,8 @@
         send_up[5] = g_map[map_row(1), :].astype(BF16)
         send_down[5] = pick(split == 1, g_map[map_row(row_count + 1), :], g_map[map_row(row_count), :]).astype(BF16)
         halo_start(thin(5))
+        weights_of(x_one, B_ONE)
+        ship(2)
         halo_wait(thin(5))
         g_map[map_row(0), :] = pick((top == 1) & has_up, from_up[5].astype(F32), 0.0)
         halo = pick((bottom == 1) & has_down, from_down[5].astype(F32), 0.0)
@@ -972,15 +1137,15 @@
 
         wins = (win0, win1, win2)
         voxels = feature.shape[0]
-        depth_cells = row_count * LANES * ZD
 
         def fetch(v, carry):
-            base = voxel_base(cells_smem[v], depth_cells, LANES, edge, split)
+            base = bases[0, v]
             for i in range(3):
-                wins[i][pl.ds(4 * v, 3), :] = g_map[pl.ds(base + (1 - i) * PITCH, 3), :]
+                wins[i][pl.ds(4 * v, 3), :] = g_map[pl.ds(base + (2 - i) * PITCH, 3), :]
             return carry
 
         lax.fori_loop(0, voxels, fetch, 0, unroll=8)
+        ship_on(2)
         for i in range(3):
             for j in range(3):
                 lanes = slice((i * 3 + j) * LANES, (i * 3 + j + 1) * LANES)
@@ -1020,6 +1185,10 @@
         pltpu.VMEM((voxels * 4, LANES), F32),
         pltpu.VMEM((voxels, 1152), BF16),
     )
+    for piece in late_list:
+        for s in (2 * piece.chip, 2 * piece.chip + 1):
+            flat_slot(s, rows_dev, piece.row, piece.row + piece.count, grad_a, grad_b, late.at[s])
+    ship_end()
     for k in range(1, n):
         sender = lax.rem(me + n - k, n)
         remote(loss_mine, loss_all.at[sender], sem_ls.at[k], sem_lr.at[sender], sender).wait_recv()
@@ -1032,23 +1201,31 @@
         loss_copy(k).wait_send()
 
 
-def convs(n, row_count, cells, feature, stat, middle_out, labels, boxes):
+def convs(n, rows_dev, row_count, bases, cells, feature, stat, middle_out, labels, boxes):
     shape = jax.ShapeDtypeStruct
     dma = pltpu.SemaphoreType.DMA
     voxels = feature.shape[0]
     row = (LANES, LANES)
+    padded = ceil_to(rows_dev, 8)
+    early = len(shard_pieces(n, rows_dev)[0])
+    late = 2 * late_chips(n, rows_dev)
     return pl.pallas_call(
-        functools.partial(conv_kernel, n, row_count),
+        functools.partial(conv_kernel, n, rows_dev, row_count),
         name="convs",
         out_shape=(
-            shape((A_ROWS, LANES), F32),
-            shape((B_ROWS, LANES), F32),
+            shape((late, padded, LANES), F32),
+            shape((n // 4, padded, LANES), F32),
             shape((voxels, LANES), F32),
             shape((8, LANES), F32),
         ),
         in_specs=[smem()] + [vmem()] * 12 + [anywhere()] * 2,
         out_specs=(vmem(),) * 4,
         scratch_shapes=[
+            pltpu.VMEM((A_ROWS, LANES), F32),
+            pltpu.VMEM((B_ROWS, LANES), F32),
+            pltpu.VMEM((n, padded, LANES), F32),
+            pltpu.VMEM((n // 2, padded, LANES), F32),
+            pltpu.VMEM((n // 4, padded, LANES), F32),
             pltpu.VMEM((20 * LANES, 768), BF16),
             pltpu.VMEM((20 * LANES, 768), BF16),
             pltpu.VMEM((20 * LANES, 768), BF16),
@@ -1078,11 +1255,12 @@
             pltpu.VMEM((LANES, 256), BF16),
             pltpu.VMEM((LANES, 256), BF16),
             dma((16,)), dma((2,)), dma((2,)), dma((12,)), dma((12,)), dma((2,)), dma((2,)), dma((n,)), dma((n,)),
+            dma((early,)), dma((early,)), dma((early,)), dma((early,)),
         ],
         compiler_params=pltpu.CompilerParams(
             collective_id=2, has_side_effects=True, vmem_limit_bytes=62 << 20
         ),
-    )(cells, cells.reshape(1, -1), feature, stat, *middle_out, labels, boxes)
+    )(bases, cells, feature, stat, *middle_out, labels, boxes)
 
 
 def adam_outer(gradient, weight, moment, second, momentum):
@@ -1099,30 +1277,19 @@
     return (moment, second, momentum, updated)
 
 
-def flat_pieces(rows, slot):
-    begin, end = slot * rows, (slot + 1) * rows
-    spans = ((0, 67, None, 0), (67, 1795, "a", 2), (1795, 1796, "both", 0), (1796, 6440, "b", 1795), (6440, 1 << 30, None, 0))
-    pieces = []
-    for low, high, run, shift in spans:
-        first, last = max(begin, low), min(end, high)
-        if first < last:
-            pieces.append((first - begin, last - first, run, first - shift))
-    return pieces
-
-
-NOTE = 112
+NOTE_A, NOTE_B = 72, 40
 
 
 def finish_kernel(
-    n, rows, points_hbm, points_in, counts_ref, small, stat, first_out, pooled_in, grad_feature, grad_a, grad_b,
+    n, rows, points_hbm, points_in, counts_ref, small, stat, first_out, pooled_in, grad_feature, late, early_part,
     gradient,
-    points, first, slots, pair, line, mine, notes, fc_rows, small_grad,
-    sem_p, sem_ps, sem_pr, sem_zs, sem_zr, sem_ns, sem_nr,
+    points, first, inner_grads, core_in, chip_in, parts, far_in, mine_a, mine_b, notes_a, notes_b, fc_rows, small_grad,
+    sem_p, sem_cs, sem_cr, sem_zs, sem_zr, sem_fs, sem_fr, sem_ns, sem_nar, sem_nbr,
 ):
     me = lax.axis_index("tile")
-    half = n // 2
-    parity, chip = lax.rem(me, 2), me // 2
-    sibling = me + 1 - 2 * parity
+    early_list, late_list = shard_pieces(n, rows)
+    core, side, my_group = lax.rem(me, 2), lax.rem(me // 2, 2), me // 4
+    sibling, other = me + 1 - 2 * core, me + 2 - 4 * side
     count_p, voxels = points_hbm.shape[1], points_hbm.shape[2]
     points[...] = jnp.ones_like(points)
     loads = [
@@ -1132,43 +1299,37 @@
         load.start()
     enter(n, me)
 
-    def realigned(ref, start, count, lane):
-        here, before = ref[pl.ds(start, count), :], ref[pl.ds(start - 1, count), :]
-        mixed = jnp.where(lane_of((count, LANES)) >= LANES - lane, before, here)
-        return pltpu.roll(mixed, lane, axis=1)
-
-    for s in range(n):
-        for row, count, run, start in flat_pieces(rows, s):
-            if run is None:
-                value = jnp.zeros((count, LANES), F32)
-            elif run == "a":
-                value = realigned(grad_a, start, count, 32)
-            elif run == "b":
-                value = realigned(grad_b, start, count, 96)
-            else:
-                lane = lane_of((8, LANES))
-                part_a = jnp.where(lane[0:1] >= 96, grad_a[1792:1793, :], grad_a[1793:1794, :])
-                part_b = jnp.where(lane[0:1] >= 32, 0.0, grad_b[0:1, :])
-                part_a = pltpu.roll(jnp.broadcast_to(part_a, (8, LANES)), 32, axis=1)
-                part_b = pltpu.roll(jnp.broadcast_to(part_b, (8, LANES)), 96, axis=1)
-                value = (jnp.where(lane < 96, part_a, part_b))[0:1]
-            slots[s, row : row + count, :] = value
-
-    def pair_copy(k):
-        return remote(slots.at[2 * k + 1 - parity], pair.at[k], sem_ps.at[k], sem_pr.at[k], sibling)
-
-    for k in range(half):
-        pair_copy(k).start()
-
-    def line_copy(k):
-        target = lax.rem(me + 2 * k, n)
-        return remote(slots.at[target], line.at[chip], sem_zs.at[k], sem_zr.at[chip], target)
-
-    for k in range(half):
-        pair_copy(k).wait()
-        slots[2 * k + parity] = slots[2 * k + parity] + pair[k]
-    for k in range(1, half):
-        line_copy(k).start()
+    def core_copy(i):
+        piece = late_list[i]
+        return remote(
+            late.at[2 * piece.chip + 1 - core, piece.rows],
+            core_in.at[piece.chip, piece.rows],
+            sem_cs.at[i], sem_cr.at[i], sibling,
+        )
+
+    def chip_copy(i):
+        piece = late_list[i]
+        return remote(
+            core_in.at[piece.chip, piece.rows],
+            chip_in.at[piece.group, piece.rows],
+            sem_zs.at[i], sem_zr.at[i], other,
+        )
+
+    def far_copy(source, piece, sender, send):
+        owner = 4 * piece.group + 2 * side + core
+        received = sem_fr.at[3 * sender + piece.order]
+        return remote(source.at[piece.group, piece.rows], far_in.at[sender, piece.rows], send, received, owner)
+
+    def far_start(source, piece, i):
+        @pl.when((side == piece.side) & (my_group != piece.group))
+        def _():
+            far_copy(source, piece, my_group, sem_fs.at[i]).start()
+
+    for i in range(len(late_list)):
+        core_copy(i).start()
+    late_count = len(late_list)
+    for i, piece in enumerate(early_list):
+        far_start(early_part, piece, late_count + i)
 
     counts = counts_ref[...]
     columns, gamma, beta = first_layer(small)
@@ -1177,38 +1338,88 @@
     order = even_first()
     rows_fc = voxel_rows(small)
     kernel = rows_fc[0:64, :].astype(BF16)
-    kernel_t = nt(order.astype(BF16), kernel).astype(BF16)
+    kernel_t = (0.5 * nt(order.astype(BF16), kernel)).astype(BF16)
     kernel = nt(kernel, order.astype(BF16)).astype(BF16)
-    bias = jnp.sum(jnp.where(order, rows_fc[64:65, :], 0.0), axis=1, keepdims=True)
-    for load in loads:
-        load.wait()
+    bias = 0.5 * jnp.sum(jnp.where(order, rows_fc[64:65, :], 0.0), axis=1, keepdims=True)
+    half_gamma, half_beta = 0.5 * gamma, 0.5 * beta
+
+    def sums_of_cores():
+        for i, piece in enumerate(late_list):
+            core_copy(i).wait()
+            core_in[piece.chip, piece.rows, :] = (
+                core_in[piece.chip, piece.rows, :] + late[2 * piece.chip + core, piece.rows, :]
+            )
+
+            @pl.when(side != piece.side)
+            def _(i=i):
+                chip_copy(i).start()
+
+    def sums_of_chips(i):
+        piece = late_list[i]
+
+        @pl.when(side == piece.side)
+        def _():
+            chip_copy(i).wait_recv()
+            own = core_in[piece.chip, piece.rows, :]
+            parts[piece.group, piece.rows, :] = own + chip_in[piece.group, piece.rows, :]
+
+        far_start(parts, piece, i)
 
     def halves(value):
         high = value.astype(BF16)
         return high, (value - high.astype(F32)).astype(BF16)
 
+    def note(ref, notes, sender, s, received):
+        return remote(ref, notes.at[sender], sem_ns.at[s], received.at[sender], 0)
+
+    def send_note(s):
+        @pl.when(me > 0)
+        def _():
+            (note(mine_a, notes_a, me, 0, sem_nar) if s == 0 else note(mine_b, notes_b, me, 1, sem_nbr)).start()
+
     tail = jnp.where(row_of((16, CHUNK)) == 0, 1.0, 0.0).astype(BF16)
     fc = jnp.zeros((80, LANES), F32)
     moments, g_gamma, centred = jnp.zeros((LANES, 16), F32), jnp.zeros((32, CHUNK), F32), jnp.zeros((8, CHUNK), F32)
-    for c in range(voxels // CHUNK):
+    chunks = voxels // CHUNK
+    for c in range(chunks):
         part = slice(c * CHUNK, (c + 1) * CHUNK)
         held_c = counts[:, part]
         counts_f = held_c.astype(F32)
-        grad_pre = jnp.transpose(grad_feature[part, :]) / counts_f
+        grad_pre = (0.5 * jnp.transpose(grad_feature[part, :])) / counts_f
         pooled_c = pooled_in[:, part]
         fixed = nn(kernel_t[:, 32:64], pooled_c) + bias
 
-        def pass_e(p, carry, part=part, held_c=held_c, grad_pre=grad_pre, pooled_c=pooled_c, fixed=fixed):
+        def spot(p):
+            return pl.ds(pl.multiple_of(p * CHUNK, LANES), CHUNK)
+
+        def pass_e(p, carry, part=part, held_c=held_c, grad_pre=grad_pre, fixed=fixed):
+            half_inner = nn(kernel_t[:, 0:32], first_out[p, :, part]) + fixed
+            grad = jnp.where(p < held_c, grad_pre * half_slope(half_inner), 0.0)
+            inner_grads[:, spot(p)] = grad.astype(BF16)
+            return carry
+
+        lax.fori_loop(0, count_p, pass_e, 0, unroll=7)
+        if c == 0:
+            sums_of_cores()
+
+        def pass_g(p, carry, part=part, pooled_c=pooled_c):
             fc, pooled = carry
-            start = first_out[p, :, part]
-            inner = nn(kernel_t[:, 0:32], start) + fixed
-            grad = jnp.where(p < held_c, grad_pre * slope(inner), 0.0).astype(BF16)
-            fc += nt(jnp.concatenate([start, pooled_c, tail], axis=0), grad)
+            grad = inner_grads[:, spot(p)]
+            fc += nt(jnp.concatenate([first_out[p, :, part], pooled_c, tail], axis=0), grad)
             down = nn(kernel, grad)
             first[p] = down[0:32]
             return fc, pooled + down[32:64]
 
-        fc, pooled = lax.fori_loop(0, count_p, pass_e, (fc, jnp.zeros((32, CHUNK), F32)), unroll=5)
+        fc, pooled = lax.fori_loop(0, count_p, pass_g, (fc, jnp.zeros((32, CHUNK), F32)), unroll=5)
+        if c == 0:
+            for load in loads:
+                load.wait()
+            sums_of_chips(0)
+        if c == chunks - 1:
+            mine_a[...] = fc[0:NOTE_A]
+            send_note(0)
+            for i in range(2 if chunks > 1 else 1, late_count):
+                sums_of_chips(i)
         pooled = pooled / counts_f
         wide = [jnp.broadcast_to(column, (32, CHUNK)) for column in columns]
         view = points_in.at[:, :, part]
@@ -1217,8 +1428,8 @@
             moments, g_gamma, centred = carry
             inside = p < held_c
             normed = jnp.where(inside, (linear_row(wide, view, p) - mean) * scale, 0.0)
-            act = gamma * normed + beta
-            grad = jnp.where(inside, (first[p] + pooled) * slope(act), 0.0)
+            slopes = half_slope(half_gamma * normed + half_beta)
+            grad = jnp.where(inside, (0.5 * (first[p] + pooled)) * slopes, 0.0)
             off = points[p, :, part] - centre
             off_high, off_low = halves(off)
             grad_high, grad_low = halves(grad)
@@ -1232,36 +1443,34 @@
             )
 
         moments, g_gamma, centred = lax.fori_loop(0, count_p, pass_f, (moments, g_gamma, centred), unroll=5)
+        if c == 0 and chunks > 1 and late_count > 1:
+            sums_of_chips(1)
     by_grad = moments[0:32] + moments[32:64]
     by_grad = by_grad[:, 0:8] + by_grad[:, 8:16]
     by_norm = moments[64:96] + moments[96:128]
     by_norm = by_norm[:, 0:8] + by_norm[:, 8:16]
-    mine[...] = jnp.zeros_like(mine)
-    mine[0:72, :] = fc[0:72]
-    mine[72:104, 0:8] = by_grad
-    mine[72:104, 8:16] = by_norm
-    mine[72:104, 16:17] = jnp.sum(g_gamma, axis=1, keepdims=True)
-    mine[104:112, 0:1] = jnp.sum(centred, axis=1, keepdims=True)
+    mine_b[...] = jnp.zeros_like(mine_b)
+    mine_b[0:32, 0:8] = by_grad
+    mine_b[0:32, 8:16] = by_norm
+    mine_b[0:32, 16:17] = jnp.sum(g_gamma, axis=1, keepdims=True)
+    mine_b[32:40, 0:1] = jnp.sum(centred, axis=1, keepdims=True)
+    send_note(1)
     small_grad[...] = jnp.zeros_like(small_grad)
-
-    def note(sender):
-        return remote(mine, notes.at[sender], sem_ns.at[0], sem_nr.at[sender], 0)
-
-    @pl.when(me > 0)
-    def _():
-        note(me).start()
 
     @pl.when(me == 0)
     def _():
-        notes[0] = mine[...]
+        notes_a[0] = mine_a[...]
+        notes_b[0] = mine_b[...]
         for d in range(1, n):
-            note(d).wait_recv()
-        total = notes[0]
+            note(mine_a, notes_a, d, 0, sem_nar).wait_recv()
+            note(mine_b, notes_b, d, 1, sem_nbr).wait_recv()
+        fc_total, total = notes_a[0], notes_b[0]
         for d in range(1, n):
-            total += notes[d]
-        by_grad, by_norm = total[72:104, 0:8], total[72:104, 8:16]
-        g_gamma, g_beta = total[72:104, 16:17], total[72:104, 7:8]
-        off_sums = jnp.transpose(jnp.broadcast_to(total[104:112, 0:1], (8, LANES)))[0:32, 0:8]
+            fc_total += notes_a[d]
+            total += notes_b[d]
+        by_grad, by_norm = total[0:32, 0:8], total[0:32, 8:16]
+        g_gamma, g_beta = total[0:32, 16:17], total[0:32, 7:8]
+        off_sums = jnp.transpose(jnp.broadcast_to(total[32:40, 0:1], (8, LANES)))[0:32, 0:8]
         g_vfe = scale * gamma * (
             by_grad - g_beta / held * off_sums - g_gamma / held * by_norm
         )
@@ -1272,31 +1481,52 @@
         tall = jnp.where(lane == 0, tall0, 0.0) + jnp.where(lane == 1, tall1, 0.0) + jnp.where(lane == 2, tall2, 0.0)
         head = jnp.transpose(tall)[0:8]
         fc_rows[...] = jnp.zeros_like(fc_rows)
-        fc_rows[8:80, :] = nn(total[0:72], order.astype(F32), HIGH)
-        small_grad[2:74, :] = realigned(fc_rows, 8, 72, 32)
+        fc_rows[8:80, :] = nn(fc_total, order.astype(F32), HIGH)
+        here, before = fc_rows[8:80, :], fc_rows[7:79, :]
+        mixed = jnp.where(lane_of((72, LANES)) >= LANES - FC_LANE, before, here)
+        small_grad[2:74, :] = pltpu.roll(mixed, FC_LANE, axis=1)
         small_grad[0:8, :] = small_grad[0:8, :] + head
 
-    total = slots[me, 0:rows, :]
-    for k in range(1, half):
-        source = lax.rem(chip + half - k, half)
-        remote(slots.at[0], line.at[source], sem_zs.at[k], sem_zr.at[source], sibling).wait_recv()
-        total += line[source, 0:rows, :]
-    gradient[...] = total
-    gradient[0:SMALL, :] = total[0:SMALL, :] + small_grad[...]
-    for k in range(1, half):
-        line_copy(k).wait_send()
+    for i, piece in enumerate(late_list + early_list):
+        source = parts if i < late_count else early_part
+        count = min(piece.count, rows - piece.row)
+        taken = pl.ds(piece.row, count)
+        here = side == piece.side
+
+        @pl.when(here & (my_group == piece.group))
+        def _(source=source, piece=piece, taken=taken):
+            gradient[taken, :] = source[piece.group, taken, :]
+            for k in range(1, n // 4):
+                sender = lax.rem(my_group + n // 4 - k, n // 4)
+                far_copy(source, piece, sender, sem_fs.at[0]).wait_recv()
+                gradient[taken, :] = gradient[taken, :] + far_in[sender, taken, :]
+
+        @pl.when(here & (my_group != piece.group))
+        def _(source=source, piece=piece, i=i):
+            far_copy(source, piece, my_group, sem_fs.at[i]).wait_send()
+
+        if i < late_count:
+
+            @pl.when(side != piece.side)
+            def _(i=i):
+                chip_copy(i).wait_send()
+
+    gradient[0:SMALL, :] = gradient[0:SMALL, :] + small_grad[...]
 
     @pl.when(me > 0)
     def _():
-        note(me).wait_send()
-
-
-def finish(n, rows, points, counts, small, stat, first_out, pooled, grad_feature, grad_a, grad_b):
+        note(mine_a, notes_a, me, 0, sem_nar).wait_send()
+        note(mine_b, notes_b, me, 1, sem_nbr).wait_send()
+
+
+def finish(n, rows, points, counts, small, stat, first_out, pooled, grad_feature, late, early_part):
     shape = jax.ShapeDtypeStruct
     dma = pltpu.SemaphoreType.DMA
     slots, voxels = points.shape[1:]
     padded = ceil_to(rows, 8)
-    half = n // 2
+    fours = n // 4
+    chips, count = late.shape[0] // 2, len(shard_pieces(n, rows)[1])
+    everything = count + len(shard_pieces(n, rows)[0])
     return pl.pallas_call(
         functools.partial(finish_kernel, n, rows),
         name="finish",
@@ -1306,19 +1536,24 @@
         scratch_shapes=[
             pltpu.VMEM((slots, 8, voxels), F32),
             pltpu.VMEM((slots, 32, CHUNK), F32),
-            pltpu.VMEM((n, padded, LANES), F32),
-            pltpu.VMEM((half, padded, LANES), F32),
-            pltpu.VMEM((half, padded, LANES), F32),
-            pltpu.VMEM((NOTE, LANES), F32),
-            pltpu.VMEM((n, NOTE, LANES), F32),
+            pltpu.VMEM((LANES, slots * CHUNK), BF16),
+            pltpu.VMEM((chips, padded, LANES), F32),
+            pltpu.VMEM((fours, padded, LANES), F32),
+            pltpu.VMEM((fours, padded, LANES), F32),
+            pltpu.VMEM((fours, padded, LANES), F32),
+            pltpu.VMEM((NOTE_A, LANES), F32),
+            pltpu.VMEM((NOTE_B, LANES), F32),
+            pltpu.VMEM((n, NOTE_A, LANES), F32),
+            pltpu.VMEM((n, NOTE_B, LANES), F32),
             pltpu.VMEM((88, LANES), F32),
             pltpu.VMEM((SMALL, LANES), F32),
-            dma((7,)), dma((half,)), dma((half,)), dma((half,)), dma((half,)), dma((1,)), dma((n,)),
+            dma((7,)), dma((count,)), dma((count,)), dma((count,)), dma((count,)),
+            dma((everything,)), dma((3 * fours,)), dma((2,)), dma((n,)), dma((n,)),
         ],
         compiler_params=pltpu.CompilerParams(
             collective_id=3, has_side_effects=True, vmem_limit_bytes=58 << 20
         ),
-    )(points, points, counts, small, stat, first_out, pooled, grad_feature, grad_a, grad_b)
+    )(points, points, counts, small, stat, first_out, pooled, grad_feature, late, early_part)
 
 
 def update_kernel(
@@ -1351,13 +1586,16 @@
     row_count = anchor_labels.shape[1]
     held = [x.reshape(rows, LANES) for x in (weights, adam_m, adam_v, outer_momentum)]
     counts = point_counts.reshape(1, -1)
-    wall, small, stat, first_out, pooled, feature = front(n, points, counts, anchor_labels, held[0])
-    ready = middle(n, rows, row_count, voxel_cells, feature, wall)
-    grad_a, grad_b, grad_feature, loss = convs(
-        n, row_count, voxel_cells, feature, stat, ready, anchor_labels, box_targets
+    cells = voxel_cells.reshape(1, -1)
+    wall, small, stat, first_out, pooled, feature, bases = front(
+        n, points, counts, cells, anchor_labels, held[0]
+    )
+    ready = middle(n, rows, row_count, bases, cells, feature, wall)
+    late, early_part, grad_feature, loss = convs(
+        n, rows, row_count, bases, cells, feature, stat, ready, anchor_labels, box_targets
     )
     gradient = finish(
-        n, rows, points, counts, small, stat, first_out, pooled, grad_feature, grad_a, grad_b
+        n, rows, points, counts, small, stat, first_out, pooled, grad_feature, late, early_part
     )
     *outs, loss_sum, positives = update(gradient, held, loss, stat)
     moment, second, momentum, updated = [x.reshape(weights.shape) for x in outs]

time: 181 us -> 150 us (0.83)
  Pallas kernels: 178 us -> 147 us
    pallas_call x1, Pallas kernels: 51.9 us -> 38.3 us  [finish(): pl.pallas_call(functools.partial(finish_kernel, n, rows), name='finish',...]
    pallas_call x1, Pallas kernels: 81.6 us -> 70.5 us  [convs(): pl.pallas_call(functools.partial(conv_kernel, n, rows_dev, row_count), na...]
    pallas_call x1, Pallas kernels: 16.2 us -> 9.94 us  [middle(): pl.pallas_call(functools.partial(middle_kernel, n, rows, row_count), name...]
where the time goes in v3:
time: 150 us; the launch traced here: 149 us
  Pallas kernels  147 us (98%)
    pallas_call x1, Pallas kernels, convs(): pl.pallas_call(functools.partial(conv_kernel, n, rows_dev, row_count), na...  70.5 us
    pallas_call x1, Pallas kernels, finish(): pl.pallas_call(functools.partial(finish_kernel, n, rows), name='finish',...  38.3 us
    pallas_call x1, Pallas kernels, front(): pl.pallas_call(functools.partial(front_kernel, n), name='front', out_shap...  27.1 us
    pallas_call x1, Pallas kernels, middle(): pl.pallas_call(functools.partial(middle_kernel, n, rows, row_count), name...  9.94 us

profile of v3, /device:TPU:0, one launch (start us, length us, event | category | flops | bytes accessed | tf_op | source)
XLA Modules:
  0.0 149.4 jit_solution(9090914910059614947)
XLA Ops:
  0.6 27.1 %front.1 = (bf16[8,816,128]{2,1,0:T(8,128)(2,1)}, f32[80,128]{1,0:T(8,128)}, f32[48,128]{1,0:T(8,128)}, bf16[35,32,512]{2,1,0:T(8,128)(2,1)}, bf16[32,512]{1,0:T...) custom-call(f32[7,35,512]{2,1,0:T(8,128)} %points_in.1, s32[1,512]{1,0:T(1,128)} %bitcast.18, s32[1,512]{1,0:T(1,128)} %bitcast.15, ...), custom_call_target="tpu_custom_call" | custom-call | tf_op jit(solution)/shard_map/front/pallas_call | solution.py:393
  27.7 9.9 %middle.1 = (f32[37,128,128]{2,1,0:T(8,128)}, bf16[512,1152]{1,0:T(8,128)(2,1)}, bf16[1536,256]{1,0:T(8,128)(2,1)}, bf16[1536,256]{1,0:T(8,128)(2,1)}, bf16[1152...) custom-call(s32[1,512]{1,0:T(1,128)} %get-tuple-element.36.bases, ...), custom_call_target="tpu_custom_call" | custom-call | tf_op jit(solution)/shard_map/middle/pallas_call | solution.py:613
  37.6 70.5 %convs.1 = (f32[4,808,128]{2,1,0:T(8,128)}, f32[2,808,128]{2,1,0:T(8,128)}, f32[512,128]{1,0:T(8,128)}, f32[8,128]{1,0:T(8,128)}) custom-call(s32[1,512]{1,0:T(1,128)} %get-tuple-element.36.bases, s32[1,512]{1,0:T(1,128)} %bitcast.17, f32[512,128]{1,0:T(8,128)} %get-tuple-element.37.feature, f32[48,128]{1,0:T(8,128)} %get-tuple-element.33.stat, ...), custom_call_target="tpu_custom_call" | custom-call | tf_op jit(solution)/shard_map/convs/pallas_call | solution.py:1212
  108.2 0.0 copy-start
  108.2 0.0 copy-start.2
  108.2 0.0 copy-start.3
  108.2 0.0 copy-start.4
  108.2 0.0 copy-start.5
  108.2 0.0 copy-start.6
  108.2 38.3 %finish.1.gradient = f32[805,128]{1,0:T(8,128)} custom-call(f32[7,35,512]{2,1,0:T(8,128)} %points_in.1, f32[7,35,512]{2,1,0:T(8,128)} %points_in.1, s32[1,512]{1,0:T(1,128)} %bitcast.19, f32[80,128]{1,0:T(8,128)} %get-tuple-element.32.small, f32[48,128]{1,0:T(8,128)} %get-tuple-element.33.stat, bf16[35,32,512]{2,1,0:T(8,128)(2,1)} %get-tuple-element.34.first_out, ...), custom_call_target="tpu_custom_call" | custom-call | tf_op jit(solution)/shard_map/finish/pallas_call | solution.py:1530
  146.5 0.0 copy-done
  146.5 0.0 copy-done.2
  146.6 0.0 copy-done.3
  146.6 0.0 copy-done.4
  146.6 0.0 copy-done.5
  146.6 0.0 copy-done.6
  146.6 0.0 copy-start.1
  146.6 1.0 copy-done.1
  147.6 1.7 %update.1 = (f32[805,128]{1,0:T(8,128)}, f32[805,128]{1,0:T(8,128)}, f32[805,128]{1,0:T(8,128)}, f32[805,128]{1,0:T(8,128)}, f32[1]{0:T(128)}, /*index=5*/f32[1]{0:T(128)}) custom-call(f32[805,128]{1,0:T(8,128)S(1)} %copy-done.1, f32[805,128]{1,0:T(8,128)S(1)} %bitcast.11, f32[805,128]{1,0:T(8,128)S(1)} %bitcast.12, f32[805,128]{1,0:T(8,128)S(1)} %bitcast.13, ...), custom_call_target="tpu_custom_call" | custom-call | tf_op jit(solution)/shard_map/update/pallas_call | solution.py:1571
Async XLA Ops:
  108.2 38.4 %copy-start = (f32[103040]{0:T(1024)S(1)}, f32[103040]{0:T(1024)}, u32[]{:S(2)}) copy-start(f32[103040]{0:T(1024)} %param.14) | copy-start | bytes 1236484
  108.2 38.4 %copy-start.2 = (f32[103040]{0:T(1024)S(1)}, f32[103040]{0:T(1024)}, u32[]{:S(2)}) copy-start(f32[103040]{0:T(1024)} %param.15) | copy-start | bytes 1236484
  108.2 38.4 %copy-start.3 = (f32[103040]{0:T(1024)S(1)}, f32[103040]{0:T(1024)}, u32[]{:S(2)}) copy-start(f32[103040]{0:T(1024)} %param.16) | copy-start | bytes 1236484
  108.2 38.4 %copy-start.4 = (f32[103040]{0:T(1024)S(1)}, f32[103040]{0:T(1024)}, u32[]{:S(2)}) copy-start(f32[103040]{0:T(1024)} %param.17) | copy-start | bytes 1236484
  108.2 38.4 %copy-start.5 = (f32[48,128]{1,0:T(8,128)S(1)}, f32[48,128]{1,0:T(8,128)}, u32[]{:S(2)}) copy-start(f32[48,128]{1,0:T(8,128)} %get-tuple-element.33.stat) | copy-start | bytes 73732
  108.2 38.4 %copy-start.6 = (f32[8,128]{1,0:T(8,128)S(1)}, f32[8,128]{1,0:T(8,128)}, u32[]{:S(2)}) copy-start(f32[8,128]{1,0:T(8,128)} %get-tuple-element.51.loss) | copy-start | bytes 12292
  146.6 1.0 copy-start.1

commit v4 on v3

--- a/solution.py
+++ b/solution.py
@@ -247,7 +247,7 @@
     n, points, counts_ref, cells_ref, labels_ref, shard_ref,
     wall, small, stat, first_out, pooled_out, feature, bases,
     own, sums, mine, messages, my_bias, biases,
-    sem_small_s, sem_small_r, sem_msg_s, sem_msg_r, sem_b_s, sem_b_r, sem_w_s, sem_w_r, sem_f_s,
+    sem_small_s, sem_small_r, sem_msg_s, sem_msg_r, sem_b_s, sem_b_r, sem_w_s, sem_w_r, sem_f_s, sem_e_s,
 ):
     me = lax.axis_index("tile")
     rows = shard_ref.shape[0]
@@ -296,8 +296,45 @@
 
     for k in range(1, n):
         bias_message(k).start()
-    for k in range(1, half):
-        shard_copy(k).start()
+    line = me // 2
+    if n == 8:
+        inner = (line == 1) | (line == 2)
+        toward = jnp.where(line == 2, 2, -2)
+        turn = jnp.where(line == 0, 2, -2)
+
+        def own_copy(step, k):
+            return remote(own, wall.at[me], sem_w_s.at[k], sem_w_r.at[me], me + step)
+
+        @pl.when(inner)
+        def _():
+            own_copy(-toward, 1).start()
+            own_copy(toward, 2).start()
+
+        @pl.when(jnp.logical_not(inner))
+        def _():
+            own_copy(turn, 1).start()
+            own_copy(2 * turn, 2).start()
+
+    else:
+        for k in range(1, half):
+            shard_copy(k).start()
+
+    def arrived(source):
+        remote(own, wall.at[source], sem_w_s.at[0], sem_w_r.at[source], sibling).wait_recv()
+
+    def pass_on(source, k, peer, sem):
+        return remote(wall.at[source], wall.at[source], sem.at[k], sem_w_r.at[source], peer)
+
+    def relay(step):
+        if n == 8 and step < 2:
+
+            @pl.when(inner)
+            def _():
+                source = me - (step + 1) * toward
+                arrived(source)
+                pass_on(source, step, me + toward, sem_e_s).start()
+                pass_on(source, step + 1, sibling, sem_f_s).start()
+
     to_sibling = remote(own, wall.at[me], sem_w_s.at[0], sem_w_r.at[me], sibling)
     to_sibling.start()
     wall[me] = own[...]
@@ -351,11 +388,29 @@
 
         total = lax.fori_loop(0, slots, pass_d, jnp.zeros((LANES, CHUNK), F32), unroll=7)
         feature[part, :] = jnp.transpose(total / held_c.astype(F32))
-
-    for k in range(1, half):
-        source = lax.rem(me + n - 2 * k, n)
-        remote(own, wall.at[source], sem_w_s.at[k], sem_w_r.at[source], source).wait_recv()
-        remote(wall.at[source], wall.at[source], sem_f_s.at[k], sem_w_r.at[source], sibling).start()
+        relay(c)
+
+    for step in range(voxels // CHUNK, 2):
+        relay(step)
+    if n == 8:
+
+        @pl.when(inner)
+        def _():
+            source = me + toward
+            arrived(source)
+            pass_on(source, 3, sibling, sem_f_s).start()
+
+        @pl.when(jnp.logical_not(inner))
+        def _():
+            for k in range(1, 4):
+                arrived(me + k * turn)
+                pass_on(me + k * turn, k, sibling, sem_f_s).start()
+
+    else:
+        for k in range(1, half):
+            source = lax.rem(me + n - 2 * k, n)
+            arrived(source)
+            pass_on(source, k, sibling, sem_f_s).start()
     for k in range(1, n):
         sender = lax.rem(me + n - k, n)
         remote(my_bias, biases.at[sender], sem_b_s.at[k], sem_b_r.at[sender], sender).wait_recv()
@@ -364,12 +419,21 @@
         total += biases[d]
     stat[32:48, :] = total
     for k in range(half):
-        source = lax.rem(sibling + n - 2 * k, n)
-        remote(own, wall.at[source], sem_w_s.at[k], sem_w_r.at[source], source).wait_recv()
+        arrived(lax.rem(sibling + n - 2 * k, n))
     for k in range(1, half):
-        source = lax.rem(me + n - 2 * k, n)
-        remote(wall.at[source], wall.at[source], sem_f_s.at[k], sem_w_r.at[source], sibling).wait_send()
-        shard_copy(k).wait_send()
+        pass_on(me, k, sibling, sem_f_s).wait_send()
+    if n == 8:
+        for k in (1, 2):
+            own_copy(turn, k).wait_send()
+
+        @pl.when(inner)
+        def _():
+            for k in range(2):
+                pass_on(me, k, sibling, sem_e_s).wait_send()
+
+    else:
+        for k in range(1, half):
+            shard_copy(k).wait_send()
     to_sibling.wait_send()
     for k in range(1, n):
         message(k).wait_send()
@@ -411,7 +475,7 @@
             pltpu.VMEM((n, 8, LANES), F32),
             pltpu.VMEM((16, LANES), F32),
             pltpu.VMEM((n, 16, LANES), F32),
-            dma((n,)), dma((1,)), dma((n,)), dma((n,)), dma((n,)), dma((n,)), dma((n,)), dma((n,)), dma((n,)),
+            dma((n,)), dma((1,)), dma((n,)), dma((n,)), dma((n,)), dma((n,)), dma((n,)), dma((n,)), dma((n,)), dma((2,)),
         ],
         compiler_params=pltpu.CompilerParams(
             collective_id=1, has_side_effects=True, vmem_limit_bytes=56 << 20
@@ -466,25 +530,21 @@
 
 def shard_pieces(n, rows):
     padded = ceil_to(rows, 8)
-    early, late = [], []
+    pieces = []
     for chip in range(n // 2):
         first = 2 * chip * rows
         cut = min(ceil_to(min(max(1796 - first, 0), rows), 8), padded)
         spans = [(0, cut)] if cut else []
         if cut >= 400:
-            half = ceil_to(cut // 2, 8)
-            spans = [(0, half), (half, cut)]
+            marks = [ceil_to(cut * k // 4, 8) for k in range(4)] + [cut]
+            spans = list(zip(marks[:-1], marks[1:]))
         for order, (low, high) in enumerate(spans):
-            late.append(Piece(chip, low, high - low, 3, order))
+            pieces.append(Piece(chip, low, high - low, 3, order))
         if cut < padded:
             begin = first + cut
             stage = 0 if begin >= 4102 else 1 if begin >= 2949 else 2
-            early.append(Piece(chip, cut, padded - cut, stage, 2))
-    return early, late
-
-
-def late_chips(n, rows):
-    return max(piece.chip for piece in shard_pieces(n, rows)[1]) + 1
+            pieces.append(Piece(chip, cut, padded - cut, stage, 4))
+    return pieces
 
 
 def z_columns(cells_row):
@@ -500,9 +560,11 @@
 def middle_kernel(
     n, rows, row_count,
     bases, cells_row, feature, wall,
-    pre, w_mid, f_one, f_two, f_three, d_one, d_two, d_three, head_t,
-    flat, run, spread, parts0, parts1, parts2, sum0, sum1, sum2,
+    pre, *refs,
 ):
+    outs, kept, (flat, run, spread, parts0, parts1, parts2, sum0, sum1, sum2, sem) = refs[:8], refs[8:16], refs[16:]
+    w_mid, f_one, f_two, f_three, d_one, d_two, d_three, head_t = kept
+    stores = [pltpu.make_async_copy(kept[a], outs[a], sem.at[a]) for a in range(8)]
     voxels = feature.shape[0]
     columns = LANES
     parts, sums = (parts0, parts1, parts2), (sum0, sum1, sum2)
@@ -515,42 +577,6 @@
         after = flat[pl.ds(row + start + 1, count), :]
         mixed = jnp.where(lane_of((count, LANES)) >= lane, here, after)
         return pltpu.roll(mixed, LANES - lane, axis=1)
-
-    low = lane_of((64, LANES)) < 64
-    for ij in range(9):
-        taps = [aligned(RUN_A, A_MID + (t * 9 + ij) * 64, 64) for t in range(3)]
-        turned = [pltpu.roll(tap, 64, axis=1) for tap in taps]
-        none = jnp.zeros((64, LANES), F32)
-        for z in range(ZD):
-            first, second = z + 1, z - 1
-            a, a_t = (taps[first], turned[first]) if first < 3 else (none, none)
-            b, b_t = (taps[second], turned[second]) if second >= 0 else (none, none)
-            lanes = slice(ij * LANES, (ij + 1) * LANES)
-            w_mid[z * C2 : z * C2 + 64, lanes] = jnp.where(low, a, b_t).astype(BF16)
-            w_mid[z * C2 + 64 : (z + 1) * C2, lanes] = jnp.where(low, a_t, b).astype(BF16)
-
-    spread_z(feature[...], z_columns(cells_row[...]), spread)
-    for i in range(3):
-        product = nn(spread[...], w_mid[:, i * 384 : (i + 1) * 384])
-        for j in range(3):
-            parts[i][pl.ds(2 - j, voxels, 4), :] = product[:, j * LANES : (j + 1) * LANES]
-        sums[i][...] = jnp.zeros_like(sums[i])
-
-    def add(v, carry):
-        base = bases[0, v]
-        for i in range(3):
-            spot = pl.ds(base + (2 - i) * PITCH, 3)
-            sums[i][spot, :] = sums[i][spot, :] + parts[i][pl.ds(4 * v, 3), :]
-        return carry
-
-    lax.fori_loop(0, voxels, add, 0, unroll=8)
-
-    def gather(p, carry):
-        spot = pl.ds(pl.multiple_of(p * PITCH + 8, 8), columns)
-        pre[p] = sum0[spot, :] + sum1[spot, :] + sum2[spot, :]
-        return carry
-
-    lax.fori_loop(0, row_count + 5, gather, 0)
 
     def zero_half(ref, row, column, height, width):
         ref[row : row + height, column : column + width] = jnp.zeros((height, width), BF16)
@@ -574,6 +600,8 @@
         for i in range(3):
             for j in range(3):
                 tap(i, j)
+        for a in (1, 4) if begin == B_ONE else (2, 5):
+            stores[a].start()
     for j in range(3):
         for e in range(2):
             outside = 3 if e == 0 else 0
@@ -592,6 +620,47 @@
     chosen = nn(eighths(), head_rows)
     chosen = jnp.where(same_eighth(), chosen, 0.0).astype(BF16)
     head_t[...] = nt(fold16(), chosen).astype(BF16)
+    for a in (3, 6, 7):
+        stores[a].start()
+
+    low = lane_of((64, LANES)) < 64
+    for ij in range(9):
+        taps = [aligned(RUN_A, A_MID + (t * 9 + ij) * 64, 64) for t in range(3)]
+        turned = [pltpu.roll(tap, 64, axis=1) for tap in taps]
+        none = jnp.zeros((64, LANES), F32)
+        for z in range(ZD):
+            first, second = z + 1, z - 1
+            a, a_t = (taps[first], turned[first]) if first < 3 else (none, none)
+            b, b_t = (taps[second], turned[second]) if second >= 0 else (none, none)
+            lanes = slice(ij * LANES, (ij + 1) * LANES)
+            w_mid[z * C2 : z * C2 + 64, lanes] = jnp.where(low, a, b_t).astype(BF16)
+            w_mid[z * C2 + 64 : (z + 1) * C2, lanes] = jnp.where(low, a_t, b).astype(BF16)
+
+    stores[0].start()
+    spread_z(feature[...], z_columns(cells_row[...]), spread)
+    for i in range(3):
+        product = nn(spread[...], w_mid[:, i * 384 : (i + 1) * 384])
+        for j in range(3):
+            parts[i][pl.ds(2 - j, voxels, 4), :] = product[:, j * LANES : (j + 1) * LANES]
+        sums[i][...] = jnp.zeros_like(sums[i])
+
+    def add(v, carry):
+        base = bases[0, v]
+        for i in range(3):
+            spot = pl.ds(base + (2 - i) * PITCH, 3)
+            sums[i][spot, :] = sums[i][spot, :] + parts[i][pl.ds(4 * v, 3), :]
+        return carry
+
+    lax.fori_loop(0, voxels, add, 0, unroll=8)
+
+    def gather(p, carry):
+        spot = pl.ds(pl.multiple_of(p * PITCH + 8, 8), columns)
+        pre[p] = sum0[spot, :] + sum1[spot, :] + sum2[spot, :]
+        return carry
+
+    lax.fori_loop(0, row_count + 5, gather, 0)
+    for store in stores:
+        store.wait()
 
 
 def eighths():
@@ -625,8 +694,16 @@
             shape((16, 256), BF16),
         ),
         in_specs=[smem(), vmem(), vmem(), vmem()],
-        out_specs=(vmem(),) * 9,
+        out_specs=(vmem(),) + (anywhere(),) * 8,
         scratch_shapes=[
+            pltpu.VMEM((512, 1152), BF16),
+            pltpu.VMEM((1536, 256), BF16),
+            pltpu.VMEM((1536, 256), BF16),
+            pltpu.VMEM((1152, 256), BF16),
+            pltpu.VMEM((256, 1536), BF16),
+            pltpu.VMEM((256, 1536), BF16),
+            pltpu.VMEM((256, 3072), BF16),
+            pltpu.VMEM((16, 256), BF16),
             pltpu.VMEM((n * rows + 24, LANES), F32),
             pltpu.VMEM((256, LANES), F32),
             pltpu.VMEM((voxels, ZD * C2), BF16),
@@ -636,11 +713,13 @@
             pltpu.VMEM((cells_all, LANES), F32),
             pltpu.VMEM((cells_all, LANES), F32),
             pltpu.VMEM((cells_all, LANES), F32),
+            pltpu.SemaphoreType.DMA((8,)),
         ],
         compiler_params=pltpu.CompilerParams(vmem_limit_bytes=56 << 20),
     )(bases, cells, feature, wall)
 
 
+NOTE_A, NOTE_B = 72, 40
 PAIRS = 18
 QB = 9
 STEPS = PAIRS // QB
@@ -651,16 +730,20 @@
 
 def conv_kernel(
     n, rows_dev, row_count,
-    bases, cells_row, feature, stat, pre_in, w_mid, f_one, f_two, f_three, d_one, d_two, d_three, head_t,
-    labels_hbm, boxes_hbm,
-    late, early_part, grad_feature, loss_out,
-    grad_a, grad_b, slots, core_in, chip_in,
+    bases, cells_row, feature, stat, pre_in,
+    w_mid_h, f_one_h, f_two_h, f_three_h, d_one_h, d_two_h, d_three_h, head_t_h,
+    labels_hbm, boxes_hbm, points_hbm, counts_ref, small, pooled_in, first_hbm,
+    gradient, loss_out,
+    grad_a, grad_b, slots, core_in, chip_in, far_in, grad_feature,
+    mine_a, mine_b, notes_a, notes_b, fc_rows, small_grad,
+    f_one, f_two, f_three, d_three, head_t, sem_k,
     x_one, x_two, x_three, pre_mid, pre_one, pre_two, back, spread,
     acc0, acc1, acc2,
     labels, boxes, logit_grads, loss_mine, loss_all,
     up_f, down_f, from_up_f, from_down_f, send_up, send_down, from_up, from_down,
     send_up_w, send_down_w, from_up_w, from_down_w,
     sem_t, sem_fs, sem_fr, sem_s, sem_r, sem_ws, sem_wr, sem_ls, sem_lr, sem_cs, sem_cr, sem_zs, sem_zr,
+    sem_gs, sem_gr, sem_p, sem_ns, sem_nar, sem_nbr,
 ):
     me = lax.axis_index("tile")
     edge, split, top, bottom = layout(n, row_count)
@@ -672,14 +755,25 @@
     ]
     for load in loads:
         load.start()
+    kernels = (
+        (f_one_h, f_one), (f_two_h, f_two), (f_three_h, f_three), (head_t_h, head_t),
+        (d_three_h, d_three),
+    )
+    kernel_loads = [pltpu.make_async_copy(a, b, sem_k.at[i]) for i, (a, b) in enumerate(kernels)]
+    for load in kernel_loads:
+        load.start()
     enter(n, me)
 
-    early, late_list = shard_pieces(n, rows_dev)
-    core, side = lax.rem(me, 2), lax.rem(me // 2, 2)
+    pieces = shard_pieces(n, rows_dev)
+    core, side, my_group = lax.rem(me, 2), lax.rem(me // 2, 2), me // 4
     sibling, other = me + 1 - 2 * core, me + 2 - 4 * side
 
+    def collects(piece):
+        nearer = jnp.where(my_group > piece.group, 0, 1)
+        return side == jnp.where(my_group == piece.group, piece.side, nearer)
+
     def core_copy(i):
-        piece = early[i]
+        piece = pieces[i]
         return remote(
             slots.at[2 * piece.chip + 1 - core, piece.rows],
             core_in.at[piece.chip, piece.rows],
@@ -687,43 +781,78 @@
         )
 
     def chip_copy(i):
-        piece = early[i]
+        piece = pieces[i]
         return remote(
             slots.at[2 * piece.chip + core, piece.rows],
-            chip_in.at[piece.group, piece.rows],
+            chip_in.at[piece.chip, piece.rows],
             sem_zs.at[i], sem_zr.at[i], other,
         )
 
+    def far_copy(i, sender):
+        piece = pieces[i]
+        return remote(
+            slots.at[2 * piece.chip + core, piece.rows],
+            far_in.at[sender, piece.rows],
+            sem_gs.at[i], sem_gr.at[5 * sender + piece.order], 2 * piece.chip + core,
+        )
+
+    def of_stage(stage):
+        return [i for i, piece in enumerate(pieces) if piece.stage == stage]
+
     def ship(stage):
-        for i, piece in enumerate(early):
-            if piece.stage == stage:
-                for s in (2 * piece.chip, 2 * piece.chip + 1):
-                    flat_slot(s, rows_dev, piece.row, piece.row + piece.count, grad_a, grad_b, slots.at[s])
-                core_copy(i).start()
+        for i in of_stage(stage):
+            piece = pieces[i]
+            for s in (2 * piece.chip, 2 * piece.chip + 1):
+                flat_slot(s, rows_dev, piece.row, piece.row + piece.count, grad_a, grad_b, slots.at[s])
+            core_copy(i).start()
 
     def ship_on(stage):
-        for i, piece in enumerate(early):
-            if piece.stage == stage:
-                core_copy(i).wait()
-                spot = 2 * piece.chip + core
-                slots[spot, piece.rows, :] = slots[spot, piece.rows, :] + core_in[piece.chip, piece.rows, :]
-
-                @pl.when(side != piece.side)
-                def _(i=i):
-                    chip_copy(i).start()
+        for i in of_stage(stage):
+            piece = pieces[i]
+            core_copy(i).wait()
+            spot = 2 * piece.chip + core
+            slots[spot, piece.rows, :] = slots[spot, piece.rows, :] + core_in[piece.chip, piece.rows, :]
+
+            @pl.when(jnp.logical_not(collects(piece)))
+            def _(i=i):
+                chip_copy(i).start()
+
+    def ship_far(i):
+        piece = pieces[i]
+
+        @pl.when(collects(piece))
+        def _():
+            chip_copy(i).wait_recv()
+            spot = 2 * piece.chip + core
+            slots[spot, piece.rows, :] = slots[spot, piece.rows, :] + chip_in[piece.chip, piece.rows, :]
+
+        @pl.when(collects(piece) & (my_group != piece.group))
+        def _():
+            far_copy(i, my_group).start()
 
     def ship_end():
-        for i, piece in enumerate(early):
-
-            @pl.when(side != piece.side)
+        for i, piece in enumerate(pieces):
+            count = min(piece.count, rows_dev - piece.row)
+            taken = pl.ds(piece.row, count)
+            here = collects(piece)
+
+            @pl.when(here & (my_group == piece.group))
+            def _(i=i, piece=piece, taken=taken):
+                gradient[taken, :] = slots[2 * piece.chip + core, taken, :]
+                for k in range(1, n // 4):
+                    sender = lax.rem(my_group + n // 4 - k, n // 4)
+                    far_copy(i, sender).wait_recv()
+                    gradient[taken, :] = gradient[taken, :] + far_in[sender, taken, :]
+
+            @pl.when(here & (my_group != piece.group))
+            def _(i=i):
+                far_copy(i, my_group).wait_send()
+
+            @pl.when(jnp.logical_not(here))
             def _(i=i):
                 chip_copy(i).wait_send()
 
-            @pl.when(side == piece.side)
-            def _(i=i, piece=piece):
-                chip_copy(i).wait_recv()
-                own = slots[2 * piece.chip + core, piece.rows, :]
-                early_part[piece.group, piece.rows, :] = own + chip_in[piece.group, piece.rows, :]
+    late = of_stage(3)
 
     def ok(place):
         return place_ok(place, edge, split, row_count)
@@ -884,8 +1013,11 @@
         put_edges(x_ref, top_row, bottom_row)
         add_edges(out_ref, nn(top_row, f_ref[0:384, 0:LANES]), nn(bottom_row, f_ref[768:1152, 0:LANES]))
 
+    kernel_loads[0].wait()
     layer_forward(x_one, f_one, bias_row(33, 96), pre_one, 0)
     activate(pre_one, x_two)
+    for load in kernel_loads[1:]:
+        load.wait()
     layer_forward(x_two, f_two, bias_row(35, 96), pre_two, 1)
     activate(pre_two, x_three)
 
@@ -1040,12 +1172,13 @@
             start = B_THREE + 2 * (i * 3 + j) * LANES + part
             grad_b[pl.ds(start, LANES, 2), :] = block
 
-        banded_back(g_three, d_three, back)
         weight_grads(g_three, x_three, 2, write)
         sums = bias_grads(g_three, 2)
         grad_b[B_HEAD - 2 : B_HEAD - 1, :] = sums[:, 0:LANES]
         grad_b[B_HEAD - 1 : B_HEAD, :] = sums[:, LANES : 2 * LANES]
         ship(0)
+        banded_back(g_three, d_three, back)
+        ship_on(0)
         halo_wait(copies)
         add_back(d_three, *edges(2, from_up_w[...], from_down_w[...]))
 
@@ -1063,7 +1196,12 @@
         pltpu.VMEM((20 * LANES, 1536), BF16),
     )
 
-    def lower_layers(g_ref, g_map, win0, win1, win2, gathered):
+    def lower_layers(g_ref, g_map, win0, win1, win2, gathered, d_two, d_one, w_mid):
+        lower = ((d_two_h, d_two), (d_one_h, d_one), (w_mid_h, w_mid))
+        lower_loads = [pltpu.make_async_copy(a, b, sem_k.at[5 + i]) for i, (a, b) in enumerate(lower)]
+        for load in lower_loads:
+            load.start()
+
         def grads_in(pre_ref):
             def step(q, carry):
                 rows = pl.ds(pl.multiple_of(q * LANES, LANES), LANES)
@@ -1091,15 +1229,18 @@
         g_ref[18 * LANES : 20 * LANES, :] = jnp.zeros((2 * LANES, 768), BF16)
         grads_in(pre_two)
         exchange(g_ref, 3)
-        ship_on(0)
-        banded_back(g_ref, d_two, back)
         weights_of(x_two, B_TWO)
         ship(1)
+        for load in lower_loads:
+            load.wait()
+        banded_back(g_ref, d_two, back)
         from_edges(d_two, 3)
+        ship_on(1)
         grads_in(pre_one)
         exchange(g_ref, 4)
-        ship_on(1)
         banded_back(g_ref, d_one, back)
+        for i in of_stage(0):
+            ship_far(i)
         from_edges(d_one, 4)
 
         g_map[...] = jnp.zeros_like(g_map)
@@ -1169,6 +1310,9 @@
                 for t in range(3):
                     start = A_MID + (t * 9 + i * 3 + j) * 64
                     grad_a[start : start + 64, :] = taps[t]
+        ship(3)
+        for i in of_stage(1):
+            ship_far(i)
         z_column = z_columns(cells_row[...])
         total = jnp.zeros((voxels, C2), F32)
         for z in range(ZD):
@@ -1184,11 +1328,184 @@
         pltpu.VMEM((voxels * 4, LANES), F32),
         pltpu.VMEM((voxels * 4, LANES), F32),
         pltpu.VMEM((voxels, 1152), BF16),
+        pltpu.VMEM(d_two_h.shape, BF16),
+        pltpu.VMEM(d_one_h.shape, BF16),
+        pltpu.VMEM(w_mid_h.shape, BF16),
     )
-    for piece in late_list:
-        for s in (2 * piece.chip, 2 * piece.chip + 1):
-            flat_slot(s, rows_dev, piece.row, piece.row + piece.count, grad_a, grad_b, late.at[s])
+    counts = counts_ref[...]
+    slot_count = points_hbm.shape[1]
+    columns, gamma, beta = first_layer(small)
+    mean, scale, held = stat[0:32, 0:1], stat[0:32, 1:2], stat[0:32, 2:3]
+    centre = stat[0:8, 4:5]
+    order = even_first()
+    rows_fc = voxel_rows(small)
+    kernel = rows_fc[0:64, :].astype(BF16)
+    kernel_t = (0.5 * nt(order.astype(BF16), kernel)).astype(BF16)
+    kernel = nt(kernel, order.astype(BF16)).astype(BF16)
+    bias = 0.5 * jnp.sum(jnp.where(order, rows_fc[64:65, :], 0.0), axis=1, keepdims=True)
+    half_gamma, half_beta = 0.5 * gamma, 0.5 * beta
+
+
+    def halves(value):
+        high = value.astype(BF16)
+        return high, (value - high.astype(F32)).astype(BF16)
+
+    def note(ref, notes, sender, s, received):
+        return remote(ref, notes.at[sender], sem_ns.at[s], received.at[sender], 0)
+
+    def send_note(s):
+        @pl.when(me > 0)
+        def _():
+            (note(mine_a, notes_a, me, 0, sem_nar) if s == 0 else note(mine_b, notes_b, me, 1, sem_nbr)).start()
+
+    chunks = voxels // CHUNK
+
+    def after(step):
+        last = 3 * chunks - 1
+        for place, i in enumerate(late):
+            if min(place + 1, last) == step:
+                ship_far(i)
+
+    def voxel_layers(points, first, inner_grads, first_out):
+        first_load = pltpu.make_async_copy(first_hbm, first_out, sem_p.at[7])
+        first_load.start()
+        points[...] = jnp.ones_like(points)
+        point_loads = [
+            pltpu.make_async_copy(points_hbm.at[k], points.at[:, k, :], sem_p.at[k]) for k in range(7)
+        ]
+        for load in point_loads:
+            load.start()
+        ship_on(3)
+        first_load.wait()
+        tail = jnp.where(row_of((16, CHUNK)) == 0, 1.0, 0.0).astype(BF16)
+        fc = jnp.zeros((80, LANES), F32)
+        pooled_grads = []
+        for c in range(chunks):
+            part = slice(c * CHUNK, (c + 1) * CHUNK)
+            held_c = counts[:, part]
+            counts_f = held_c.astype(F32)
+            grad_pre = (0.5 * jnp.transpose(grad_feature[part, :])) / counts_f
+            pooled_c = pooled_in[:, part]
+            fixed = nn(kernel_t[:, 32:64], pooled_c) + bias
+
+            def spot(p):
+                return pl.ds(pl.multiple_of(p * CHUNK, LANES), CHUNK)
+
+            def pass_e(p, carry, part=part, held_c=held_c, grad_pre=grad_pre, fixed=fixed):
+                half_inner = nn(kernel_t[:, 0:32], first_out[p, :, part]) + fixed
+                grad = jnp.where(p < held_c, grad_pre * half_slope(half_inner), 0.0)
+                inner_grads[:, spot(p)] = grad.astype(BF16)
+                return carry
+
+            lax.fori_loop(0, slot_count, pass_e, 0, unroll=7)
+            if c == 0:
+                for i in of_stage(2):
+                    ship_far(i)
+            else:
+                after(2 * c)
+
+            def pass_g(p, carry, c=c, part=part, pooled_c=pooled_c):
+                fc, pooled = carry
+                grad = inner_grads[:, spot(p)]
+                fc += nt(jnp.concatenate([first_out[p, :, part], pooled_c, tail], axis=0), grad)
+                down = nn(kernel, grad)
+                first[c, p] = down[0:32]
+                return fc, pooled + down[32:64]
+
+            fc, pooled = lax.fori_loop(0, slot_count, pass_g, (fc, jnp.zeros((32, CHUNK), F32)), unroll=5)
+            pooled_grads.append(pooled / counts_f)
+            after(2 * c + 1)
+        mine_a[...] = fc[0:NOTE_A]
+        send_note(0)
+        for load in point_loads:
+            load.wait()
+        moments, g_gamma, centred = jnp.zeros((LANES, 16), F32), jnp.zeros((32, CHUNK), F32), jnp.zeros((8, CHUNK), F32)
+        for c in range(chunks):
+            part = slice(c * CHUNK, (c + 1) * CHUNK)
+            wide = [jnp.broadcast_to(column, (32, CHUNK)) for column in columns]
+
+            def pass_f(p, carry, c=c, part=part, held_c=counts[:, part], pooled=pooled_grads[c], wide=wide):
+                moments, g_gamma, centred = carry
+                inside = p < held_c
+                value = wide[0] * points[p, 0:1, part]
+                for k in range(1, 7):
+                    value += wide[k] * points[p, k : k + 1, part]
+                normed = jnp.where(inside, (value - mean) * scale, 0.0)
+                slopes = half_slope(half_gamma * normed + half_beta)
+                grad = jnp.where(inside, (0.5 * (first[c, p] + pooled)) * slopes, 0.0)
+                off = points[p, :, part] - centre
+                off_high, off_low = halves(off)
+                grad_high, grad_low = halves(grad)
+                norm_high, norm_low = halves(normed)
+                left = jnp.concatenate([grad_high, grad_low, norm_high, norm_low], axis=0)
+                right = jnp.concatenate([off_high, off_low], axis=0)
+                return (
+                    moments + nt(left, right),
+                    g_gamma + grad * normed,
+                    centred + jnp.where(inside, off, 0.0),
+                )
+
+            moments, g_gamma, centred = lax.fori_loop(0, slot_count, pass_f, (moments, g_gamma, centred), unroll=5)
+            after(2 * chunks + c)
+        by_grad = moments[0:32] + moments[32:64]
+        by_norm = moments[64:96] + moments[96:128]
+        mine_b[...] = jnp.zeros_like(mine_b)
+        mine_b[0:32, 0:8] = by_grad[:, 0:8] + by_grad[:, 8:16]
+        mine_b[0:32, 8:16] = by_norm[:, 0:8] + by_norm[:, 8:16]
+        mine_b[0:32, 16:17] = jnp.sum(g_gamma, axis=1, keepdims=True)
+        mine_b[32:40, 0:1] = jnp.sum(centred, axis=1, keepdims=True)
+        send_note(1)
+
+    pl.run_scoped(
+        voxel_layers,
+        pltpu.VMEM((slot_count, 8, voxels), F32),
+        pltpu.VMEM((chunks, slot_count, 32, CHUNK), F32),
+        pltpu.VMEM((LANES, slot_count * CHUNK), BF16),
+        pltpu.VMEM(first_hbm.shape, BF16),
+    )
+    small_grad[...] = jnp.zeros_like(small_grad)
+
+    @pl.when(me == 0)
+    def _():
+        notes_a[0] = mine_a[...]
+        notes_b[0] = mine_b[...]
+        for d in range(1, n):
+            note(mine_a, notes_a, d, 0, sem_nar).wait_recv()
+        fc_total = notes_a[0]
+        for d in range(1, n):
+            fc_total += notes_a[d]
+        fc_rows[...] = jnp.zeros_like(fc_rows)
+        fc_rows[8:80, :] = nn(fc_total, order.astype(F32), HIGH)
+        here, before = fc_rows[8:80, :], fc_rows[7:79, :]
+        mixed = jnp.where(lane_of((72, LANES)) >= LANES - FC_LANE, before, here)
+        small_grad[2:74, :] = pltpu.roll(mixed, FC_LANE, axis=1)
+        for d in range(1, n):
+            note(mine_b, notes_b, d, 1, sem_nbr).wait_recv()
+        total = notes_b[0]
+        for d in range(1, n):
+            total += notes_b[d]
+        by_grad, by_norm = total[0:32, 0:8], total[0:32, 8:16]
+        g_gamma, g_beta = total[0:32, 16:17], total[0:32, 7:8]
+        off_sums = jnp.transpose(jnp.broadcast_to(total[32:40, 0:1], (8, LANES)))[0:32, 0:8]
+        g_vfe = scale * gamma * (
+            by_grad - g_beta / held * off_sums - g_gamma / held * by_norm
+        )
+        tall0 = jnp.concatenate([g_vfe[:, k : k + 1] for k in range(4)], axis=0)
+        tall1 = jnp.concatenate([g_vfe[:, 4:5], g_vfe[:, 5:6], g_vfe[:, 6:7], g_gamma], axis=0)
+        tall2 = jnp.concatenate([g_beta, jnp.zeros((96, 1), F32)], axis=0)
+        lane = lane_of((LANES, LANES))
+        tall = jnp.where(lane == 0, tall0, 0.0) + jnp.where(lane == 1, tall1, 0.0) + jnp.where(lane == 2, tall2, 0.0)
+        head = jnp.transpose(tall)[0:8]
+        small_grad[0:8, :] = small_grad[0:8, :] + head
+
     ship_end()
+    gradient[0:SMALL, :] = gradient[0:SMALL, :] + small_grad[...]
+
+    @pl.when(me > 0)
+    def _():
+        note(mine_a, notes_a, me, 0, sem_nar).wait_send()
+        note(mine_b, notes_b, me, 1, sem_nbr).wait_send()
+
     for k in range(1, n):
         sender = lax.rem(me + n - k, n)
         remote(loss_mine, loss_all.at[sender], sem_ls.at[k], sem_lr.at[sender], sender).wait_recv()
@@ -1201,31 +1518,39 @@
         loss_copy(k).wait_send()
 
 
-def convs(n, rows_dev, row_count, bases, cells, feature, stat, middle_out, labels, boxes):
+def train(n, rows_dev, row_count, bases, cells, feature, stat, middle_out, labels, boxes, points, counts, small, pooled, first_out):
     shape = jax.ShapeDtypeStruct
     dma = pltpu.SemaphoreType.DMA
     voxels = feature.shape[0]
     row = (LANES, LANES)
     padded = ceil_to(rows_dev, 8)
-    early = len(shard_pieces(n, rows_dev)[0])
-    late = 2 * late_chips(n, rows_dev)
+    pieces = len(shard_pieces(n, rows_dev))
+    fours = n // 4
     return pl.pallas_call(
         functools.partial(conv_kernel, n, rows_dev, row_count),
-        name="convs",
+        name="train",
         out_shape=(
-            shape((late, padded, LANES), F32),
-            shape((n // 4, padded, LANES), F32),
-            shape((voxels, LANES), F32),
+            shape((rows_dev, LANES), F32),
             shape((8, LANES), F32),
         ),
-        in_specs=[smem()] + [vmem()] * 12 + [anywhere()] * 2,
-        out_specs=(vmem(),) * 4,
+        in_specs=[smem()] + [vmem()] * 4 + [anywhere()] * 11 + [vmem()] * 3 + [anywhere()],
+        out_specs=(vmem(),) * 2,
         scratch_shapes=[
             pltpu.VMEM((A_ROWS, LANES), F32),
             pltpu.VMEM((B_ROWS, LANES), F32),
             pltpu.VMEM((n, padded, LANES), F32),
             pltpu.VMEM((n // 2, padded, LANES), F32),
-            pltpu.VMEM((n // 4, padded, LANES), F32),
+            pltpu.VMEM((n // 2, padded, LANES), F32),
+            pltpu.VMEM((fours, padded, LANES), F32),
+            pltpu.VMEM((voxels, LANES), F32),
+            pltpu.VMEM((NOTE_A, LANES), F32),
+            pltpu.VMEM((NOTE_B, LANES), F32),
+            pltpu.VMEM((n, NOTE_A, LANES), F32),
+            pltpu.VMEM((n, NOTE_B, LANES), F32),
+            pltpu.VMEM((88, LANES), F32),
+            pltpu.VMEM((SMALL, LANES), F32),
+            *[pltpu.VMEM(middle_out[a].shape, BF16) for a in (2, 3, 4, 7, 8)],
+            dma((8,)),
             pltpu.VMEM((20 * LANES, 768), BF16),
             pltpu.VMEM((20 * LANES, 768), BF16),
             pltpu.VMEM((20 * LANES, 768), BF16),
@@ -1255,12 +1580,13 @@
             pltpu.VMEM((LANES, 256), BF16),
             pltpu.VMEM((LANES, 256), BF16),
             dma((16,)), dma((2,)), dma((2,)), dma((12,)), dma((12,)), dma((2,)), dma((2,)), dma((n,)), dma((n,)),
-            dma((early,)), dma((early,)), dma((early,)), dma((early,)),
+            dma((pieces,)), dma((pieces,)), dma((pieces,)), dma((pieces,)),
+            dma((pieces,)), dma((5 * fours,)), dma((8,)), dma((2,)), dma((n,)), dma((n,)),
         ],
         compiler_params=pltpu.CompilerParams(
-            collective_id=2, has_side_effects=True, vmem_limit_bytes=62 << 20
+            collective_id=2, has_side_effects=True, vmem_limit_bytes=63 << 20
         ),
-    )(bases, cells, feature, stat, *middle_out, labels, boxes)
+    )(bases, cells, feature, stat, *middle_out, labels, boxes, points, counts, small, pooled, first_out)
 
 
 def adam_outer(gradient, weight, moment, second, momentum):
@@ -1277,304 +1603,62 @@
     return (moment, second, momentum, updated)
 
 
-NOTE_A, NOTE_B = 72, 40
-
-
-def finish_kernel(
-    n, rows, points_hbm, points_in, counts_ref, small, stat, first_out, pooled_in, grad_feature, late, early_part,
-    gradient,
-    points, first, inner_grads, core_in, chip_in, parts, far_in, mine_a, mine_b, notes_a, notes_b, fc_rows, small_grad,
-    sem_p, sem_cs, sem_cr, sem_zs, sem_zr, sem_fs, sem_fr, sem_ns, sem_nar, sem_nbr,
-):
-    me = lax.axis_index("tile")
-    early_list, late_list = shard_pieces(n, rows)
-    core, side, my_group = lax.rem(me, 2), lax.rem(me // 2, 2), me // 4
-    sibling, other = me + 1 - 2 * core, me + 2 - 4 * side
-    count_p, voxels = points_hbm.shape[1], points_hbm.shape[2]
-    points[...] = jnp.ones_like(points)
-    loads = [
-        pltpu.make_async_copy(points_hbm.at[k], points.at[:, k, :], sem_p.at[k]) for k in range(7)
-    ]
-    for load in loads:
-        load.start()
-    enter(n, me)
-
-    def core_copy(i):
-        piece = late_list[i]
-        return remote(
-            late.at[2 * piece.chip + 1 - core, piece.rows],
-            core_in.at[piece.chip, piece.rows],
-            sem_cs.at[i], sem_cr.at[i], sibling,
-        )
-
-    def chip_copy(i):
-        piece = late_list[i]
-        return remote(
-            core_in.at[piece.chip, piece.rows],
-            chip_in.at[piece.group, piece.rows],
-            sem_zs.at[i], sem_zr.at[i], other,
-        )
-
-    def far_copy(source, piece, sender, send):
-        owner = 4 * piece.group + 2 * side + core
-        received = sem_fr.at[3 * sender + piece.order]
-        return remote(source.at[piece.group, piece.rows], far_in.at[sender, piece.rows], send, received, owner)
-
-    def far_start(source, piece, i):
-        @pl.when((side == piece.side) & (my_group != piece.group))
-        def _():
-            far_copy(source, piece, my_group, sem_fs.at[i]).start()
-
-    for i in range(len(late_list)):
-        core_copy(i).start()
-    late_count = len(late_list)
-    for i, piece in enumerate(early_list):
-        far_start(early_part, piece, late_count + i)
-
-    counts = counts_ref[...]
-    columns, gamma, beta = first_layer(small)
-    mean, scale, held = stat[0:32, 0:1], stat[0:32, 1:2], stat[0:32, 2:3]
-    centre = stat[0:8, 4:5]
-    order = even_first()
-    rows_fc = voxel_rows(small)
-    kernel = rows_fc[0:64, :].astype(BF16)
-    kernel_t = (0.5 * nt(order.astype(BF16), kernel)).astype(BF16)
-    kernel = nt(kernel, order.astype(BF16)).astype(BF16)
-    bias = 0.5 * jnp.sum(jnp.where(order, rows_fc[64:65, :], 0.0), axis=1, keepdims=True)
-    half_gamma, half_beta = 0.5 * gamma, 0.5 * beta
-
-    def sums_of_cores():
-        for i, piece in enumerate(late_list):
-            core_copy(i).wait()
-            core_in[piece.chip, piece.rows, :] = (
-                core_in[piece.chip, piece.rows, :] + late[2 * piece.chip + core, piece.rows, :]
-            )
-
-            @pl.when(side != piece.side)
-            def _(i=i):
-                chip_copy(i).start()
-
-    def sums_of_chips(i):
-        piece = late_list[i]
-
-        @pl.when(side == piece.side)
-        def _():
-            chip_copy(i).wait_recv()
-            own = core_in[piece.chip, piece.rows, :]
-            parts[piece.group, piece.rows, :] = own + chip_in[piece.group, piece.rows, :]
-
-        far_start(parts, piece, i)
-
-    def halves(value):
-        high = value.astype(BF16)
-        return high, (value - high.astype(F32)).astype(BF16)
-
-    def note(ref, notes, sender, s, received):
-        return remote(ref, notes.at[sender], sem_ns.at[s], received.at[sender], 0)
-
-    def send_note(s):
-        @pl.when(me > 0)
-        def _():
-            (note(mine_a, notes_a, me, 0, sem_nar) if s == 0 else note(mine_b, notes_b, me, 1, sem_nbr)).start()
-
-    tail = jnp.where(row_of((16, CHUNK)) == 0, 1.0, 0.0).astype(BF16)
-    fc = jnp.zeros((80, LANES), F32)
-    moments, g_gamma, centred = jnp.zeros((LANES, 16), F32), jnp.zeros((32, CHUNK), F32), jnp.zeros((8, CHUNK), F32)
-    chunks = voxels // CHUNK
-    for c in range(chunks):
-        part = slice(c * CHUNK, (c + 1) * CHUNK)
-        held_c = counts[:, part]
-        counts_f = held_c.astype(F32)
-        grad_pre = (0.5 * jnp.transpose(grad_feature[part, :])) / counts_f
-        pooled_c = pooled_in[:, part]
-        fixed = nn(kernel_t[:, 32:64], pooled_c) + bias
-
-        def spot(p):
-            return pl.ds(pl.multiple_of(p * CHUNK, LANES), CHUNK)
-
-        def pass_e(p, carry, part=part, held_c=held_c, grad_pre=grad_pre, fixed=fixed):
-            half_inner = nn(kernel_t[:, 0:32], first_out[p, :, part]) + fixed
-            grad = jnp.where(p < held_c, grad_pre * half_slope(half_inner), 0.0)
-            inner_grads[:, spot(p)] = grad.astype(BF16)
-            return carry
-
-        lax.fori_loop(0, count_p, pass_e, 0, unroll=7)
-        if c == 0:
-            sums_of_cores()
-
-        def pass_g(p, carry, part=part, pooled_c=pooled_c):
-            fc, pooled = carry
-            grad = inner_grads[:, spot(p)]
-            fc += nt(jnp.concatenate([first_out[p, :, part], pooled_c, tail], axis=0), grad)
-            down = nn(kernel, grad)
-            first[p] = down[0:32]
-            return fc, pooled + down[32:64]
-
-        fc, pooled = lax.fori_loop(0, count_p, pass_g, (fc, jnp.zeros((32, CHUNK), F32)), unroll=5)
-        if c == 0:
-            for load in loads:
-                load.wait()
-            sums_of_chips(0)
-        if c == chunks - 1:
-            mine_a[...] = fc[0:NOTE_A]
-            send_note(0)
-            for i in range(2 if chunks > 1 else 1, late_count):
-                sums_of_chips(i)
-        pooled = pooled / counts_f
-        wide = [jnp.broadcast_to(column, (32, CHUNK)) for column in columns]
-        view = points_in.at[:, :, part]
-
-        def pass_f(p, carry, part=part, held_c=held_c, pooled=pooled, wide=wide, view=view):
-            moments, g_gamma, centred = carry
-            inside = p < held_c
-            normed = jnp.where(inside, (linear_row(wide, view, p) - mean) * scale, 0.0)
-            slopes = half_slope(half_gamma * normed + half_beta)
-            grad = jnp.where(inside, (0.5 * (first[p] + pooled)) * slopes, 0.0)
-            off = points[p, :, part] - centre
-            off_high, off_low = halves(off)
-            grad_high, grad_low = halves(grad)
-            norm_high, norm_low = halves(normed)
-            left = jnp.concatenate([grad_high, grad_low, norm_high, norm_low], axis=0)
-            right = jnp.concatenate([off_high, off_low], axis=0)
-            return (
-                moments + nt(left, right),
-                g_gamma + grad * normed,
-                centred + jnp.where(inside, off, 0.0),
-            )
-
-        moments, g_gamma, centred = lax.fori_loop(0, count_p, pass_f, (moments, g_gamma, centred), unroll=5)
-        if c == 0 and chunks > 1 and late_count > 1:
-            sums_of_chips(1)
-    by_grad = moments[0:32] + moments[32:64]
-    by_grad = by_grad[:, 0:8] + by_grad[:, 8:16]
-    by_norm = moments[64:96] + moments[96:128]
-    by_norm = by_norm[:, 0:8] + by_norm[:, 8:16]
-    mine_b[...] = jnp.zeros_like(mine_b)
-    mine_b[0:32, 0:8] = by_grad
-    mine_b[0:32, 8:16] = by_norm
-    mine_b[0:32, 16:17] = jnp.sum(g_gamma, axis=1, keepdims=True)
-    mine_b[32:40, 0:1] = jnp.sum(centred, axis=1, keepdims=True)
-    send_note(1)
-    small_grad[...] = jnp.zeros_like(small_grad)
-
-    @pl.when(me == 0)
-    def _():
-        notes_a[0] = mine_a[...]
-        notes_b[0] = mine_b[...]
-        for d in range(1, n):
-            note(mine_a, notes_a, d, 0, sem_nar).wait_recv()
-            note(mine_b, notes_b, d, 1, sem_nbr).wait_recv()
-        fc_total, total = notes_a[0], notes_b[0]
-        for d in range(1, n):
-            fc_total += notes_a[d]
-            total += notes_b[d]
-        by_grad, by_norm = total[0:32, 0:8], total[0:32, 8:16]
-        g_gamma, g_beta = total[0:32, 16:17], total[0:32, 7:8]
-        off_sums = jnp.transpose(jnp.broadcast_to(total[32:40, 0:1], (8, LANES)))[0:32, 0:8]
-        g_vfe = scale * gamma * (
-            by_grad - g_beta / held * off_sums - g_gamma / held * by_norm
-        )
-        tall0 = jnp.concatenate([g_vfe[:, k : k + 1] for k in range(4)], axis=0)
-        tall1 = jnp.concatenate([g_vfe[:, 4:5], g_vfe[:, 5:6], g_vfe[:, 6:7], g_gamma], axis=0)
-        tall2 = jnp.concatenate([g_beta, jnp.zeros((96, 1), F32)], axis=0)
-        lane = lane_of((LANES, LANES))
-        tall = jnp.where(lane == 0, tall0, 0.0) + jnp.where(lane == 1, tall1, 0.0) + jnp.where(lane == 2, tall2, 0.0)
-        head = jnp.transpose(tall)[0:8]
-        fc_rows[...] = jnp.zeros_like(fc_rows)
-        fc_rows[8:80, :] = nn(fc_total, order.astype(F32), HIGH)
-        here, before = fc_rows[8:80, :], fc_rows[7:79, :]
-        mixed = jnp.where(lane_of((72, LANES)) >= LANES - FC_LANE, before, here)
-        small_grad[2:74, :] = pltpu.roll(mixed, FC_LANE, axis=1)
-        small_grad[0:8, :] = small_grad[0:8, :] + head
-
-    for i, piece in enumerate(late_list + early_list):
-        source = parts if i < late_count else early_part
-        count = min(piece.count, rows - piece.row)
-        taken = pl.ds(piece.row, count)
-        here = side == piece.side
-
-        @pl.when(here & (my_group == piece.group))
-        def _(source=source, piece=piece, taken=taken):
-            gradient[taken, :] = source[piece.group, taken, :]
-            for k in range(1, n // 4):
-                sender = lax.rem(my_group + n // 4 - k, n // 4)
-                far_copy(source, piece, sender, sem_fs.at[0]).wait_recv()
-                gradient[taken, :] = gradient[taken, :] + far_in[sender, taken, :]
-
-        @pl.when(here & (my_group != piece.group))
-        def _(source=source, piece=piece, i=i):
-            far_copy(source, piece, my_group, sem_fs.at[i]).wait_send()
-
-        if i < late_count:
-
-            @pl.when(side != piece.side)
-            def _(i=i):
-                chip_copy(i).wait_send()
-
-    gradient[0:SMALL, :] = gradient[0:SMALL, :] + small_grad[...]
-
-    @pl.when(me > 0)
-    def _():
-        note(mine_a, notes_a, me, 0, sem_nar).wait_send()
-        note(mine_b, notes_b, me, 1, sem_nbr).wait_send()
-
-
-def finish(n, rows, points, counts, small, stat, first_out, pooled, grad_feature, late, early_part):
-    shape = jax.ShapeDtypeStruct
-    dma = pltpu.SemaphoreType.DMA
-    slots, voxels = points.shape[1:]
-    padded = ceil_to(rows, 8)
-    fours = n // 4
-    chips, count = late.shape[0] // 2, len(shard_pieces(n, rows)[1])
-    everything = count + len(shard_pieces(n, rows)[0])
-    return pl.pallas_call(
-        functools.partial(finish_kernel, n, rows),
-        name="finish",
-        out_shape=shape((rows, LANES), F32),
-        in_specs=[anywhere()] + [vmem()] * 9,
-        out_specs=vmem(),
-        scratch_shapes=[
-            pltpu.VMEM((slots, 8, voxels), F32),
-            pltpu.VMEM((slots, 32, CHUNK), F32),
-            pltpu.VMEM((LANES, slots * CHUNK), BF16),
-            pltpu.VMEM((chips, padded, LANES), F32),
-            pltpu.VMEM((fours, padded, LANES), F32),
-            pltpu.VMEM((fours, padded, LANES), F32),
-            pltpu.VMEM((fours, padded, LANES), F32),
-            pltpu.VMEM((NOTE_A, LANES), F32),
-            pltpu.VMEM((NOTE_B, LANES), F32),
-            pltpu.VMEM((n, NOTE_A, LANES), F32),
-            pltpu.VMEM((n, NOTE_B, LANES), F32),
-            pltpu.VMEM((88, LANES), F32),
-            pltpu.VMEM((SMALL, LANES), F32),
-            dma((7,)), dma((count,)), dma((count,)), dma((count,)), dma((count,)),
-            dma((everything,)), dma((3 * fours,)), dma((2,)), dma((n,)), dma((n,)),
-        ],
-        compiler_params=pltpu.CompilerParams(
-            collective_id=3, has_side_effects=True, vmem_limit_bytes=58 << 20
-        ),
-    )(points, points, counts, small, stat, first_out, pooled, grad_feature, late, early_part)
-
-
 def update_kernel(
     gradient, weight, moment, second, momentum, loss, stat,
     moment_out, second_out, momentum_out, weight_out, loss_out, positives_out,
+    grad, held, outs, sem_in, sem_out,
 ):
-    outs = adam_outer(gradient[...], weight[...], moment[...], second[...], momentum[...])
-    moment_out[...], second_out[...], momentum_out[...], weight_out[...] = outs
+    sources = (weight, moment, second, momentum)
+    targets = (moment_out, second_out, momentum_out, weight_out)
+    rows = grad.shape[0]
+    steps = 4
+    marks = [s * rows // steps // 8 * 8 for s in range(steps)] + [rows]
+    loads, stores = [], []
+    for s in range(steps):
+        window = pl.ds(marks[s], marks[s + 1] - marks[s])
+        loads.append([
+            pltpu.make_async_copy(source.at[window], target.at[window], sem_in.at[5 * s + a])
+            for a, (source, target) in enumerate(
+                [(gradient, grad)] + [(source, held.at[a]) for a, source in enumerate(sources)]
+            )
+        ])
+        for load in loads[-1]:
+            load.start()
     loss_out[0] = loss[0, 0]
     positives_out[0] = stat[0, 3]
+    for s in range(steps):
+        part = slice(marks[s], marks[s + 1])
+        window = pl.ds(marks[s], marks[s + 1] - marks[s])
+        for load in loads[s]:
+            load.wait()
+        values = adam_outer(grad[part, :], held[0, part, :], held[1, part, :], held[2, part, :], held[3, part, :])
+        for a, value in enumerate(values):
+            outs[a, part, :] = value
+            store = pltpu.make_async_copy(outs.at[a, window], targets[a].at[window], sem_out.at[4 * s + a])
+            store.start()
+            stores.append(store)
+    for store in stores:
+        store.wait()
 
 
 def update(gradient, held, loss, stat):
     shape = jax.ShapeDtypeStruct
+    rows = gradient.shape[0]
+    dma = pltpu.SemaphoreType.DMA
     return pl.pallas_call(
         update_kernel,
         name="update",
         out_shape=(shape(gradient.shape, F32),) * 4 + (shape((1,), F32),) * 2,
-        in_specs=[vmem()] * 7,
-        out_specs=(vmem(),) * 4 + (smem(),) * 2,
-        compiler_params=pltpu.CompilerParams(vmem_limit_bytes=32 << 20),
+        in_specs=[anywhere()] * 5 + [vmem()] * 2,
+        out_specs=(anywhere(),) * 4 + (smem(),) * 2,
+        scratch_shapes=[
+            pltpu.VMEM((rows, LANES), F32),
+            pltpu.VMEM((4, rows, LANES), F32),
+            pltpu.VMEM((4, rows, LANES), F32),
+            dma((20,)),
+            dma((16,)),
+        ],
+        compiler_params=pltpu.CompilerParams(vmem_limit_bytes=60 << 20),
     )(gradient, *held, loss, stat)
 
 
@@ -1591,11 +1675,9 @@
         n, points, counts, cells, anchor_labels, held[0]
     )
     ready = middle(n, rows, row_count, bases, cells, feature, wall)
-    late, early_part, grad_feature, loss = convs(
-        n, rows, row_count, bases, cells, feature, stat, ready, anchor_labels, box_targets
-    )
-    gradient = finish(
-        n, rows, points, counts, small, stat, first_out, pooled, grad_feature, late, early_part
+    gradient, loss = train(
+        n, rows, row_count, bases, cells, feature, stat, ready, anchor_labels, box_targets,
+        points, counts, small, pooled, first_out,
     )
     *outs, loss_sum, positives = update(gradient, held, loss, stat)
     moment, second, momentum, updated = [x.reshape(weights.shape) for x in outs]

time: 150 us -> 140 us (0.933)
  Pallas kernels: 147 us -> 139 us
    pallas_call x2 -> x1, Pallas kernels: 109 us -> 93.6 us  [train(): pl.pallas_call(functools.partial(conv_kernel, n, rows_dev, row_count), na...]
    pallas_call x1, Pallas kernels: 27.1 us -> 32.5 us  [front(): pl.pallas_call(functools.partial(front_kernel, n), name='front', out_shap...]
    pallas_call x1, Pallas kernels: 1.66 us -> 4 us  [update(): pl.pallas_call(update_kernel, name='update', out_shape=(shape(gradient.sh...]
where the time goes in v4:
time: 140 us
  Pallas kernels  139 us (99%)
    pallas_call x1, Pallas kernels, train(): pl.pallas_call(functools.partial(conv_kernel, n, rows_dev, row_count), na...  93.6 us
    pallas_call x1, Pallas kernels, front(): pl.pallas_call(functools.partial(front_kernel, n), name='front', out_shap...  32.5 us
    pallas_call x1, Pallas kernels, middle(): pl.pallas_call(functools.partial(middle_kernel, n, rows, row_count), name...  8.91 us
    pallas_call x1, Pallas kernels, update(): pl.pallas_call(update_kernel, name='update', out_shape=(shape(gradient.sh...  4 us

profile of v4, /device:TPU:0, one launch (start us, length us, event | category | flops | bytes accessed | tf_op | source)
XLA Modules:
  0.0 139.9 jit_solution(6027435290740482557)
XLA Ops:
  0.6 32.5 %front.1 = (bf16[8,816,128]{2,1,0:T(8,128)(2,1)}, f32[80,128]{1,0:T(8,128)}, f32[48,128]{1,0:T(8,128)}, bf16[35,32,512]{2,1,0:T(8,128)(2,1)}, bf16[32,512]{1,0:T...) custom-call(f32[7,35,512]{2,1,0:T(8,128)} %points_hbm.1, s32[1,512]{1,0:T(1,128)} %bitcast.18, s32[1,512]{1,0:T(1,128)} %bitcast.15, ...), custom_call_target="tpu_custom_call" | custom-call | tf_op jit(solution)/shard_map/front/pallas_call | solution.py:457
  33.2 8.9 %middle.1 = (f32[37,128,128]{2,1,0:T(8,128)}, bf16[512,1152]{1,0:T(8,128)(2,1)}, bf16[1536,256]{1,0:T(8,128)(2,1)}, bf16[1536,256]{1,0:T(8,128)(2,1)}, bf16[1152...) custom-call(s32[1,512]{1,0:T(1,128)} %get-tuple-element.30.bases, ...), custom_call_target="tpu_custom_call" | custom-call | tf_op jit(solution)/shard_map/middle/pallas_call | solution.py:682
  42.1 93.6 %train.1 = (f32[805,128]{1,0:T(8,128)}, f32[8,128]{1,0:T(8,128)}) custom-call(s32[1,512]{1,0:T(1,128)} %get-tuple-element.30.bases, s32[1,512]{1,0:T(1,128)} %bitcast.17, f32[512,128]{1,0:T(8,128)} %get-tuple-element.31.feature, f32[48,128]{1,0:T(8,128)} %get-tuple-element.32.stat, f32[37,128,128]{2,1,0:T(8,128)} %get-tuple-element.34.pre_in, ...), custom_call_target="tpu_custom_call" | custom-call | tf_op jit(solution)/shard_map/train/pallas_call | solution.py:1529
  135.7 4.0 %update.1 = (f32[805,128]{1,0:T(8,128)}, f32[805,128]{1,0:T(8,128)}, f32[805,128]{1,0:T(8,128)}, f32[805,128]{1,0:T(8,128)}, f32[1]{0:T(128)}, /*index=5*/f32[1]{0:T(128)}) custom-call(f32[805,128]{1,0:T(8,128)} %get-tuple-element.46.gradient, f32[805,128]{1,0:T(8,128)} %bitcast.11, f32[805,128]{1,0:T(8,128)} %bitcast.12, f32[805,128]{1,0:T(8,128)} %bitcast.13, ...), custom_call_target="tpu_custom_call" | custom-call | tf_op jit(solution)/shard_map/update/pallas_call | solution.py:1648

commit v5 on v4

--- a/solution.py
+++ b/solution.py
@@ -326,7 +326,7 @@
         return remote(wall.at[source], wall.at[source], sem.at[k], sem_w_r.at[source], peer)
 
     def relay(step):
-        if n == 8 and step < 2:
+        if n == 8:
 
             @pl.when(inner)
             def _():
@@ -381,6 +381,8 @@
         pooled = (pooled / held_c.astype(F32)).astype(BF16)
         pooled_out[:, part] = pooled
         fixed = nn(kernel_t[:, 32:64], pooled) + bias
+        if c < 2:
+            relay(c)
 
         def pass_d(p, total, fixed=fixed, held_c=held_c, part=part):
             half_inner = nn(kernel_t[:, 0:32], first_out[p, :, part]) + fixed
@@ -388,7 +390,6 @@
 
         total = lax.fori_loop(0, slots, pass_d, jnp.zeros((LANES, CHUNK), F32), unroll=7)
         feature[part, :] = jnp.transpose(total / held_c.astype(F32))
-        relay(c)
 
     for step in range(voxels // CHUNK, 2):
         relay(step)
@@ -937,13 +938,13 @@
     halo_start(copies)
     for ref, wide in ((x_one, 768), (x_two, 768), (x_three, 768)):
         ref[0:LANES, 0:384] = jnp.zeros((LANES, 384), BF16)
-        ref[18 * LANES : 20 * LANES, :] = jnp.zeros((2 * LANES, wide), BF16)
+        ref[18 * LANES : 19 * LANES, :] = jnp.zeros((LANES, wide), BF16)
     spread_z(feature[...], z_columns(cells_row[...]), spread)
     bias_mid = stat[32:33, :]
     b_mid = jnp.concatenate([bias_mid[:, 32:96], bias_mid[:, 32:96]], axis=1)
 
     def activated(value, x_ref, q, e):
-        value = pick(ok(2 * q + 1 + e), value * sigmoid(value), 0.0)
+        value = pick(ok(2 * q + 1 + e), half_silu(0.5 * value), 0.0)
         put(x_ref, q + e, 1 - e, value, 0, 1)
 
     def mid_step(q, carry):
@@ -962,29 +963,10 @@
     for q, e in ((0, 0), (15, 1), (16, 0)):
         activated(pre_mid[q * LANES : (q + 1) * LANES, e * LANES : (e + 1) * LANES], x_one, q, e)
 
-    def activate(pre_ref, x_ref):
-        def step(q, carry):
-            rows = pl.ds(pl.multiple_of(q * LANES, LANES), LANES)
-            for e in range(2):
-                activated(pre_ref[rows, e * LANES : (e + 1) * LANES], x_ref, q, e)
-            return carry
-
-        lax.fori_loop(0, PAIRS, step, 0)
-
     def exchange(x_ref, s):
         send_up[s] = x_ref[0:LANES, 512:640]
         send_down[s] = pick(split == 1, x_ref[16 * LANES : 17 * LANES, 512:640], x_ref[16 * LANES : 17 * LANES, 128:256])
         halo_start(thin(s))
-
-    def banded(x_ref, f_ref, bias, out_ref):
-        def step(b, carry):
-            start = pl.multiple_of(b * SPAN, LANES)
-            total = nn(x_ref[pl.ds(start, SPAN), :], f_ref[0:768, :])
-            total += nn(x_ref[pl.ds(start + LANES, SPAN), :], f_ref[768:1536, :])
-            out_ref[pl.ds(start, SPAN), :] = total + bias
-            return carry
-
-        lax.fori_loop(0, STEPS, step, 0)
 
     def banded_back(g_ref, d_ref, out_ref):
         width = g_ref.shape[1]
@@ -1005,21 +987,45 @@
     def twice(row):
         return jnp.concatenate([row, row], axis=1)
 
-    def layer_forward(x_ref, f_ref, bias, out_ref, s):
+    def layer_forward(x_ref, f_ref, bias, out_ref, s, x_next):
         exchange(x_ref, s)
-        banded(x_ref, f_ref, twice(bias), out_ref)
+        bias = twice(bias)
+
+        def products(b):
+            rows, more = pl.ds(b * SPAN, SPAN), pl.ds(b * SPAN + LANES, SPAN)
+            total = nn(x_ref[rows, :], f_ref[0:768, :])
+            total += nn(x_ref[more, :], f_ref[768:1536, :])
+            out_ref[rows, :] = total + bias
+
+        def piece(q, e):
+            rows = pl.ds(q * LANES, LANES)
+            activated(out_ref[rows, e * LANES : (e + 1) * LANES], x_next, q, e)
+
+        products(0)
+        products(1)
+        for q in range(QB):
+            for e in range(2):
+                piece(q, e)
+
+        def step(q, carry):
+            rows = pl.ds(pl.multiple_of(q * LANES, LANES), LANES)
+            for e in range(2):
+                activated(out_ref[rows, e * LANES : (e + 1) * LANES], x_next, q, e)
+            return carry
+
+        lax.fori_loop(QB, PAIRS, step, 0)
         halo_wait(thin(s))
         top_row, bottom_row = edges(1, from_up[s], from_down[s])
         put_edges(x_ref, top_row, bottom_row)
         add_edges(out_ref, nn(top_row, f_ref[0:384, 0:LANES]), nn(bottom_row, f_ref[768:1152, 0:LANES]))
+        for q, e in ((0, 0), (15, 1), (16, 0)):
+            piece(q, e)
 
     kernel_loads[0].wait()
-    layer_forward(x_one, f_one, bias_row(33, 96), pre_one, 0)
-    activate(pre_one, x_two)
+    layer_forward(x_one, f_one, bias_row(33, 96), pre_one, 0, x_two)
     for load in kernel_loads[1:]:
         load.wait()
-    layer_forward(x_two, f_two, bias_row(35, 96), pre_two, 1)
-    activate(pre_two, x_three)
+    layer_forward(x_two, f_two, bias_row(35, 96), pre_two, 1, x_three)
 
     def weight_grads(g_ref, x_ref, parts, write):
         width, wide = parts * LANES, 3 * parts * LANES
@@ -1067,30 +1073,32 @@
     def last_layers(pre_three, x_head, g_three):
         bias = jnp.concatenate([bias_row(37, 96), bias_row(38, 96)], axis=1)
 
-        def conv_step(b, carry):
-            start = pl.multiple_of(b * SPAN, LANES)
-            rows, more = pl.ds(start, SPAN), pl.ds(start + LANES, SPAN)
-            total = nn(x_ref3[rows, :], f_three[0:768, :]) + nn(x_ref3[more, 0:384], f_three[768:1152, :])
+        def products(b):
+            rows, more = pl.ds(b * SPAN, SPAN), pl.ds(b * SPAN + LANES, SPAN)
+            total = nn(x_three[rows, :], f_three[0:768, :]) + nn(x_three[more, 0:384], f_three[768:1152, :])
             pre_three[rows, 0:256] = total + bias
-            total = nn(x_ref3[rows, 384:768], f_three[0:384, :]) + nn(x_ref3[more, :], f_three[384:1152, :])
+            total = nn(x_three[rows, 384:768], f_three[0:384, :]) + nn(x_three[more, :], f_three[384:1152, :])
             pre_three[rows, 256:512] = total + bias
+
+        def head_rows(rows):
+            x_head[rows, :] = half_silu(0.5 * pre_three[rows, :]).astype(BF16)
+
+        def head_step(q, carry):
+            head_rows(pl.ds(pl.multiple_of(q * LANES, LANES), LANES))
             return carry
 
-        x_ref3 = x_three
         exchange(x_three, 2)
-        lax.fori_loop(0, STEPS, conv_step, 0)
+        products(0)
+        products(1)
+        for q in range(QB):
+            head_rows(pl.ds(q * LANES, LANES))
+        lax.fori_loop(QB, PAIRS, head_step, 0)
         halo_wait(thin(2))
         top_row, bottom_row = edges(1, from_up[2], from_down[2])
         put_edges(x_three, top_row, bottom_row)
         add_edges(pre_three, nn(top_row, f_three[0:384, :]), nn(bottom_row, f_three[768:1152, :]))
-
-        def head_step(q, carry):
-            rows = pl.ds(pl.multiple_of(q * LANES, LANES), LANES)
-            value = pre_three[rows, :]
-            x_head[rows, :] = (value * sigmoid(value)).astype(BF16)
-            return carry
-
-        lax.fori_loop(0, PAIRS, head_step, 0)
+        for q in (0, 15, 16):
+            head_rows(pl.ds(q * LANES, LANES))
         for load in loads:
             load.wait()
         head_row = jnp.broadcast_to(stat[40:41, :], (LANES, LANES))
@@ -1160,7 +1168,7 @@
             return carry
 
         g_three[0:LANES, 0:768] = jnp.zeros((LANES, 768), BF16)
-        g_three[18 * LANES : 20 * LANES, :] = jnp.zeros((2 * LANES, 1536), BF16)
+        g_three[18 * LANES : 19 * LANES, :] = jnp.zeros((LANES, 1536), BF16)
         lax.fori_loop(0, PAIRS, back_step, 0)
         last_row = slice(16 * LANES, 17 * LANES)
         send_up_w[...] = g_three[0:LANES, 1024:1280]
@@ -1193,7 +1201,7 @@
         last_layers,
         pltpu.VMEM((GRID, 512), F32),
         pltpu.VMEM((GRID, 512), BF16),
-        pltpu.VMEM((20 * LANES, 1536), BF16),
+        pltpu.VMEM((19 * LANES, 1536), BF16),
     )
 
     def lower_layers(g_ref, g_map, win0, win1, win2, gathered, d_two, d_one, w_mid):
@@ -1202,16 +1210,33 @@
         for load in lower_loads:
             load.start()
 
-        def grads_in(pre_ref):
+        def piece_in(pre_ref, rows, q, e):
+            lanes = slice(e * LANES, (e + 1) * LANES)
+            value = (0.5 * back[rows, lanes]) * half_slope(0.5 * pre_ref[rows, lanes])
+            put(g_ref, q + e, 1 - e, pick(ok(2 * q + 1 + e), value, 0.0), 0, 1)
+
+        def all_pieces(first, take):
             def step(q, carry):
                 rows = pl.ds(pl.multiple_of(q * LANES, LANES), LANES)
                 for e in range(2):
-                    lanes = slice(e * LANES, (e + 1) * LANES)
-                    value = back[rows, lanes] * slope(pre_ref[rows, lanes])
-                    put(g_ref, q + e, 1 - e, pick(ok(2 * q + 1 + e), value, 0.0), 0, 1)
+                    take(rows, q, e)
                 return carry
 
-            lax.fori_loop(0, PAIRS, step, 0)
+            lax.fori_loop(first, PAIRS, step, 0)
+
+        def back_and_on(d_ref, s, take, between):
+            for b in range(STEPS):
+                total = nt(g_ref[b * SPAN : (b + 1) * SPAN, :], d_ref[:, 0:768])
+                total += nt(g_ref[b * SPAN + LANES : (b + 1) * SPAN + LANES, :], d_ref[:, 768:1536])
+                back[b * SPAN : (b + 1) * SPAN, :] = total
+            for q in range(QB):
+                for e in range(2):
+                    take(pl.ds(q * LANES, LANES), q, e)
+            all_pieces(QB, take)
+            between()
+            from_edges(d_ref, s)
+            for q, e in ((0, 0), (15, 1), (16, 0)):
+                take(pl.ds(q * LANES, LANES), q, e)
 
         def weights_of(x_ref, begin):
             def write(i, j, part, block):
@@ -1226,37 +1251,37 @@
             add_back(d_ref, *edges(1, from_up[s], from_down[s]))
 
         g_ref[0:LANES, 0:384] = jnp.zeros((LANES, 384), BF16)
-        g_ref[18 * LANES : 20 * LANES, :] = jnp.zeros((2 * LANES, 768), BF16)
-        grads_in(pre_two)
+        g_ref[18 * LANES : 19 * LANES, :] = jnp.zeros((LANES, 768), BF16)
+        all_pieces(0, functools.partial(piece_in, pre_two))
         exchange(g_ref, 3)
         weights_of(x_two, B_TWO)
         ship(1)
         for load in lower_loads:
             load.wait()
-        banded_back(g_ref, d_two, back)
-        from_edges(d_two, 3)
-        ship_on(1)
-        grads_in(pre_one)
+        back_and_on(d_two, 3, functools.partial(piece_in, pre_one), lambda: ship_on(1))
         exchange(g_ref, 4)
-        banded_back(g_ref, d_one, back)
-        for i in of_stage(0):
-            ship_far(i)
-        from_edges(d_one, 4)
 
         g_map[...] = jnp.zeros_like(g_map)
 
-        def to_map(q, total):
-            rows = pl.ds(pl.multiple_of(q * LANES, LANES), LANES)
-            for e in range(2):
-                p = 2 * q + 1 + e
-                lanes = slice(e * LANES, (e + 1) * LANES)
-                value = back[rows, lanes] * slope(pre_mid[rows, lanes])
-                value = pick(ok(p), value, 0.0).astype(BF16).astype(F32)
-                g_map[pl.ds(pl.multiple_of(p * PITCH + 8, 8), LANES), :] = value
-                total += jnp.sum(value, axis=0, keepdims=True)
-            return total
-
-        total = lax.fori_loop(0, PAIRS, to_map, jnp.zeros((1, LANES), F32))
+        def piece_to_map(rows, q, e):
+            p = 2 * q + 1 + e
+            lanes = slice(e * LANES, (e + 1) * LANES)
+            value = (0.5 * back[rows, lanes]) * half_slope(0.5 * pre_mid[rows, lanes])
+            value = pick(ok(p), value, 0.0).astype(BF16).astype(F32)
+            spot = p * PITCH + 8
+            g_map[pl.ds(spot if isinstance(q, int) else pl.multiple_of(spot, 8), LANES), :] = value
+
+        def far_zero():
+            for i in of_stage(0):
+                ship_far(i)
+
+        back_and_on(d_one, 4, piece_to_map, far_zero)
+
+        def map_sum(p, total):
+            return total + g_map[pl.ds(pl.multiple_of(p * PITCH + 8, 8), LANES), :]
+
+        total = lax.fori_loop(1, 2 * PAIRS + 1, map_sum, jnp.zeros((LANES, LANES), F32))
+        total = jnp.sum(total, axis=0, keepdims=True)
         total = total[:, 0:CM] + total[:, CM : 2 * CM]
         grad_a[0:A_MID, :] = jnp.zeros((A_MID, LANES), F32)
         grad_a[A_MID + 1728 : A_ROWS, :] = jnp.zeros((A_ROWS - A_MID - 1728, LANES), F32)
@@ -1322,7 +1347,7 @@
     voxels = feature.shape[0]
     pl.run_scoped(
         lower_layers,
-        pltpu.VMEM((20 * LANES, 768), BF16),
+        pltpu.VMEM((19 * LANES, 768), BF16),
         pltpu.VMEM(((row_count + 6) * PITCH, LANES), F32),
         pltpu.VMEM((voxels * 4, LANES), F32),
         pltpu.VMEM((voxels * 4, LANES), F32),
@@ -1350,13 +1375,26 @@
         high = value.astype(BF16)
         return high, (value - high.astype(F32)).astype(BF16)
 
-    def note(ref, notes, sender, s, received):
-        return remote(ref, notes.at[sender], sem_ns.at[s], received.at[sender], 0)
+    def note(s, sender, target):
+        mine, notes, received = ((mine_a, notes_a, sem_nar), (mine_b, notes_b, sem_nbr))[s]
+        spot = sender // 2
+        return remote(mine, notes.at[spot], sem_ns.at[s], received.at[spot], target)
 
     def send_note(s):
-        @pl.when(me > 0)
+        mine, notes = ((mine_a, notes_a), (mine_b, notes_b))[s]
+
+        @pl.when(core == 1)
         def _():
-            (note(mine_a, notes_a, me, 0, sem_nar) if s == 0 else note(mine_b, notes_b, me, 1, sem_nbr)).start()
+            note(s, me, sibling).start()
+
+        @pl.when(core == 0)
+        def _():
+            note(s, me + 1, sibling).wait_recv()
+            mine[...] = mine[...] + notes[me // 2]
+
+        @pl.when((core == 0) & (me > 0))
+        def _():
+            note(s, me, 0).start()
 
     chunks = voxels // CHUNK
 
@@ -1467,23 +1505,19 @@
 
     @pl.when(me == 0)
     def _():
-        notes_a[0] = mine_a[...]
-        notes_b[0] = mine_b[...]
-        for d in range(1, n):
-            note(mine_a, notes_a, d, 0, sem_nar).wait_recv()
-        fc_total = notes_a[0]
-        for d in range(1, n):
-            fc_total += notes_a[d]
+        fc_total = mine_a[...]
+        for d in range(2, n, 2):
+            note(0, d, sibling).wait_recv()
+            fc_total += notes_a[d // 2]
         fc_rows[...] = jnp.zeros_like(fc_rows)
         fc_rows[8:80, :] = nn(fc_total, order.astype(F32), HIGH)
         here, before = fc_rows[8:80, :], fc_rows[7:79, :]
         mixed = jnp.where(lane_of((72, LANES)) >= LANES - FC_LANE, before, here)
         small_grad[2:74, :] = pltpu.roll(mixed, FC_LANE, axis=1)
-        for d in range(1, n):
-            note(mine_b, notes_b, d, 1, sem_nbr).wait_recv()
-        total = notes_b[0]
-        for d in range(1, n):
-            total += notes_b[d]
+        total = mine_b[...]
+        for d in range(2, n, 2):
+            note(1, d, sibling).wait_recv()
+            total += notes_b[d // 2]
         by_grad, by_norm = total[0:32, 0:8], total[0:32, 8:16]
         g_gamma, g_beta = total[0:32, 16:17], total[0:32, 7:8]
         off_sums = jnp.transpose(jnp.broadcast_to(total[32:40, 0:1], (8, LANES)))[0:32, 0:8]
@@ -1503,8 +1537,8 @@
 
     @pl.when(me > 0)
     def _():
-        note(mine_a, notes_a, me, 0, sem_nar).wait_send()
-        note(mine_b, notes_b, me, 1, sem_nbr).wait_send()
+        for s in range(2):
+            note(s, me, sibling).wait_send()
 
     for k in range(1, n):
         sender = lax.rem(me + n - k, n)
@@ -1545,15 +1579,15 @@
             pltpu.VMEM((voxels, LANES), F32),
             pltpu.VMEM((NOTE_A, LANES), F32),
             pltpu.VMEM((NOTE_B, LANES), F32),
-            pltpu.VMEM((n, NOTE_A, LANES), F32),
-            pltpu.VMEM((n, NOTE_B, LANES), F32),
+            pltpu.VMEM((n // 2, NOTE_A, LANES), F32),
+            pltpu.VMEM((n // 2, NOTE_B, LANES), F32),
             pltpu.VMEM((88, LANES), F32),
             pltpu.VMEM((SMALL, LANES), F32),
             *[pltpu.VMEM(middle_out[a].shape, BF16) for a in (2, 3, 4, 7, 8)],
             dma((8,)),
-            pltpu.VMEM((20 * LANES, 768), BF16),
-            pltpu.VMEM((20 * LANES, 768), BF16),
-            pltpu.VMEM((20 * LANES, 768), BF16),
+            pltpu.VMEM((19 * LANES, 768), BF16),
+            pltpu.VMEM((19 * LANES, 768), BF16),
+            pltpu.VMEM((19 * LANES, 768), BF16),
             pltpu.VMEM((GRID, 256), F32),
             pltpu.VMEM((GRID, 256), F32),
             pltpu.VMEM((GRID, 256), F32),
@@ -1581,7 +1615,7 @@
             pltpu.VMEM((LANES, 256), BF16),
             dma((16,)), dma((2,)), dma((2,)), dma((12,)), dma((12,)), dma((2,)), dma((2,)), dma((n,)), dma((n,)),
             dma((pieces,)), dma((pieces,)), dma((pieces,)), dma((pieces,)),
-            dma((pieces,)), dma((5 * fours,)), dma((8,)), dma((2,)), dma((n,)), dma((n,)),
+            dma((pieces,)), dma((5 * fours,)), dma((8,)), dma((2,)), dma((n // 2,)), dma((n // 2,)),
         ],
         compiler_params=pltpu.CompilerParams(
             collective_id=2, has_side_effects=True, vmem_limit_bytes=63 << 20

time: 140 us -> 136 us (0.971)
  Pallas kernels: 139 us -> 134 us
    pallas_call x1, Pallas kernels: 93.6 us -> 89 us  [train(): pl.pallas_call(functools.partial(conv_kernel, n, rows_dev, row_count), na...]
where the time goes in v5:
time: 136 us; the launch traced here: 135 us
  Pallas kernels  134 us (99%)
    pallas_call x1, Pallas kernels, train(): pl.pallas_call(functools.partial(conv_kernel, n, rows_dev, row_count), na...  89 us
    pallas_call x1, Pallas kernels, front(): pl.pallas_call(functools.partial(front_kernel, n), name='front', out_shap...  32.5 us
    pallas_call x1, Pallas kernels, middle(): pl.pallas_call(functools.partial(middle_kernel, n, rows, row_count), name...  8.92 us
    pallas_call x1, Pallas kernels, update(): pl.pallas_call(update_kernel, name='update', out_shape=(shape(gradient.sh...  4 us

profile of v5, /device:TPU:0, one launch (start us, length us, event | category | flops | bytes accessed | tf_op | source)
XLA Modules:
  0.0 135.3 jit_solution(455795203145539471)
XLA Ops:
  0.6 32.5 %front.1 = (bf16[8,816,128]{2,1,0:T(8,128)(2,1)}, f32[80,128]{1,0:T(8,128)}, f32[48,128]{1,0:T(8,128)}, bf16[35,32,512]{2,1,0:T(8,128)(2,1)}, bf16[32,512]{1,0:T...) custom-call(f32[7,35,512]{2,1,0:T(8,128)} %points_hbm.1, s32[1,512]{1,0:T(1,128)} %bitcast.18, s32[1,512]{1,0:T(1,128)} %bitcast.15, ...), custom_call_target="tpu_custom_call" | custom-call | tf_op jit(solution)/shard_map/front/pallas_call | solution.py:458
  33.2 8.9 %middle.1 = (f32[37,128,128]{2,1,0:T(8,128)}, bf16[512,1152]{1,0:T(8,128)(2,1)}, bf16[1536,256]{1,0:T(8,128)(2,1)}, bf16[1536,256]{1,0:T(8,128)(2,1)}, bf16[1152...) custom-call(s32[1,512]{1,0:T(1,128)} %get-tuple-element.30.bases, ...), custom_call_target="tpu_custom_call" | custom-call | tf_op jit(solution)/shard_map/middle/pallas_call | solution.py:683
  42.1 89.0 %train.1 = (f32[805,128]{1,0:T(8,128)}, f32[8,128]{1,0:T(8,128)}) custom-call(s32[1,512]{1,0:T(1,128)} %get-tuple-element.30.bases, s32[1,512]{1,0:T(1,128)} %bitcast.17, f32[512,128]{1,0:T(8,128)} %get-tuple-element.31.feature, f32[48,128]{1,0:T(8,128)} %get-tuple-element.32.stat, f32[37,128,128]{2,1,0:T(8,128)} %get-tuple-element.34.pre_in, ...), custom_call_target="tpu_custom_call" | custom-call | tf_op jit(solution)/shard_map/train/pallas_call | solution.py:1563
  131.1 4.0 %update.1 = (f32[805,128]{1,0:T(8,128)}, f32[805,128]{1,0:T(8,128)}, f32[805,128]{1,0:T(8,128)}, f32[805,128]{1,0:T(8,128)}, f32[1]{0:T(128)}, /*index=5*/f32[1]{0:T(128)}) custom-call(f32[805,128]{1,0:T(8,128)} %get-tuple-element.46.gradient, f32[805,128]{1,0:T(8,128)} %bitcast.11, f32[805,128]{1,0:T(8,128)} %bitcast.12, f32[805,128]{1,0:T(8,128)} %bitcast.13, ...), custom_call_target="tpu_custom_call" | custom-call | tf_op jit(solution)/shard_map/update/pallas_call | solution.py:1682

commit v6 on v5

--- a/solution.py
+++ b/solution.py
@@ -1040,13 +1040,16 @@
             rows = pl.ds(start, SPAN)
             g0, g1 = g_ref[rows, middle0], g_ref[rows, middle1]
             both = jnp.concatenate([g0, g1], axis=1)
+            sums = both.astype(F32).reshape(SPAN // 8, 8, 2 * width)
+            carry = carry + jnp.sum(sums, axis=0)
             acc0[0 : 2 * width, :] += tn(both, x_ref[rows, :])
             acc2[0:width, :] += tn(g1, x_ref[pl.ds(start + LANES, SPAN), 0:384])
             after = g_ref[pl.ds(start + LANES, SPAN), middle0]
             acc1[0:width, :] += tn(after, x_ref[rows, 384:768])
             return carry
 
-        lax.fori_loop(0, STEPS, step, 0)
+        sums = lax.fori_loop(0, STEPS, step, jnp.zeros((8, 2 * width), F32))
+        sums = jnp.sum(sums, axis=0, keepdims=True)
         for i in range(3):
             if i == 0:
                 total = acc0[width : 2 * width, 0:384] + acc1[0:width, :]
@@ -1058,17 +1061,7 @@
                 for part in range(parts):
                     block = total[part * LANES : (part + 1) * LANES, j * LANES : (j + 1) * LANES]
                     write(i, j, part, jnp.transpose(block))
-
-    def bias_grads(g_ref, parts):
-        width, wide = parts * LANES, 3 * parts * LANES
-        ones = jnp.ones((16, SPAN), BF16)
-
-        def step(b, total):
-            rows = pl.ds(pl.multiple_of(b * SPAN, LANES), SPAN)
-            total += nn(ones, g_ref[rows, width : 2 * width])
-            return total + nn(ones, g_ref[rows, wide + width : wide + 2 * width])
-
-        return lax.fori_loop(0, STEPS, step, jnp.zeros((16, width), F32))[0:1, :]
+        return sums[:, 0:width] + sums[:, width : 2 * width]
 
     def last_layers(pre_three, x_head, g_three):
         bias = jnp.concatenate([bias_row(37, 96), bias_row(38, 96)], axis=1)
@@ -1180,8 +1173,7 @@
             start = B_THREE + 2 * (i * 3 + j) * LANES + part
             grad_b[pl.ds(start, LANES, 2), :] = block
 
-        weight_grads(g_three, x_three, 2, write)
-        sums = bias_grads(g_three, 2)
+        sums = weight_grads(g_three, x_three, 2, write)
         grad_b[B_HEAD - 2 : B_HEAD - 1, :] = sums[:, 0:LANES]
         grad_b[B_HEAD - 1 : B_HEAD, :] = sums[:, LANES : 2 * LANES]
         ship(0)
@@ -1243,8 +1235,7 @@
                 start = begin + (i * 3 + j) * LANES
                 grad_b[start : start + LANES, :] = block
 
-            weight_grads(g_ref, x_ref, 1, write)
-            grad_b[begin + 1152 : begin + 1153, :] = bias_grads(g_ref, 1)
+            grad_b[begin + 1152 : begin + 1153, :] = weight_grads(g_ref, x_ref, 1, write)
 
         def from_edges(d_ref, s):
             halo_wait(thin(s))
@@ -1258,7 +1249,8 @@
         ship(1)
         for load in lower_loads:
             load.wait()
-        back_and_on(d_two, 3, functools.partial(piece_in, pre_one), lambda: ship_on(1))
+        ship_on(1)
+        back_and_on(d_two, 3, functools.partial(piece_in, pre_one), lambda: None)
         exchange(g_ref, 4)
 
         g_map[...] = jnp.zeros_like(g_map)
@@ -1277,6 +1269,13 @@
 
         back_and_on(d_one, 4, piece_to_map, far_zero)
 
+        def map_row(place):
+            return slice(place * PITCH + 8, place * PITCH + 8 + LANES)
+
+        send_up[5] = g_map[map_row(1), :].astype(BF16)
+        send_down[5] = pick(split == 1, g_map[map_row(row_count + 1), :], g_map[map_row(row_count), :]).astype(BF16)
+        halo_start(thin(5))
+
         def map_sum(p, total):
             return total + g_map[pl.ds(pl.multiple_of(p * PITCH + 8, 8), LANES), :]
 
@@ -1286,13 +1285,6 @@
         grad_a[0:A_MID, :] = jnp.zeros((A_MID, LANES), F32)
         grad_a[A_MID + 1728 : A_ROWS, :] = jnp.zeros((A_ROWS - A_MID - 1728, LANES), F32)
         grad_a[A_MID + 1728 : A_MID + 1729, 0:CM] = total
-
-        def map_row(place):
-            return slice(place * PITCH + 8, place * PITCH + 8 + LANES)
-
-        send_up[5] = g_map[map_row(1), :].astype(BF16)
-        send_down[5] = pick(split == 1, g_map[map_row(row_count + 1), :], g_map[map_row(row_count), :]).astype(BF16)
-        halo_start(thin(5))
         weights_of(x_one, B_ONE)
         ship(2)
         halo_wait(thin(5))

time: 136 us -> 133 us (0.978)
  Pallas kernels: 134 us -> 132 us
    pallas_call x1, Pallas kernels: 89 us -> 86.4 us  [train(): pl.pallas_call(functools.partial(conv_kernel, n, rows_dev, row_count), na...]
where the time goes in v6:
time: 133 us
  Pallas kernels  132 us (99%)
    pallas_call x1, Pallas kernels, train(): pl.pallas_call(functools.partial(conv_kernel, n, rows_dev, row_count), na...  86.4 us
    pallas_call x1, Pallas kernels, front(): pl.pallas_call(functools.partial(front_kernel, n), name='front', out_shap...  32.5 us
    pallas_call x1, Pallas kernels, middle(): pl.pallas_call(functools.partial(middle_kernel, n, rows, row_count), name...  8.92 us
    pallas_call x1, Pallas kernels, update(): pl.pallas_call(update_kernel, name='update', out_shape=(shape(gradient.sh...  4 us

profile of v6, /device:TPU:0, one launch (start us, length us, event | category | flops | bytes accessed | tf_op | source)
XLA Modules:
  0.0 132.7 jit_solution(11537723571258673610)
XLA Ops:
  0.6 32.5 %front.1 = (bf16[8,816,128]{2,1,0:T(8,128)(2,1)}, f32[80,128]{1,0:T(8,128)}, f32[48,128]{1,0:T(8,128)}, bf16[35,32,512]{2,1,0:T(8,128)(2,1)}, bf16[32,512]{1,0:T...) custom-call(f32[7,35,512]{2,1,0:T(8,128)} %points_hbm.1, s32[1,512]{1,0:T(1,128)} %bitcast.18, s32[1,512]{1,0:T(1,128)} %bitcast.15, ...), custom_call_target="tpu_custom_call" | custom-call | tf_op jit(solution)/shard_map/front/pallas_call | solution.py:458
  33.2 8.9 %middle.1 = (f32[37,128,128]{2,1,0:T(8,128)}, bf16[512,1152]{1,0:T(8,128)(2,1)}, bf16[1536,256]{1,0:T(8,128)(2,1)}, bf16[1536,256]{1,0:T(8,128)(2,1)}, bf16[1152...) custom-call(s32[1,512]{1,0:T(1,128)} %get-tuple-element.30.bases, ...), custom_call_target="tpu_custom_call" | custom-call | tf_op jit(solution)/shard_map/middle/pallas_call | solution.py:683
  42.1 86.4 %train.1 = (f32[805,128]{1,0:T(8,128)}, f32[8,128]{1,0:T(8,128)}) custom-call(s32[1,512]{1,0:T(1,128)} %get-tuple-element.30.bases, s32[1,512]{1,0:T(1,128)} %bitcast.17, f32[512,128]{1,0:T(8,128)} %get-tuple-element.31.feature, f32[48,128]{1,0:T(8,128)} %get-tuple-element.32.stat, f32[37,128,128]{2,1,0:T(8,128)} %get-tuple-element.34.pre_in, ...), custom_call_target="tpu_custom_call" | custom-call | tf_op jit(solution)/shard_map/train/pallas_call | solution.py:1555
  128.6 4.0 %update.1 = (f32[805,128]{1,0:T(8,128)}, f32[805,128]{1,0:T(8,128)}, f32[805,128]{1,0:T(8,128)}, f32[805,128]{1,0:T(8,128)}, f32[1]{0:T(128)}, /*index=5*/f32[1]{0:T(128)}) custom-call(f32[805,128]{1,0:T(8,128)} %get-tuple-element.46.gradient, f32[805,128]{1,0:T(8,128)} %bitcast.11, f32[805,128]{1,0:T(8,128)} %bitcast.12, f32[805,128]{1,0:T(8,128)} %bitcast.13, ...), custom_call_target="tpu_custom_call" | custom-call | tf_op jit(solution)/shard_map/update/pallas_call | solution.py:1674

commit v7 on v6

--- a/solution.py
+++ b/solution.py
@@ -955,7 +955,7 @@
             activated(value, x_one, q, e)
         return carry
 
-    lax.fori_loop(0, PAIRS, mid_step, 0)
+    lax.fori_loop(0, PAIRS, mid_step, 0, unroll=2)
     halo_wait(copies)
     at_top = pick((top == 1) & has_up, from_up_f[...], 0.0)
     at_bottom = pick((bottom == 1) & has_down, from_down_f[...], 0.0)
@@ -1155,14 +1155,14 @@
             rows = pl.ds(pl.multiple_of(q * LANES, LANES), LANES)
             for e in range(2):
                 grad = tn(logit_grads[e, :, rows], head_t[...])
-                grad = grad * slope(pre_three[rows, e * 256 : (e + 1) * 256])
+                grad = (0.5 * grad) * half_slope(0.5 * pre_three[rows, e * 256 : (e + 1) * 256])
                 for part in range(2):
                     put(g_three, q + e, 1 - e, grad[:, part * LANES : (part + 1) * LANES], part, 2)
             return carry
 
         g_three[0:LANES, 0:768] = jnp.zeros((LANES, 768), BF16)
         g_three[18 * LANES : 19 * LANES, :] = jnp.zeros((LANES, 1536), BF16)
-        lax.fori_loop(0, PAIRS, back_step, 0)
+        lax.fori_loop(0, PAIRS, back_step, 0, unroll=2)
         last_row = slice(16 * LANES, 17 * LANES)
         send_up_w[...] = g_three[0:LANES, 1024:1280]
         send_down_w[...] = pick(split == 1, g_three[last_row, 1024:1280], g_three[last_row, 256:512])

time: 133 us -> 132 us (level)
  no operation moved by 1% of the time
where the time goes in v7:
time: 132 us
  Pallas kernels  131 us (99%)
    pallas_call x1, Pallas kernels, train(): pl.pallas_call(functools.partial(conv_kernel, n, rows_dev, row_count), na...  85.6 us
    pallas_call x1, Pallas kernels, front(): pl.pallas_call(functools.partial(front_kernel, n), name='front', out_shap...  32.5 us
    pallas_call x1, Pallas kernels, middle(): pl.pallas_call(functools.partial(middle_kernel, n, rows, row_count), name...  8.92 us
    pallas_call x1, Pallas kernels, update(): pl.pallas_call(update_kernel, name='update', out_shape=(shape(gradient.sh...  4 us

profile of v7, /device:TPU:0, one launch (start us, length us, event | category | flops | bytes accessed | tf_op | source)
XLA Modules:
  0.0 131.9 jit_solution(4052754439302021354)
XLA Ops:
  0.6 32.5 %front.1 = (bf16[8,816,128]{2,1,0:T(8,128)(2,1)}, f32[80,128]{1,0:T(8,128)}, f32[48,128]{1,0:T(8,128)}, bf16[35,32,512]{2,1,0:T(8,128)(2,1)}, bf16[32,512]{1,0:T...) custom-call(f32[7,35,512]{2,1,0:T(8,128)} %points_hbm.1, s32[1,512]{1,0:T(1,128)} %bitcast.18, s32[1,512]{1,0:T(1,128)} %bitcast.15, ...), custom_call_target="tpu_custom_call" | custom-call | tf_op jit(solution)/shard_map/front/pallas_call | solution.py:458
  33.2 8.9 %middle.1 = (f32[37,128,128]{2,1,0:T(8,128)}, bf16[512,1152]{1,0:T(8,128)(2,1)}, bf16[1536,256]{1,0:T(8,128)(2,1)}, bf16[1536,256]{1,0:T(8,128)(2,1)}, bf16[1152...) custom-call(s32[1,512]{1,0:T(1,128)} %get-tuple-element.30.bases, ...), custom_call_target="tpu_custom_call" | custom-call | tf_op jit(solution)/shard_map/middle/pallas_call | solution.py:683
  42.1 85.6 %train.1 = (f32[805,128]{1,0:T(8,128)}, f32[8,128]{1,0:T(8,128)}) custom-call(s32[1,512]{1,0:T(1,128)} %get-tuple-element.30.bases, s32[1,512]{1,0:T(1,128)} %bitcast.17, f32[512,128]{1,0:T(8,128)} %get-tuple-element.31.feature, f32[48,128]{1,0:T(8,128)} %get-tuple-element.32.stat, f32[37,128,128]{2,1,0:T(8,128)} %get-tuple-element.34.pre_in, ...), custom_call_target="tpu_custom_call" | custom-call | tf_op jit(solution)/shard_map/train/pallas_call | solution.py:1555
  127.7 4.0 %update.1 = (f32[805,128]{1,0:T(8,128)}, f32[805,128]{1,0:T(8,128)}, f32[805,128]{1,0:T(8,128)}, f32[805,128]{1,0:T(8,128)}, f32[1]{0:T(128)}, /*index=5*/f32[1]{0:T(128)}) custom-call(f32[805,128]{1,0:T(8,128)} %get-tuple-element.46.gradient, f32[805,128]{1,0:T(8,128)} %bitcast.11, f32[805,128]{1,0:T(8,128)} %bitcast.12, f32[805,128]{1,0:T(8,128)} %bitcast.13, ...), custom_call_target="tpu_custom_call" | custom-call | tf_op jit(solution)/shard_map/update/pallas_call | solution.py:1674
